TPU v7x, 32 devices: a whole 2x2x4 slice. The times are simulated.
32 devices in a mesh: mem: 16 (over z, y, x), sp: 2 (over core).
Axes of the slice: x: 2, y: 2, z: 4, core: 2. Of those that a mesh axis runs over, the one named last changes fastest.
Arguments:
- logarithmic_diffusivity: float32 [128, 16, 1024], P('mem', 'sp'), may hold values from -0.9 to 0.9
- starting_warmth: float32 [16, 1024], P('sp'), may hold values from -4 to 4
- thermal_supply: float32 [16, 1024], P('sp'), may hold values from -4 to 4
- probe_positions: int32 [128], P('sp'), may hold values from 0 to 8191, as said below
- recorded_temps: float32 [128], P('sp'), may hold values from -4 to 4
- probe_error_sigma: float32 [128], P('sp'), may hold values from 0.005 to 0.5
- perturb_draws: float32 [128, 128], P('mem', 'sp'), may hold values from -4 to 4
Outputs:
- revised_lncond: float32 [128, 16, 1024], P('mem', 'sp')
- predicted: float32 [128, 128], P('mem', 'sp')
Inputs may be any that keep to these rules, and one draw needn't show every extreme that they name: `probe_positions`: each entry indexes a cell of its own device's slab, row-major over 8 rows of 1024 cells; entry j of a slab's block of 64 lies in row j * 8 // 64.
All inputs are finite; a program needn't handle non-finite values.
Results may differ from a plain program's by a relative error of at most 0.0042.
Values may be sent and summed in bfloat16 or wider, within the bound.
No kernel may reach another device: no remote copies, remote signals or barrier semaphores. Data moves between devices by JAX's collectives and lax.ppermute only.
A program may use at most 64 MiB of HBM per device.

v0:
```python
import math

import jax
import jax.numpy as jnp
from jax import lax
from jax.sharding import PartitionSpec as P

STEPS = 4


time_step = 0.06
damping = 2.0
block_width = 16


def padded(cells, sides, width):
    for axis, dim in sides:
        count = lax.axis_size(axis)
        ends = count - 1
        head = lax.slice_in_dim(cells, 0, width, axis=dim)
        tail = lax.slice_in_dim(cells, cells.shape[dim] - width, cells.shape[dim], axis=dim)
        cells = jnp.concatenate(
            [
                lax.ppermute(tail, axis, [(i, (i + 1) % count) for i in range(ends)]),
                cells,
                lax.ppermute(head, axis, [((i + 1) % count, i) for i in range(ends)]),
            ],
            axis=dim,
        )
    return cells


def invert_block(matrix):
    augmented = jnp.concatenate([matrix, jnp.eye(block_width, dtype=matrix.dtype)], axis=1)
    for place in range(block_width):
        pivot_row = augmented[place] / augmented[place, place]
        augmented = augmented - augmented[:, place : place + 1] * pivot_row[None, :]
        augmented = jnp.concatenate(
            [augmented[:place], pivot_row[None, :], augmented[place + 1 :]], axis=0
        )
    return augmented[:, block_width:]


def eliminate(gram_matrix, cross_term):
    order = gram_matrix.shape[0]
    tableau = jnp.concatenate([gram_matrix, cross_term], axis=1)

    def one_turn(block_number, tableau):
        first_row = (block_number * block_width).astype(jnp.int32)
        row_band = lax.dynamic_slice_in_dim(tableau, first_row, block_width, 0)
        pivot_block = lax.dynamic_slice_in_dim(row_band, first_row, block_width, 1)
        inverse = invert_block(pivot_block)
        scaled_rows = jnp.dot(
            inverse, row_band, precision=lax.Precision.HIGHEST, preferred_element_type=tableau.dtype
        )
        column = lax.dynamic_slice_in_dim(tableau, first_row, block_width, 1)
        tableau = tableau - jnp.dot(
            column,
            scaled_rows,
            precision=lax.Precision.HIGHEST,
            preferred_element_type=tableau.dtype,
        )
        return lax.dynamic_update_slice_in_dim(tableau, scaled_rows, first_row, 0)

    tableau = lax.fori_loop(0, order // block_width, one_turn, tableau)
    return tableau[:, order:]


def advance_solution(padded_warmth, padded_coefficient, thermal_supply):
    warmth_margin = jnp.pad(padded_warmth, ((0, 0), (0, 0), (1, 1)))
    field_pad = jnp.pad(padded_coefficient, ((0, 0), (0, 0), (1, 1)))
    conduct = jnp.exp(field_pad) * (1.0 + 0.5 * jnp.tanh(warmth_margin))
    center = warmth_margin[:, 1:-1, 1:-1]
    cond_mid = conduct[:, 1:-1, 1:-1]
    inflow = jnp.zeros_like(center)
    for row_cut, col_cut in (
        (slice(2, None), slice(1, -1)),
        (slice(None, -2), slice(1, -1)),
        (slice(1, -1), slice(2, None)),
        (slice(1, -1), slice(None, -2)),
    ):
        inflow = inflow + 0.5 * (cond_mid + conduct[:, row_cut, col_cut]) * (
            warmth_margin[:, row_cut, col_cut] - center
        )
    return center + time_step * (inflow + thermal_supply)


def body(
    logarithmic_diffusivity,
    starting_warmth,
    thermal_supply,
    probe_positions,
    recorded_temps,
    probe_error_sigma,
    perturb_draws,
):
    resident_realizations, strip_lines, vertical_sequence = logarithmic_diffusivity.shape
    total_members = resident_realizations * lax.axis_size("mem")
    norm_scale = 1.0 / math.sqrt(total_members - 1)
    padded_coefficient = padded(logarithmic_diffusivity, (("sp", 1),), 1)
    thermal_snapshot = jnp.broadcast_to(starting_warmth, logarithmic_diffusivity.shape)
    for iteration in range(STEPS):
        padded_warmth = padded(thermal_snapshot, (("sp", 1),), 1)
        thermal_snapshot = advance_solution(padded_warmth, padded_coefficient, thermal_supply)
    probe_count = probe_positions.shape[0]
    per_line = probe_count // strip_lines
    line_values = jnp.broadcast_to(
        thermal_snapshot[:, :, None, :],
        (resident_realizations, strip_lines, per_line, vertical_sequence),
    ).reshape(resident_realizations, probe_count, vertical_sequence)
    probe_lines = jnp.arange(probe_count, dtype=jnp.int32) * strip_lines // probe_count
    probe_columns = probe_positions - probe_lines * vertical_sequence
    selector = (
        probe_columns[:, None] == jnp.arange(vertical_sequence, dtype=jnp.int32)[None, :]
    ).astype(jnp.float32)
    kept_prediction = jnp.sum(line_values * selector[None], axis=-1)
    mismatch_current = (recorded_temps - kept_prediction) / probe_error_sigma + perturb_draws
    complete_predicted_outputs = lax.all_gather(kept_prediction, "mem", axis=0, tiled=True)
    centered = complete_predicted_outputs - jnp.mean(
        complete_predicted_outputs, axis=0, keepdims=True
    )
    scaled = centered * (norm_scale / probe_error_sigma)
    gram_part = jnp.dot(
        scaled, scaled.T, precision=lax.Precision.HIGHEST, preferred_element_type=jnp.float32
    )
    cross_part = jnp.dot(
        scaled,
        mismatch_current.T,
        precision=lax.Precision.HIGHEST,
        preferred_element_type=jnp.float32,
    )
    gram_matrix, cross_term = lax.psum((gram_part, cross_part), "sp")
    gram_matrix = gram_matrix + damping * jnp.eye(total_members, dtype=jnp.float32)
    coeffs = eliminate(gram_matrix, cross_term)
    coeff_round = coeffs.astype(jnp.bfloat16)
    field_round = logarithmic_diffusivity.astype(jnp.bfloat16)
    flat_field = field_round.reshape(resident_realizations, strip_lines * vertical_sequence)
    change = lax.dot_general(
        coeff_round,
        lax.all_gather(flat_field, "mem", axis=0, tiled=True),
        (((0,), (0,)), ((), ())),
        preferred_element_type=jnp.float32,
    ).reshape(logarithmic_diffusivity.shape)
    revised_lncond = logarithmic_diffusivity + change * norm_scale
    return (revised_lncond, kept_prediction)


def solution(mesh):
    in_specs = (
        P("mem", "sp", None),
        P("sp", None),
        P("sp", None),
        P("sp"),
        P("sp"),
        P("sp"),
        P("mem", "sp"),
    )
    out_specs = (P("mem", "sp", None), P("mem", "sp"))
    return jax.shard_map(body, mesh=mesh, in_specs=in_specs, out_specs=out_specs, check_vma=False)
```

profile of v0, /device:TPU:0, one launch (start us, length us, event | category | flops | bytes accessed | tf_op | source)
XLA Modules:
  0.0 331.2 jit_solution(8536674126818408407)
XLA Ops:
  8.1 1.1 fusion.111
  9.2 2.4 collective-permute-start
  11.5 1.3 collective-permute-start.1
  13.7 3.0 collective-permute-start.2
  16.8 1.3 collective-permute-start.3
  18.1 1.8 collective-permute-done.3
  20.7 1.7 add_multiply_fusion.3
  23.0 2.1 collective-permute-start.4
  25.1 1.3 collective-permute-start.5
  26.5 1.7 collective-permute-done.5
  29.4 2.1 collective-permute-start.6
  31.5 1.3 collective-permute-start.7
  32.9 1.7 collective-permute-done.7
  35.9 2.1 collective-permute-start.8
  38.0 1.3 collective-permute-start.9
  39.3 1.8 collective-permute-done.9
  42.6 42.1 %all_gather.6 = f32[128,64]{1,0:T(8,128)S(1)} all-gather(f32[8,64]{1,0:T(8,128)S(1)} %reduce_sum.21), channel_id=1, replica_groups=mesh['mem'=16,'sp'=2] {'mem'}, dimensions={0}, use_global_device_ids=true | all-gather | bytes 34816 | tf_op jit(solution)/shard_map/all_gather | solution.py:118
  84.8 0.9 fusion.81
  86.7 3.6 %psum.15 = f32[128,8]{1,0:T(8,128)S(1)} all-reduce(f32[128,8]{1,0:T(8,128)S(1)} %fusion.80), channel_id=1, replica_groups=mesh['mem'=16,'sp'=2] {'sp'}, use_global_device_ids=true, to_apply=%region_3.4 | all-reduce | flops 1024 | bytes 8192 | tf_op jit(solution)/shard_map/psum | solution.py:132
  90.3 9.1 %all-reduce.7.cloned.1.call-done = f32[128,128]{1,0:T(8,128)} async-done(((f32[128,128]{1,0:T(8,128)}), f32[128,128]{1,0:T(8,128)}) %all-reduce.7.cloned.1.call-update) | async-done | bytes 65552 | tf_op jit(solution)/shard_map/psum | solution.py:132
  99.4 0.9 select_add_fusion
  100.4 220.4 %while.13 = (s32[]{:T(128)}, f32[128,136]{0,1:T(8,128)S(1)}, s32[]{:T(128)}, s32[]{:T(128)}, s32[]{:T(128)}, /*index=5*/s32[]{:T(128)}, s32[]{:T(128)}, s32[]{:T(128)}, s32[]{:T(128)}) while((s32[]{:T(128)}, f32[128,136]{0,1:T(8,128)S(1)}, s32[]{:T(128)}, s32[]{:T(128)}, s32[]{:T(128)}, /*index=5*/s32[]{:T(128)}, s32[]{:T(128)}, s32[]{:T(128)}, ...), condition=%wide.region_5.6_spmd, body=%wide.region_4.5_spmd.sunk | while | flops 3823866 | bytes 590428 | solution.py:65
  320.9 2.0 convolution_multiply_fusion
  322.8 0.9 copy_add_fusion
  (844 shorter events, 226.5 us)
Async XLA Ops:
  8.0 14.4 %copy-start.1 = (f32[8,1024]{1,0:T(8,128)S(1)}, f32[8,1024]{1,0:T(8,128)}, u32[]{:S(2)}) copy-start(f32[8,1024]{1,0:T(8,128)} %param.11) | copy-start | bytes 98308
  8.0 91.4 %all-reduce.7.cloned.1.call-start = ((), (), s32[]{:S(2)}) async-start(), calls=%async_computation | async-start | bytes 131072 | tf_op jit(solution)/shard_map/psum | solution.py:132
  9.2 8.9 %collective-permute-start = (f32[8,1,1024]{2,1,0:T(1,128)S(1)}, f32[8,1,1024]{2,1,0:T(1,128)S(1)}, u32[]{:S(2)}, u32[]{:S(2)}) collective-permute-start(f32[8,1,1024]{2,1,0:T(1,128)S(1)} %get-tuple-element.106), channel_id=1, source_target_pairs={{0,1},{2,3},{4,5},{6,7},{8,9},{10,11},{12,13},{14,15},{16,17},{18,... | collective-permute-start | bytes 98312 | tf_op jit(solution)/shard_map/ppermute | solution.py:24
  11.5 6.5 %collective-permute-start.1 = (f32[8,1,1024]{2,1,0:T(1,128)S(1)}, f32[8,1,1024]{2,1,0:T(1,128)S(1)}, u32[]{:S(2)}, u32[]{:S(2)}) collective-permute-start(f32[8,1,1024]{2,1,0:T(1,128)S(1)} %get-tuple-element.107), channel_id=1, source_target_pairs={{1,0},{3,2},{5,4},{7,6},{9,8},{11,10},{13,12},{15,14},{17,16},{19,... | collective-permute-start | bytes 98312 | tf_op jit(solution)/shard_map/ppermute | solution.py:26
  13.7 4.4 %collective-permute-start.2 = (f32[8,1,1024]{2,1,0:T(1,128)S(1)}, f32[8,1,1024]{2,1,0:T(1,128)S(1)}, u32[]{:S(2)}, u32[]{:S(2)}) collective-permute-start(f32[8,1,1024]{2,1,0:T(1,128)S(1)} %broadcast_in_dim.41), channel_id=1, source_target_pairs={{0,1},{2,3},{4,5},{6,7},{8,9},{10,11},{12,13},{14,15},{16,17},{18,... | collective-permute-start | bytes 98312 | tf_op jit(solution)/shard_map/ppermute | solution.py:24
  16.8 3.1 collective-permute-start.3
  20.7 5.7 %copy-start.6 = (s32[64]{0:T(128)S(1)}, s32[64]{0:T(128)}, u32[]{:S(2)}) copy-start(s32[64]{0:T(128)} %param.12) | copy-start | bytes 772
  20.7 7.5 %copy-start = (f32[8,8,1024]{2,1,0:T(8,128)S(1)}, f32[8,8,1024]{2,1,0:T(8,128)}, u32[]{:S(2)}) copy-start(f32[8,8,1024]{2,1,0:T(8,128)} %param.9) | copy-start | bytes 786436
  23.0 3.5 %collective-permute-start.4 = (f32[8,1,1024]{2,1,0:T(1,128)S(1)}, f32[8,1,1024]{2,1,0:T(1,128)S(1)}, u32[]{:S(2)}, u32[]{:S(2)}) collective-permute-start(f32[8,1,1024]{2,1,0:T(1,128)S(1)} %get-tuple-element.104), channel_id=1, source_target_pairs={{0,1},{2,3},{4,5},{6,7},{8,9},{10,11},{12,13},{14,15},{16,17},{18,... | collective-permute-start | bytes 98312 | tf_op jit(solution)/shard_map/ppermute | solution.py:24
  25.1 3.1 collective-permute-start.5
  29.4 3.5 %collective-permute-start.6 = (f32[8,1,1024]{2,1,0:T(1,128)S(1)}, f32[8,1,1024]{2,1,0:T(1,128)S(1)}, u32[]{:S(2)}, u32[]{:S(2)}) collective-permute-start(f32[8,1,1024]{2,1,0:T(1,128)S(1)} %get-tuple-element.102), channel_id=1, source_target_pairs={{0,1},{2,3},{4,5},{6,7},{8,9},{10,11},{12,13},{14,15},{16,17},{18,... | collective-permute-start | bytes 98312 | tf_op jit(solution)/shard_map/ppermute | solution.py:24
  31.5 3.1 collective-permute-start.7
  32.9 6.4 %copy-start.4 = (f32[64]{0:T(128)S(1)}, f32[64]{0:T(128)}, u32[]{:S(2)}) copy-start(f32[64]{0:T(128)} %param.14) | copy-start | bytes 772
  35.9 3.4 %collective-permute-start.8 = (f32[8,1,1024]{2,1,0:T(1,128)S(1)}, f32[8,1,1024]{2,1,0:T(1,128)S(1)}, u32[]{:S(2)}, u32[]{:S(2)}) collective-permute-start(f32[8,1,1024]{2,1,0:T(1,128)S(1)} %get-tuple-element.100), channel_id=1, source_target_pairs={{0,1},{2,3},{4,5},{6,7},{8,9},{10,11},{12,13},{14,15},{16,17},{18,... | collective-permute-start | bytes 98312 | tf_op jit(solution)/shard_map/ppermute | solution.py:24
  38.0 3.1 collective-permute-start.9
  41.8 44.7 %copy-start.3 = (f32[8,64]{1,0:T(8,128)S(1)}, f32[8,64]{1,0:T(8,128)}, u32[]{:S(2)}) copy-start(f32[8,64]{1,0:T(8,128)} %param.15) | copy-start | bytes 6148
  41.8 44.7 %copy-start.5 = (f32[64]{0:T(128)S(1)}, f32[64]{0:T(128)}, u32[]{:S(2)}) copy-start(f32[64]{0:T(128)} %param.13) | copy-start | bytes 772
  42.6 57.7 %copy-start.2 = (f32[8,64]{1,0:T(8,128)}, f32[8,64]{1,0:T(8,128)S(1)}, u32[]{:S(2)}) copy-start(f32[8,64]{1,0:T(8,128)S(1)} %reduce_sum.21) | copy-start | bytes 6148
  85.7 235.2 %all-gather.2.cloned.1.call-start = ((), (), s32[]{:S(2)}) async-start(), calls=%async_computation.1 | async-start | bytes 2228224 | tf_op jit(solution)/shard_map/all_gather | solution.py:140
Sparse Core Ops, SparseCore 0:
  85.8 13.5 all-reduce.6
Sparse Core Ops, SparseCore 1:
  89.5 56.7 all-gather.1
where the time goes:
time: 333 us; the launch traced here: 331 us
  other arithmetic  129 us (39%)
  local copies, waits for them, and re-layouts  96.1 us (29%)
  blocking collectives  45.7 us (14%)
  starting transfers between devices  18.1 us (5%)
  waiting for transfers between devices  16.1 us (5%)
  between operations  15.9 us (5%)
  matrix products  8.55 us (3%)
    div x128, other arithmetic, invert_block(): pivot_row = augmented[place] / augmented[place, place]  101 us
    slice x128, local copies, waits for them, and re-layouts, invert_block(): pivot_row = augmented[place] / augmented[place, place]  76.6 us
    all_gather x1, blocking collectives, body(): lax.all_gather(kept_prediction, 'mem', axis=0, tiled=True)  42.1 us
    ppermute x5, starting transfers between devices, padded(): lax.ppermute(tail, axis, [(i, (i + 1) % count) for i in range(ends)])  11.6 us
    sub x128, other arithmetic, invert_block(): augmented = augmented - augmented[:, place:place + 1] * pivot_row[None, :]  10.7 us
    psum x1, waiting for transfers between devices, body(): gram_matrix, cross_term = lax.psum((gram_part, cross_part), 'sp')  9.08 us
    concatenate x112, other arithmetic, invert_block(): jnp.concatenate([augmented[:place], pivot_row[None, :], augmented[place +...  8.89 us
    slice x112, local copies, waits for them, and re-layouts, invert_block(): augmented[place + 1:]  8.17 us
  transfers between devices with their start and end apart: 12, of which 5 were waited for; matrix products, arithmetic and copies ran while one was open for 67% of the time, Pallas kernels for 0%

commit v1 on v0

v1 whole, which is shorter than its diff:
```python
import math

import jax
import jax.numpy as jnp
from jax import lax
from jax.experimental import pallas as pl
from jax.experimental.pallas import tpu as pltpu
from jax.sharding import PartitionSpec as P

STEPS = 4


time_step = 0.06
damping = 2.0
block_width = 16
LANES = 128
ROWS = 8


def invert_block(matrix):
    augmented = jnp.concatenate([matrix, jnp.eye(block_width, dtype=matrix.dtype)], axis=1)
    for place in range(block_width):
        pivot_row = augmented[place] / augmented[place, place]
        augmented = augmented - augmented[:, place : place + 1] * pivot_row[None, :]
        augmented = jnp.concatenate(
            [augmented[:place], pivot_row[None, :], augmented[place + 1 :]], axis=0
        )
    return augmented[:, block_width:]


def eliminate(gram_matrix, cross_term):
    order = gram_matrix.shape[0]
    tableau = jnp.concatenate([gram_matrix, cross_term], axis=1)

    def one_turn(block_number, tableau):
        first_row = (block_number * block_width).astype(jnp.int32)
        row_band = lax.dynamic_slice_in_dim(tableau, first_row, block_width, 0)
        pivot_block = lax.dynamic_slice_in_dim(row_band, first_row, block_width, 1)
        inverse = invert_block(pivot_block)
        scaled_rows = jnp.dot(
            inverse, row_band, precision=lax.Precision.HIGHEST, preferred_element_type=tableau.dtype
        )
        column = lax.dynamic_slice_in_dim(tableau, first_row, block_width, 1)
        tableau = tableau - jnp.dot(
            column,
            scaled_rows,
            precision=lax.Precision.HIGHEST,
            preferred_element_type=tableau.dtype,
        )
        return lax.dynamic_update_slice_in_dim(tableau, scaled_rows, first_row, 0)

    tableau = lax.fori_loop(0, order // block_width, one_turn, tableau)
    return tableau[:, order:]


def conduct_kernel(
    flags_ref,
    columns_ref,
    field_ref,
    field_up_ref,
    field_down_ref,
    small_ref,
    small_up_ref,
    small_down_ref,
    recorded_ref,
    sigma_ref,
    draws_ref,
    predicted_ref,
    payload_ref,
    warmth,
    half_exp,
    supply,
):
    members, lines, width = predicted_ref.shape[0], small_ref.shape[0] // 2, small_ref.shape[1]
    tiles = width // LANES
    window = lines + 2 * STEPS
    lane = lax.broadcasted_iota(jnp.int32, (members, LANES), 1)
    first, last = lane == 0, lane == LANES - 1

    def place(row, ref, small, line, count, inside):
        coefficient = jnp.swapaxes(ref[...].reshape(members, lines, width), 0, 1)
        for step in range(count):
            part = coefficient[line + step]
            heat = small[pl.ds(line + step, 1), :]
            if inside is not None:
                part = jnp.where(inside, part, 0.0)
                heat = jnp.where(inside, heat, 0.0)
            half_exp[row + step] = 0.5 * jnp.exp(part)
            warmth[row + step] = jnp.broadcast_to(heat, (members, width))
        supply[pl.ds(row, count), :] = small[pl.ds(lines + line, count), :]

    above, below = flags_ref[0] > 0, flags_ref[1] > 0
    place(0, field_up_ref, small_up_ref, lines - STEPS, STEPS, above)
    place(STEPS, field_ref, small_ref, 0, lines, None)
    place(STEPS + lines, field_down_ref, small_down_ref, 0, STEPS, below)

    def cut(value):
        return [value[:, k * LANES : (k + 1) * LANES] for k in range(tiles)]

    def conductivity(row, warm):
        half = cut(half_exp[row])
        return [h * (1.0 + 0.5 * jnp.tanh(t)) for h, t in zip(half, warm)]

    half_one = jnp.full((members, LANES), 0.5, jnp.float32)
    zero = jnp.zeros((members, LANES), jnp.float32)

    for step in range(STEPS):
        low, high = step + 1, window - 1 - step
        t_up = cut(warmth[low - 1])
        c_up = conductivity(low - 1, t_up)
        t_here = cut(warmth[low])
        c_here = conductivity(low, t_here)
        flow_up = [(a + b) * (y - x) for a, b, x, y in zip(c_up, c_here, t_up, t_here)]

        def one_row(row, carry):
            t, c, up = carry
            t_next = cut(warmth[row + 1])
            c_next = conductivity(row + 1, t_next)
            down = [(a + b) * (y - x) for a, b, x, y in zip(c, c_next, t, t_next)]
            t_roll = [pltpu.roll(x, LANES - 1, 1) for x in t] + [zero]
            c_roll = [pltpu.roll(x, LANES - 1, 1) for x in c] + [half_one]
            right = []
            for k in range(tiles):
                t_right = jnp.where(last, t_roll[k + 1], t_roll[k])
                c_right = jnp.where(last, c_roll[k + 1], c_roll[k])
                right.append((c[k] + c_right) * (t_right - t[k]))
            back = [pltpu.roll(x, 1, 1) for x in right]
            outside = jnp.logical_or(
                jnp.logical_and(row < STEPS, flags_ref[0] <= 0),
                jnp.logical_and(row >= STEPS + lines, flags_ref[1] <= 0),
            )
            keep = jnp.where(outside, 0.0, 1.0)
            source = supply[pl.ds(row, 1), :]
            for k in range(tiles):
                edge = (c[0] + 0.5) * t[0] if k == 0 else back[k - 1]
                left = jnp.where(first, edge, back[k])
                inflow = (down[k] - up[k]) + (right[k] - left)
                heat = source[:, k * LANES : (k + 1) * LANES]
                warmth[row, :, k * LANES : (k + 1) * LANES] = keep * (
                    t[k] + time_step * (inflow + heat)
                )
            return t_next, c_next, down

        lax.fori_loop(low, high, one_row, (t_here, c_here, flow_up))

    probes = predicted_ref.shape[1]
    lane_probe = lax.broadcasted_iota(jnp.int32, (members, LANES), 1)
    picked = [zero for _ in range(4)]
    for probe in range(probes):
        line = probe * lines // probes
        column = columns_ref[probe] - line * width
        tile = column // LANES
        shift = lax.rem(probe - lax.rem(column, LANES) + LANES, LANES)
        values = warmth[STEPS + line, :, pl.ds(pl.multiple_of(tile * LANES, LANES), LANES)]
        moved = pltpu.roll(values, shift, 1)
        picked[probe % 4] = jnp.where(lane_probe == probe, moved, picked[probe % 4])
    total = (picked[0] + picked[1]) + (picked[2] + picked[3])
    predicted = total[:, :probes]
    predicted_ref[...] = predicted
    normal = (recorded_ref[...] - predicted) / sigma_ref[...]
    payload_ref[0:members, :] = normal
    payload_ref[members : 2 * members, :] = normal + draws_ref[...]


def update_kernel(norm_scale, slabs, place_ref, payload_ref, field_ref, gathered_ref, out_ref):
    devices = payload_ref.shape[0]
    owners = devices // slabs
    members = payload_ref.shape[1] // 2
    order = owners * members
    lines = field_ref.shape[0] // members
    mine = place_ref[0]
    dims = (((1,), (1,)), ((), ()))
    gram, cross = None, None
    for slab in range(slabs):
        normal = jnp.concatenate(
            [payload_ref[owner * slabs + slab, 0:members, :] for owner in range(owners)], axis=0
        )
        center = jnp.sum(normal, axis=0, keepdims=True) * (1.0 / order)
        scaled = (center - normal) * norm_scale
        misfit = payload_ref[mine * slabs + slab, members : 2 * members, :]
        one = lax.dot_general(
            scaled, scaled, dims, precision=lax.Precision.HIGHEST, preferred_element_type=jnp.float32
        )
        two = lax.dot_general(
            misfit, scaled, dims, precision=lax.Precision.HIGHEST, preferred_element_type=jnp.float32
        )
        gram = one if gram is None else gram + one
        cross = two if cross is None else cross + two
    row_id = lax.broadcasted_iota(jnp.int32, (ROWS, order), 0)
    lane_id = lax.broadcasted_iota(jnp.int32, (ROWS, order), 1)
    blocks = order // ROWS
    tableau = [
        gram[k * ROWS : (k + 1) * ROWS, :]
        + jnp.where(lane_id == row_id + k * ROWS, damping, 0.0)
        for k in range(blocks)
    ]
    tableau.append(cross)

    def lanes_of(value, at):
        return jnp.broadcast_to(value[:, at : at + 1], (ROWS, order))

    def row_of(value, at):
        return jnp.broadcast_to(value[at : at + 1, :], (ROWS, order))

    for block in range(blocks):
        base = block * ROWS
        inside = jnp.logical_and(lane_id >= base, lane_id < base + ROWS)
        band = tableau[block]
        column = [lanes_of(band, base + q) for q in range(ROWS)]
        band = jnp.where(inside, jnp.where(lane_id == row_id + base, -1.0, 0.0), band)
        for q in range(ROWS):
            here = row_id == q
            inverse = 1.0 / row_of(column[q], q)
            pivot_row = row_of(band, q) * inverse
            band = jnp.where(here, pivot_row, band - column[q] * pivot_row)
            for j in range(q + 1, ROWS):
                factor = row_of(column[j], q) * inverse
                column[j] = jnp.where(here, factor, column[j] - column[q] * factor)
        rows = [row_of(band, q) for q in range(ROWS)]
        for other in range(block + 1, blocks + 1):
            value = tableau[other]
            products = [lanes_of(value, base + q) * rows[q] for q in range(ROWS)]
            while len(products) > 1:
                products = [a + b for a, b in zip(products[::2], products[1::2])]
            tableau[other] = jnp.where(inside, 0.0, value) - products[0]
    solved = tableau[blocks].astype(jnp.bfloat16)

    wide = order * lines
    spread = (
        lax.broadcasted_iota(jnp.int32, (order, wide), 1) // lines
        == lax.broadcasted_iota(jnp.int32, (order, wide), 0)
    ).astype(jnp.bfloat16)
    stretched = jnp.dot(solved, spread, preferred_element_type=jnp.float32)
    on_line = lax.broadcasted_iota(jnp.int32, (lines, wide), 1) % lines == (
        lax.broadcasted_iota(jnp.int32, (lines, wide), 0)
    )
    weights = jnp.concatenate(
        [
            jnp.where(on_line, jnp.broadcast_to(stretched[j : j + 1, :], (lines, wide)), 0.0)
            for j in range(members)
        ],
        axis=0,
    ).astype(jnp.bfloat16)
    change = jnp.dot(weights, gathered_ref[...], preferred_element_type=jnp.float32)
    out_ref[...] = field_ref[...] + change * norm_scale


def body(
    logarithmic_diffusivity,
    starting_warmth,
    thermal_supply,
    probe_positions,
    recorded_temps,
    probe_error_sigma,
    perturb_draws,
):
    members, lines, width = logarithmic_diffusivity.shape
    owners, slabs = lax.axis_size("mem"), lax.axis_size("sp")
    order = members * owners
    norm_scale = 1.0 / math.sqrt(order - 1)
    probes = probe_positions.shape[0]
    slab = lax.axis_index("sp")

    field_flat = logarithmic_diffusivity.reshape(members * lines, width)
    gathered = lax.all_gather(field_flat.astype(jnp.bfloat16), "mem", axis=0, tiled=True)

    small = jnp.concatenate([starting_warmth, thermal_supply], axis=0)
    if slabs == 2:
        swap = [(0, 1), (1, 0)]
        field_up = field_down = lax.ppermute(field_flat, "sp", swap)
        small_up = small_down = lax.ppermute(small, "sp", swap)
    else:
        fall = [(i, i + 1) for i in range(slabs - 1)]
        rise = [(i + 1, i) for i in range(slabs - 1)]
        field_up, small_up = lax.ppermute((field_flat, small), "sp", fall)
        field_down, small_down = lax.ppermute((field_flat, small), "sp", rise)
    flags = jnp.stack([slab > 0, slab < slabs - 1]).astype(jnp.int32)
    vmem = pl.BlockSpec(memory_space=pltpu.VMEM)
    smem = pl.BlockSpec(memory_space=pltpu.SMEM)
    window = lines + 2 * STEPS
    predicted, payload = pl.pallas_call(
        conduct_kernel,
        out_shape=(
            jax.ShapeDtypeStruct((members, probes), jnp.float32),
            jax.ShapeDtypeStruct((2 * members, probes), jnp.float32),
        ),
        in_specs=[smem, smem] + [vmem] * 9,
        out_specs=(vmem, vmem),
        scratch_shapes=[
            pltpu.VMEM((window, members, width), jnp.float32),
            pltpu.VMEM((window, members, width), jnp.float32),
            pltpu.VMEM((window, width), jnp.float32),
        ],
        compiler_params=pltpu.CompilerParams(vmem_limit_bytes=16 * 1024 * 1024),
        cost_estimate=pl.CostEstimate(
            flops=30 * STEPS * window * members * width,
            bytes_accessed=4 * 3 * members * lines * width,
            transcendentals=STEPS * window * members * width,
        ),
        name="conduct",
    )(
        flags,
        probe_positions,
        field_flat,
        field_up,
        field_down,
        small,
        small_up,
        small_down,
        recorded_temps[None, :],
        probe_error_sigma[None, :],
        perturb_draws,
    )
    devices = owners * slabs
    everyone = lax.all_to_all(
        jnp.broadcast_to(payload[None], (devices,) + payload.shape), ("mem", "sp"), 0, 0
    )
    place = lax.axis_index("mem").astype(jnp.int32)[None]
    if order <= LANES:
        revised = pl.pallas_call(
            lambda *refs: update_kernel(norm_scale, slabs, *refs),
            out_shape=jax.ShapeDtypeStruct((members * lines, width), jnp.float32),
            in_specs=[smem] + [vmem] * 3,
            out_specs=vmem,
            compiler_params=pltpu.CompilerParams(vmem_limit_bytes=32 * 1024 * 1024),
            cost_estimate=pl.CostEstimate(
                flops=2 * order * order * order,
                bytes_accessed=2 * order * lines * width,
                transcendentals=0,
            ),
            name="update",
        )(place, everyone, field_flat, gathered)
    else:
        split = everyone.reshape(owners, slabs, 2, members, probes)
        normal = split[:, :, 0].transpose(0, 2, 1, 3).reshape(order, slabs * probes)
        misfit = lax.dynamic_index_in_dim(split[:, :, 1], place[0], 0, False)
        misfit = misfit.transpose(1, 0, 2).reshape(members, slabs * probes)
        scaled = (jnp.mean(normal, axis=0, keepdims=True) - normal) * norm_scale
        gram_matrix = jnp.dot(
            scaled, scaled.T, precision=lax.Precision.HIGHEST, preferred_element_type=jnp.float32
        ) + damping * jnp.eye(order, dtype=jnp.float32)
        cross_term = jnp.dot(
            scaled, misfit.T, precision=lax.Precision.HIGHEST, preferred_element_type=jnp.float32
        )
        coeff_round = eliminate(gram_matrix, cross_term).astype(jnp.bfloat16)
        change = lax.dot_general(
            coeff_round,
            gathered.reshape(order, lines * width),
            (((0,), (0,)), ((), ())),
            preferred_element_type=jnp.float32,
        ).reshape(field_flat.shape)
        revised = field_flat + change * norm_scale
    return (revised.reshape(logarithmic_diffusivity.shape), predicted)


def solution(mesh):
    in_specs = (
        P("mem", "sp", None),
        P("sp", None),
        P("sp", None),
        P("sp"),
        P("sp"),
        P("sp"),
        P("mem", "sp"),
    )
    out_specs = (P("mem", "sp", None), P("mem", "sp"))
    return jax.shard_map(body, mesh=mesh, in_specs=in_specs, out_specs=out_specs, check_vma=False)
```

time: 333 us -> 89.9 us (0.27)
  other arithmetic: 129 us -> 2.67 us
  local copies, waits for them, and re-layouts: 96.1 us -> 8.19 us
  blocking collectives: 45.7 us -> 0 us
  waiting for transfers between devices: 16.1 us -> 41.2 us
  Pallas kernels: 0 us -> 15.7 us
  starting transfers between devices: 18.1 us -> 7.61 us
  matrix products: 8.55 us -> 0 us
    div x130 -> x0, other arithmetic: 101 us -> none  [the longest x128 101 us: invert_block(): pivot_row = augmented[place] / augmented[place, place]]
    slice x245 -> x0, local copies, waits for them, and re-layouts: 86.9 us -> none  [the longest x128 76.6 us: invert_block(): pivot_row = augmented[place] / augmented[place, place]]
    all_gather x1 -> x0, blocking collectives: 42.1 us -> none  [body(): lax.all_gather(kept_prediction, 'mem', axis=0, tiled=True)]
    all_gather x1, waiting for transfers between devices: 0.03 us -> 31.8 us  [body(): lax.all_gather(field_flat.astype(jnp.bfloat16), 'mem', axis=0, tiled=True)]
    ppermute x10 -> x2, starting transfers between devices: 18.1 us -> 0.58 us  [the longest x1 0.52 us: body(): field_up = field_down = lax.ppermute(field_flat, 'sp', swap)]
    pallas_call x0 -> x2, Pallas kernels: none -> 15.7 us  [the longest x1 9 us: body(): pl.pallas_call(conduct_kernel, out_shape=(jax.ShapeDtypeStruct((members,...]
    sub x129 -> x0, other arithmetic: 10.7 us -> none  [the longest x128 10.7 us: invert_block(): augmented = augmented - augmented[:, place:place + 1] * pivot_row[None, :]]
    psum x1 -> x0, waiting for transfers between devices: 9.08 us -> none  [body(): gram_matrix, cross_term = lax.psum((gram_part, cross_part), 'sp')]
  transfers between devices with their start and end apart: 12 -> 4, of which waited for: 5 -> 3; matrix products, arithmetic and copies ran while one was open for 67% -> 4% of each run, Pallas kernels for 0% -> 10%
where the time goes in v1:
time: 89.9 us; the launch traced here: 89.5 us
  waiting for transfers between devices  41.2 us (46%)
  Pallas kernels  15.7 us (17%)
  between operations  14.1 us (16%)
  local copies, waits for them, and re-layouts  8.19 us (9%)
  starting transfers between devices  7.61 us (8%)
  other arithmetic  2.67 us (3%)
    all_gather x1, waiting for transfers between devices, body(): lax.all_gather(field_flat.astype(jnp.bfloat16), 'mem', axis=0, tiled=True)  31.8 us
    pallas_call x1, Pallas kernels, body(): pl.pallas_call(conduct_kernel, out_shape=(jax.ShapeDtypeStruct((members,...  9 us
    all_to_all x1, waiting for transfers between devices, body(): lax.all_to_all(jnp.broadcast_to(payload[None], (devices,) + payload.shape...  8.22 us
    all_to_all x1, starting transfers between devices, body(): lax.all_to_all(jnp.broadcast_to(payload[None], (devices,) + payload.shape...  7 us
    unnamed x17, local copies, waits for them, and re-layouts  6.9 us
    pallas_call x1, Pallas kernels, body(): pl.pallas_call(lambda *refs: update_kernel(norm_scale, slabs, *refs), out...  6.73 us
  transfers between devices with their start and end apart: 4, of which 3 were waited for; matrix products, arithmetic and copies ran while one was open for 4% of the time, Pallas kernels for 10%

profile of v1, /device:TPU:0, one launch (start us, length us, event | category | flops | bytes accessed | tf_op | source)
XLA Modules:
  0.0 89.5 jit_solution(6565568644479673706)
XLA Ops:
  7.2 0.0 all-gather.2.cloned.1.call-start
  7.2 1.6 %bitcast_convert_fusion = bf16[64,1024]{1,0:T(8,128)(2,1)} fusion(f32[8,8,1024]{2,1,0:T(8,128)} %param.7), kind=kLoop, calls=%fused_computation.3 | loop fusion | flops 65536 | bytes 393216 | tf_op jit(solution)/shard_map/convert_element_type | solution.py:265
  8.9 0.0 all-gather.2.cloned.1.call-update
  8.9 0.5 collective-permute-start
  9.4 0.8 constant_dynamic-update-slice_fusion.1
  10.2 0.8 constant_dynamic-update-slice_fusion.small_ref
  10.9 0.1 collective-permute-start.1
  11.0 0.1 add_convert_fusion.flags_ref
  11.1 1.1 %collective-permute-done.1.small_up_ref.small_down_ref = f32[16,1024]{1,0:T(8,128)S(1)} collective-permute-done((f32[16,1024]{1,0:T(8,128)S(1)}, f32[16,1024]{1,0:T(8,128)S(1)}, u32[]{:S(2)}, u32[]{:S(2)}) %collective-permute-start.1) | collective-permute-done | bytes 65568 | tf_op jit(solution)/shard_map/ppermute | solution.py:271
  12.2 0.9 %copy-done.1 = f32[8,8,1024]{2,1,0:T(8,128)S(1)} copy-done((f32[8,8,1024]{2,1,0:T(8,128)S(1)}, f32[8,8,1024]{2,1,0:T(8,128)}, u32[]{:S(2)}) %copy-start.1) | copy-done | bytes 262168
  13.1 0.7 copy-done.3
  13.8 0.7 copy-done.4
  14.5 0.7 copy-done.5
  15.1 0.7 copy-done.6
  15.8 9.0 %conduct.1 = (f32[8,64]{1,0:T(8,128)}, f32[16,64]{1,0:T(8,128)S(1)}) custom-call(s32[2]{0:T(128)S(1)} %add_convert_fusion.flags_ref, s32[64]{0:T(128)S(1)} %copy-done.4, f32[64,1024]{1,0:T(8,128)S(1)} %bitcast.9, f32[64,1024]{1,0:T(8,128)S(1)} %collective-permute-done.field_up_ref.field_down_ref, ...), custom_call_target="tpu_custom_call" | custom-call | flops 15728640 | bytes 786432 | tf_op jit(solution)/shard_map/conduct/pallas_call | solution.py:281
  24.8 0.8 reshape.13
  25.6 7.0 %all-to-all-start = ((f32[32,1,1024]{2,1,0:T(1,128)}), f32[32,1,1024]{2,1,0:T(1,128)S(1)}, u32[]{:S(2)}, u32[]{:S(2)}) async-start(f32[32,1,1024]{2,1,0:T(1,128)} %reshape.13), calls=%async_computation | async-start | bytes 262144 | tf_op jit(solution)/shard_map/all_to_all | solution.py:315
  32.7 8.2 %all-to-all-done = f32[32,1,1024]{2,1,0:T(1,128)S(1)} async-done(((f32[32,1,1024]{2,1,0:T(1,128)}), f32[32,1,1024]{2,1,0:T(1,128)S(1)}, u32[]{:S(2)}, u32[]{:S(2)}) %all-to-all-start) | async-done | bytes 131104 | tf_op jit(solution)/shard_map/all_to_all | solution.py:315
  40.9 0.5 broadcast.1
  41.4 0.9 %reduce = f32[32,1024]{1,0:T(8,128)S(1)} reduce(f32[32,1,1024]{2,1,0:T(1,128)S(1)} %all-to-all-done, f32[]{:T(128)} %broadcast.1), dimensions={1}, to_apply=%all_to_all.3.reduce_sub_computation | reduce | bytes 262148 | tf_op jit(solution)/shard_map/all_to_all | solution.py:315
  42.4 0.1 reshape.14.refs_1_
  42.5 31.8 %all-gather.2.cloned.1.call-done.refs_3_ = bf16[1024,1024]{1,0:T(8,128)(2,1)} async-done(((bf16[64,1024]{1,0:T(8,128)(2,1)}), bf16[1024,1024]{1,0:T(8,128)(2,1)}) %all-gather.2.cloned.1.call-update) | async-done | bytes 2097168 | tf_op jit(solution)/shard_map/all_gather | solution.py:265
  74.3 1.6 %copy-done = bf16[1024,1024]{1,0:T(8,128)(2,1)S(1)} copy-done((bf16[1024,1024]{1,0:T(8,128)(2,1)S(1)}, bf16[1024,1024]{1,0:T(8,128)(2,1)}, u32[]{:S(2)}) %copy-start) | copy-done | bytes 2097176
  75.9 6.7 %update.1 = f32[64,1024]{1,0:T(8,128)} custom-call(s32[1]{0:T(128)} %bitcast.refs_0_, f32[32,16,64]{2,1,0:T(8,128)S(1)} %reshape.14.refs_1_, f32[64,1024]{1,0:T(8,128)S(1)} %bitcast.10, bf16[1024,1024]{1,0:T(8,128)(2,1)S(1)} %copy-done), custom_call_target="tpu_custom_call" | custom-call | flops 4194304 | bytes 2097152 | tf_op jit(solution)/shard_map/update/pallas_call | solution.py:320
  (10 shorter events, 0.0 us)
Async XLA Ops:
  7.2 67.1 %copy-start.2 = (f32[8,8,1024]{2,1,0:T(8,128)S(1)}, f32[8,8,1024]{2,1,0:T(8,128)}, u32[]{:S(2)}) copy-start(f32[8,8,1024]{2,1,0:T(8,128)} %param.7) | copy-start | bytes 786436
  7.2 67.1 %all-gather.2.cloned.1.call-start = ((), (), s32[]{:S(2)}) async-start(), calls=%async_computation.1 | async-start | bytes 2228224 | tf_op jit(solution)/shard_map/all_gather | solution.py:265
  8.9 3.3 %collective-permute-start = (f32[64,1024]{1,0:T(8,128)}, f32[64,1024]{1,0:T(8,128)S(1)}, u32[]{:S(2)}, u32[]{:S(2)}) collective-permute-start(f32[64,1024]{1,0:T(8,128)} %bitcast.8), channel_id=1, source_target_pairs={{0,1},{1,0},{2,3},{3,2},{4,5},{5,4},{6,7},{7,6},{8,9},{9,8},{10,11... | collective-permute-start | bytes 786440 | tf_op jit(solution)/shard_map/ppermute | solution.py:270
  10.9 1.3 %collective-permute-start.1 = (f32[16,1024]{1,0:T(8,128)S(1)}, f32[16,1024]{1,0:T(8,128)S(1)}, u32[]{:S(2)}, u32[]{:S(2)}) collective-permute-start(f32[16,1024]{1,0:T(8,128)S(1)} %constant_dynamic-update-slice_fusion.small_ref), channel_id=1, source_target_pairs={{0,1},{1,0},{2,3},{3,2},{4,5},{5,4},{6,7},{7,6},{8,9},{9,8},{10,11... | collective-permute-start | bytes 196616 | tf_op jit(solution)/shard_map/ppermute | solution.py:271
  12.2 1.0 %copy-start.1 = (f32[8,8,1024]{2,1,0:T(8,128)S(1)}, f32[8,8,1024]{2,1,0:T(8,128)}, u32[]{:S(2)}) copy-start(f32[8,8,1024]{2,1,0:T(8,128)} %param.7) | copy-start | bytes 786436
  13.1 0.7 copy-start.3
  13.8 0.7 copy-start.4
  14.5 0.7 copy-start.5
  15.1 0.7 copy-start.6
  25.6 15.2 %all-to-all-start = ((f32[32,1,1024]{2,1,0:T(1,128)}), f32[32,1,1024]{2,1,0:T(1,128)S(1)}, u32[]{:S(2)}, u32[]{:S(2)}) async-start(f32[32,1,1024]{2,1,0:T(1,128)} %reshape.13), calls=%async_computation | async-start | bytes 262144 | tf_op jit(solution)/shard_map/all_to_all | solution.py:315
  74.3 1.6 %copy-start = (bf16[1024,1024]{1,0:T(8,128)(2,1)S(1)}, bf16[1024,1024]{1,0:T(8,128)(2,1)}, u32[]{:S(2)}) copy-start(bf16[1024,1024]{1,0:T(8,128)(2,1)} %all-gather.2.cloned.1.call-done.refs_3_) | copy-start | bytes 6291460
Sparse Core Ops, SparseCore 0:
  10.8 63.4 all-gather.1

commit v2 on v1

--- a/solution.py
+++ b/solution.py
@@ -55,44 +55,69 @@
 
 def conduct_kernel(
     flags_ref,
-    columns_ref,
+    columns_hbm,
     field_ref,
-    field_up_ref,
-    field_down_ref,
-    small_ref,
-    small_up_ref,
-    small_down_ref,
-    recorded_ref,
-    sigma_ref,
-    draws_ref,
+    up_ref,
+    down_ref,
+    warmth_hbm,
+    supply_hbm,
+    recorded_hbm,
+    sigma_hbm,
+    draws_hbm,
     predicted_ref,
     payload_ref,
     warmth,
     half_exp,
     supply,
+    columns_ref,
+    small_ref,
+    recorded_ref,
+    sigma_ref,
+    draws_ref,
+    sems,
 ):
-    members, lines, width = predicted_ref.shape[0], small_ref.shape[0] // 2, small_ref.shape[1]
+    lines = warmth_hbm.shape[0]
+    copies = [
+        pltpu.make_async_copy(source, target, sems.at[k])
+        for k, (source, target) in enumerate(
+            (
+                (warmth_hbm, small_ref.at[pl.ds(0, lines)]),
+                (supply_hbm, small_ref.at[pl.ds(lines, lines)]),
+                (columns_hbm, columns_ref),
+                (recorded_hbm, recorded_ref),
+                (sigma_hbm, sigma_ref),
+                (draws_hbm, draws_ref),
+            )
+        )
+    ]
+    for copy in copies:
+        copy.start()
+    for copy in copies:
+        copy.wait()
+    members, width = predicted_ref.shape[0], small_ref.shape[1]
     tiles = width // LANES
     window = lines + 2 * STEPS
     lane = lax.broadcasted_iota(jnp.int32, (members, LANES), 1)
     first, last = lane == 0, lane == LANES - 1
 
-    def place(row, ref, small, line, count, inside):
-        coefficient = jnp.swapaxes(ref[...].reshape(members, lines, width), 0, 1)
+    def place(row, ref, small, base, line, count, inside):
+        coefficient = jnp.swapaxes(
+            ref[0 : members * lines, :].reshape(members, lines, width), 0, 1
+        )
         for step in range(count):
             part = coefficient[line + step]
-            heat = small[pl.ds(line + step, 1), :]
+            heat = small[pl.ds(base + line + step, 1), :]
             if inside is not None:
                 part = jnp.where(inside, part, 0.0)
                 heat = jnp.where(inside, heat, 0.0)
             half_exp[row + step] = 0.5 * jnp.exp(part)
             warmth[row + step] = jnp.broadcast_to(heat, (members, width))
-        supply[pl.ds(row, count), :] = small[pl.ds(lines + line, count), :]
+        supply[pl.ds(row, count), :] = small[pl.ds(base + lines + line, count), :]
 
     above, below = flags_ref[0] > 0, flags_ref[1] > 0
-    place(0, field_up_ref, small_up_ref, lines - STEPS, STEPS, above)
-    place(STEPS, field_ref, small_ref, 0, lines, None)
-    place(STEPS + lines, field_down_ref, small_down_ref, 0, STEPS, below)
+    place(0, up_ref, up_ref, members * lines, lines - STEPS, STEPS, above)
+    place(STEPS, field_ref, small_ref, 0, 0, lines, None)
+    place(STEPS + lines, down_ref, down_ref, members * lines, 0, STEPS, below)
 
     def cut(value):
         return [value[:, k * LANES : (k + 1) * LANES] for k in range(tiles)]
@@ -158,26 +183,25 @@
     predicted = total[:, :probes]
     predicted_ref[...] = predicted
     normal = (recorded_ref[...] - predicted) / sigma_ref[...]
-    payload_ref[0:members, :] = normal
-    payload_ref[members : 2 * members, :] = normal + draws_ref[...]
-
-
-def update_kernel(norm_scale, slabs, place_ref, payload_ref, field_ref, gathered_ref, out_ref):
-    devices = payload_ref.shape[0]
-    owners = devices // slabs
-    members = payload_ref.shape[1] // 2
-    order = owners * members
-    lines = field_ref.shape[0] // members
+    payload = jnp.concatenate([normal, normal + draws_ref[...]], axis=1)
+    for device in range(payload_ref.shape[0]):
+        payload_ref[device] = payload
+
+
+def solve_kernel(norm_scale, slabs, offsets, place_ref, payload_ref, solved_ref):
+    members, probes = payload_ref.shape[1], payload_ref.shape[2] // 2
+    order = len(offsets) * members
     mine = place_ref[0]
     dims = (((1,), (1,)), ((), ()))
     gram, cross = None, None
     for slab in range(slabs):
-        normal = jnp.concatenate(
-            [payload_ref[owner * slabs + slab, 0:members, :] for owner in range(owners)], axis=0
-        )
+        blocks = [
+            payload_ref[jnp.bitwise_xor(mine, offset) * slabs + slab] for offset in offsets
+        ]
+        normal = jnp.concatenate([block[:, :probes] for block in blocks], axis=0)
         center = jnp.sum(normal, axis=0, keepdims=True) * (1.0 / order)
         scaled = (center - normal) * norm_scale
-        misfit = payload_ref[mine * slabs + slab, members : 2 * members, :]
+        misfit = jnp.concatenate([block[:, probes:] for block in blocks[:2]], axis=0)
         one = lax.dot_general(
             scaled, scaled, dims, precision=lax.Precision.HIGHEST, preferred_element_type=jnp.float32
         )
@@ -194,7 +218,7 @@
         + jnp.where(lane_id == row_id + k * ROWS, damping, 0.0)
         for k in range(blocks)
     ]
-    tableau.append(cross)
+    tableau += [cross[k : k + ROWS, :] for k in range(0, 2 * members, ROWS)]
 
     def lanes_of(value, at):
         return jnp.broadcast_to(value[:, at : at + 1], (ROWS, order))
@@ -217,14 +241,19 @@
                 factor = row_of(column[j], q) * inverse
                 column[j] = jnp.where(here, factor, column[j] - column[q] * factor)
         rows = [row_of(band, q) for q in range(ROWS)]
-        for other in range(block + 1, blocks + 1):
+        for other in range(block + 1, len(tableau)):
             value = tableau[other]
             products = [lanes_of(value, base + q) * rows[q] for q in range(ROWS)]
             while len(products) > 1:
                 products = [a + b for a, b in zip(products[::2], products[1::2])]
             tableau[other] = jnp.where(inside, 0.0, value) - products[0]
-    solved = tableau[blocks].astype(jnp.bfloat16)
-
+    solved_ref[...] = jnp.concatenate(tableau[blocks:], axis=0).astype(jnp.bfloat16)
+
+
+def apply_kernel(norm_scale, lines, solved_ref, *refs):
+    part_refs, own_ref, give_ref = refs[:-2], refs[-2], refs[-1]
+    solved = solved_ref[...]
+    pair, order = solved.shape
     wide = order * lines
     spread = (
         lax.broadcasted_iota(jnp.int32, (order, wide), 1) // lines
@@ -237,12 +266,30 @@
     weights = jnp.concatenate(
         [
             jnp.where(on_line, jnp.broadcast_to(stretched[j : j + 1, :], (lines, wide)), 0.0)
-            for j in range(members)
+            for j in range(pair)
         ],
         axis=0,
     ).astype(jnp.bfloat16)
-    change = jnp.dot(weights, gathered_ref[...], preferred_element_type=jnp.float32)
-    out_ref[...] = field_ref[...] + change * norm_scale
+    change, start = None, 0
+    for ref in part_refs:
+        deep = ref.shape[0]
+        part = jnp.dot(
+            weights[:, start : start + deep], ref[...], preferred_element_type=jnp.float32
+        )
+        change = part if change is None else change + part
+        start += deep
+    change = change * norm_scale
+    rows = own_ref.shape[0]
+    own_ref[...] = change[:rows]
+    give_ref[...] = change[rows:].astype(give_ref.dtype)
+
+
+def merge_kernel(odd_ref, field_ref, own_ref, got_ref, out_ref):
+    own, got = own_ref[...], got_ref[...].astype(jnp.float32)
+    half = own.shape[1]
+    even = odd_ref[0] == 0
+    out_ref[:, :half] = field_ref[:, :half] + jnp.where(even, own, got)
+    out_ref[:, half:] = field_ref[:, half:] + jnp.where(even, got, own)
 
 
 def body(
@@ -261,37 +308,58 @@
     probes = probe_positions.shape[0]
     slab = lax.axis_index("sp")
 
+    mine = lax.axis_index("mem").astype(jnp.int32)
+    odd = mine & 1
+    half = width // 2
+
+    def across(value, bit):
+        return lax.ppermute(value, "mem", [(i, i ^ bit) for i in range(owners)])
+
     field_flat = logarithmic_diffusivity.reshape(members * lines, width)
-    gathered = lax.all_gather(field_flat.astype(jnp.bfloat16), "mem", axis=0, tiled=True)
-
-    small = jnp.concatenate([starting_warmth, thermal_supply], axis=0)
+    field_round = field_flat.astype(jnp.bfloat16)
+    left, right = field_round[:, :half], field_round[:, half:]
+    held = jnp.where(odd == 0, left, right)
+    parts = [held, across(jnp.where(odd == 0, right, left), 1)]
+    offsets = [0, 1]
+    bit = owners // 2
+    while bit > 1:
+        held = jnp.concatenate(parts, axis=0)
+        parts = [held, across(held, bit)]
+        offsets = offsets + [offset ^ bit for offset in offsets]
+        bit //= 2
+
+    edges = jnp.concatenate([field_flat, starting_warmth, thermal_supply], axis=0)
     if slabs == 2:
-        swap = [(0, 1), (1, 0)]
-        field_up = field_down = lax.ppermute(field_flat, "sp", swap)
-        small_up = small_down = lax.ppermute(small, "sp", swap)
+        up = down = lax.ppermute(edges, "sp", [(0, 1), (1, 0)])
     else:
-        fall = [(i, i + 1) for i in range(slabs - 1)]
-        rise = [(i + 1, i) for i in range(slabs - 1)]
-        field_up, small_up = lax.ppermute((field_flat, small), "sp", fall)
-        field_down, small_down = lax.ppermute((field_flat, small), "sp", rise)
+        up = lax.ppermute(edges, "sp", [(i, i + 1) for i in range(slabs - 1)])
+        down = lax.ppermute(edges, "sp", [(i + 1, i) for i in range(slabs - 1)])
     flags = jnp.stack([slab > 0, slab < slabs - 1]).astype(jnp.int32)
     vmem = pl.BlockSpec(memory_space=pltpu.VMEM)
     smem = pl.BlockSpec(memory_space=pltpu.SMEM)
+    anywhere = pl.BlockSpec(memory_space=pl.ANY)
     window = lines + 2 * STEPS
+    devices = owners * slabs
     predicted, payload = pl.pallas_call(
         conduct_kernel,
         out_shape=(
             jax.ShapeDtypeStruct((members, probes), jnp.float32),
-            jax.ShapeDtypeStruct((2 * members, probes), jnp.float32),
+            jax.ShapeDtypeStruct((devices, members, 2 * probes), jnp.float32),
         ),
-        in_specs=[smem, smem] + [vmem] * 9,
+        in_specs=[smem, anywhere] + [vmem] * 3 + [anywhere] * 5,
         out_specs=(vmem, vmem),
         scratch_shapes=[
             pltpu.VMEM((window, members, width), jnp.float32),
             pltpu.VMEM((window, members, width), jnp.float32),
             pltpu.VMEM((window, width), jnp.float32),
+            pltpu.SMEM((probes,), jnp.int32),
+            pltpu.VMEM((2 * lines, width), jnp.float32),
+            pltpu.VMEM((1, probes), jnp.float32),
+            pltpu.VMEM((1, probes), jnp.float32),
+            pltpu.VMEM((members, probes), jnp.float32),
+            pltpu.SemaphoreType.DMA((6,)),
         ],
-        compiler_params=pltpu.CompilerParams(vmem_limit_bytes=16 * 1024 * 1024),
+        compiler_params=pltpu.CompilerParams(vmem_limit_bytes=24 * 1024 * 1024),
         cost_estimate=pl.CostEstimate(
             flops=30 * STEPS * window * members * width,
             bytes_accessed=4 * 3 * members * lines * width,
@@ -302,39 +370,34 @@
         flags,
         probe_positions,
         field_flat,
-        field_up,
-        field_down,
-        small,
-        small_up,
-        small_down,
+        up,
+        down,
+        starting_warmth,
+        thermal_supply,
         recorded_temps[None, :],
         probe_error_sigma[None, :],
         perturb_draws,
     )
-    devices = owners * slabs
-    everyone = lax.all_to_all(
-        jnp.broadcast_to(payload[None], (devices,) + payload.shape), ("mem", "sp"), 0, 0
-    )
-    place = lax.axis_index("mem").astype(jnp.int32)[None]
+    everyone = lax.all_to_all(payload, ("mem", "sp"), 0, 0, tiled=True)
     if order <= LANES:
-        revised = pl.pallas_call(
-            lambda *refs: update_kernel(norm_scale, slabs, *refs),
-            out_shape=jax.ShapeDtypeStruct((members * lines, width), jnp.float32),
-            in_specs=[smem] + [vmem] * 3,
+        solved = pl.pallas_call(
+            lambda *refs: solve_kernel(norm_scale, slabs, offsets, *refs),
+            out_shape=jax.ShapeDtypeStruct((2 * members, order), jnp.bfloat16),
+            in_specs=[smem, vmem],
             out_specs=vmem,
-            compiler_params=pltpu.CompilerParams(vmem_limit_bytes=32 * 1024 * 1024),
+            compiler_params=pltpu.CompilerParams(vmem_limit_bytes=16 * 1024 * 1024),
             cost_estimate=pl.CostEstimate(
                 flops=2 * order * order * order,
-                bytes_accessed=2 * order * lines * width,
+                bytes_accessed=4 * devices * members * 2 * probes,
                 transcendentals=0,
             ),
-            name="update",
-        )(place, everyone, field_flat, gathered)
+            name="solve",
+        )(mine[None], everyone)
     else:
-        split = everyone.reshape(owners, slabs, 2, members, probes)
-        normal = split[:, :, 0].transpose(0, 2, 1, 3).reshape(order, slabs * probes)
-        misfit = lax.dynamic_index_in_dim(split[:, :, 1], place[0], 0, False)
-        misfit = misfit.transpose(1, 0, 2).reshape(members, slabs * probes)
+        owner = mine ^ jnp.array(offsets, jnp.int32)
+        split = everyone.reshape(owners, slabs, members, 2, probes)[owner]
+        split = split.transpose(3, 0, 2, 1, 4).reshape(2, order, slabs * probes)
+        normal, misfit = split[0], split[1, : 2 * members]
         scaled = (jnp.mean(normal, axis=0, keepdims=True) - normal) * norm_scale
         gram_matrix = jnp.dot(
             scaled, scaled.T, precision=lax.Precision.HIGHEST, preferred_element_type=jnp.float32
@@ -342,14 +405,31 @@
         cross_term = jnp.dot(
             scaled, misfit.T, precision=lax.Precision.HIGHEST, preferred_element_type=jnp.float32
         )
-        coeff_round = eliminate(gram_matrix, cross_term).astype(jnp.bfloat16)
-        change = lax.dot_general(
-            coeff_round,
-            gathered.reshape(order, lines * width),
-            (((0,), (0,)), ((), ())),
-            preferred_element_type=jnp.float32,
-        ).reshape(field_flat.shape)
-        revised = field_flat + change * norm_scale
+        solved = eliminate(gram_matrix, cross_term).T.astype(jnp.bfloat16)
+    own, give = pl.pallas_call(
+        lambda *refs: apply_kernel(norm_scale, lines, *refs),
+        out_shape=(
+            jax.ShapeDtypeStruct((members * lines, half), jnp.float32),
+            jax.ShapeDtypeStruct((members * lines, half), jnp.bfloat16),
+        ),
+        in_specs=[vmem] * (1 + len(parts)),
+        out_specs=(vmem, vmem),
+        compiler_params=pltpu.CompilerParams(vmem_limit_bytes=40 * 1024 * 1024),
+        cost_estimate=pl.CostEstimate(
+            flops=4 * members * lines * order * lines * half,
+            bytes_accessed=2 * order * lines * half,
+            transcendentals=0,
+        ),
+        name="apply",
+    )(solved, *parts)
+    got = across(give, 1)
+    revised = pl.pallas_call(
+        merge_kernel,
+        out_shape=jax.ShapeDtypeStruct((members * lines, width), jnp.float32),
+        in_specs=[smem] + [vmem] * 3,
+        out_specs=vmem,
+        name="merge",
+    )(odd[None], field_flat, own, got)
     return (revised.reshape(logarithmic_diffusivity.shape), predicted)
 
 

time: 89.9 us -> 60.3 us (0.67)
  waiting for transfers between devices: 41.2 us -> 16.8 us
  blocking collectives: 0 us -> 13.7 us
  between operations: 14.1 us -> 0.75 us
  local copies, waits for them, and re-layouts: 8.19 us -> 1.96 us
  other arithmetic: 2.67 us -> 1.14 us
  starting transfers between devices: 7.61 us -> 9.12 us
  Pallas kernels: 15.7 us -> 16.6 us
    all_gather x1 -> x0, waiting for transfers between devices: 31.8 us -> none  [body(): lax.all_gather(field_flat.astype(jnp.bfloat16), 'mem', axis=0, tiled=True)]
    ppermute x2 -> x6, waiting for transfers between devices: 1.12 us -> 16.8 us  [the longest x5 16.8 us: across(): return lax.ppermute(value, 'mem', [(i, i ^ bit) for i in range(owners)])]
    all_to_all x0 -> x1, blocking collectives: none -> 13.7 us  [body(): everyone = lax.all_to_all(payload, ('mem', 'sp'), 0, 0, tiled=True)]
    ppermute x2 -> x6, starting transfers between devices: 0.58 us -> 9.12 us  [the longest x5 9.05 us: across(): return lax.ppermute(value, 'mem', [(i, i ^ bit) for i in range(owners)])]
    all_to_all x1 -> x0, waiting for transfers between devices: 8.22 us -> none  [body(): lax.all_to_all(jnp.broadcast_to(payload[None], (devices,) + payload.shape...]
    all_to_all x1 -> x0, starting transfers between devices: 7 us -> none  [body(): lax.all_to_all(jnp.broadcast_to(payload[None], (devices,) + payload.shape...]
    unnamed x17 -> x18, local copies, waits for them, and re-layouts: 6.9 us -> 1.96 us
    all_to_all x1 -> x0, other arithmetic: 0.95 us -> none  [body(): lax.all_to_all(jnp.broadcast_to(payload[None], (devices,) + payload.shape...]
  transfers between devices with their start and end apart: 4 -> 6, of which waited for: 3 -> 4; matrix products, arithmetic and copies ran while one was open for 4% -> 0% of each run, Pallas kernels for 10% -> 24%
where the time goes in v2:
time: 60.3 us; the launch traced here: 60.1 us
  waiting for transfers between devices  16.8 us (28%)
  Pallas kernels  16.6 us (28%)
  blocking collectives  13.7 us (23%)
  starting transfers between devices  9.12 us (15%)
  local copies, waits for them, and re-layouts  1.96 us (3%)
  other arithmetic  1.14 us (2%)
  between operations  0.75 us (1%)
    ppermute x5, waiting for transfers between devices, across(): return lax.ppermute(value, 'mem', [(i, i ^ bit) for i in range(owners)])  16.8 us
    all_to_all x1, blocking collectives, body(): everyone = lax.all_to_all(payload, ('mem', 'sp'), 0, 0, tiled=True)  13.7 us
    pallas_call x1, Pallas kernels, body(): pl.pallas_call(conduct_kernel, out_shape=(jax.ShapeDtypeStruct((members,...  9.67 us
    ppermute x5, starting transfers between devices, across(): return lax.ppermute(value, 'mem', [(i, i ^ bit) for i in range(owners)])  9.05 us
    pallas_call x1, Pallas kernels, body(): pl.pallas_call(lambda *refs: solve_kernel(norm_scale, slabs, offsets, *re...  4.79 us
    unnamed x18, local copies, waits for them, and re-layouts  1.96 us
    pallas_call x1, Pallas kernels, body(): pl.pallas_call(merge_kernel, out_shape=jax.ShapeDtypeStruct((members * li...  1.75 us
  transfers between devices with their start and end apart: 6, of which 4 were waited for; matrix products, arithmetic and copies ran while one was open for 0% of the time, Pallas kernels for 24%

profile of v2, /device:TPU:0, one launch (start us, length us, event | category | flops | bytes accessed | tf_op | source)
XLA Modules:
  0.0 60.1 jit_solution(4343714702999751022)
XLA Ops:
  0.6 1.0 %bitcast_convert_fusion = bf16[64,1024]{1,0:T(8,128)(2,1)S(1)} fusion(f32[8,8,1024]{2,1,0:T(8,128)} %param.7), kind=kLoop, calls=%fused_computation.7 | loop fusion | flops 65536 | bytes 393216 | tf_op jit(solution)/shard_map/convert_element_type | solution.py:319
  1.6 3.0 %collective-permute-start.1 = (bf16[64,512]{1,0:T(8,128)(2,1)S(1)}, bf16[64,512]{1,0:T(8,128)(2,1)S(1)}, u32[]{:S(2)}, u32[]{:S(2)}) collective-permute-start(bf16[64,512]{1,0:T(8,128)(2,1)S(1)} %get-tuple-element.11), channel_id=1, source_target_pairs={{0,2},{2,0},{4,6},{6,4},{8,10},{10,8},{12,14},{14,12},{16,18},{18,... | collective-permute-start | bytes 196616 | tf_op jit(solution)/shard_map/ppermute | solution.py:316
  4.6 2.2 %collective-permute-done.1 = bf16[64,512]{1,0:T(8,128)(2,1)S(1)} collective-permute-done((bf16[64,512]{1,0:T(8,128)(2,1)S(1)}, bf16[64,512]{1,0:T(8,128)(2,1)S(1)}, u32[]{:S(2)}, u32[]{:S(2)}) %collective-permute-start.1) | collective-permute-done | bytes 65568 | tf_op jit(solution)/shard_map/ppermute | solution.py:316
  6.9 0.0 copy-start
  6.9 3.2 %collective-permute-start.2 = (bf16[128,512]{1,0:T(8,128)(2,1)S(1)}, bf16[128,512]{1,0:T(8,128)(2,1)S(1)}, u32[]{:S(2)}, u32[]{:S(2)}) collective-permute-start(bf16[128,512]{1,0:T(8,128)(2,1)S(1)} %pad_maximum_fusion.3), channel_id=1, source_target_pairs={{0,16},{2,18},{4,20},{6,22},{8,24},{10,26},{12,28},{14,30},{16,0},... | collective-permute-start | bytes 393224 | tf_op jit(solution)/shard_map/ppermute | solution.py:316
  10.1 5.2 %collective-permute-done.2 = bf16[128,512]{1,0:T(8,128)(2,1)S(1)} collective-permute-done((bf16[128,512]{1,0:T(8,128)(2,1)S(1)}, bf16[128,512]{1,0:T(8,128)(2,1)S(1)}, u32[]{:S(2)}, u32[]{:S(2)}) %collective-permute-start.2) | collective-permute-done | bytes 131104 | tf_op jit(solution)/shard_map/ppermute | solution.py:316
  15.3 0.8 %collective-permute-start.3 = (bf16[256,512]{1,0:T(8,128)(2,1)S(1)}, bf16[256,512]{1,0:T(8,128)(2,1)S(1)}, u32[]{:S(2)}, u32[]{:S(2)}) collective-permute-start(bf16[256,512]{1,0:T(8,128)(2,1)S(1)} %pad_maximum_fusion.2), channel_id=1, source_target_pairs={{0,8},{2,10},{4,12},{6,14},{8,0},{10,2},{12,4},{14,6},{16,24},{18,... | collective-permute-start | bytes 786440 | tf_op jit(solution)/shard_map/ppermute | solution.py:316
  16.1 0.1 collective-permute-start
  16.2 5.5 %collective-permute-done.3 = bf16[256,512]{1,0:T(8,128)(2,1)S(1)} collective-permute-done((bf16[256,512]{1,0:T(8,128)(2,1)S(1)}, bf16[256,512]{1,0:T(8,128)(2,1)S(1)}, u32[]{:S(2)}, u32[]{:S(2)}) %collective-permute-start.3) | collective-permute-done | bytes 262176 | tf_op jit(solution)/shard_map/ppermute | solution.py:316
  21.8 1.6 %collective-permute-start.4 = (bf16[512,512]{1,0:T(8,128)(2,1)S(1)}, bf16[512,512]{1,0:T(8,128)(2,1)S(1)}, u32[]{:S(2)}, u32[]{:S(2)}) collective-permute-start(bf16[512,512]{1,0:T(8,128)(2,1)S(1)} %pad_maximum_fusion.refs_1_), channel_id=1, source_target_pairs={{0,4},{2,6},{4,0},{6,2},{8,12},{10,14},{12,8},{14,10},{16,20},{18,... | collective-permute-start | bytes 1572872 | tf_op jit(solution)/shard_map/ppermute | solution.py:316
  23.4 0.1 add_convert_fusion.flags_ref
  23.5 0.6 copy-done.4
  24.1 0.0 copy-done.5
  24.1 0.0 copy-done.6
  24.2 0.0 copy-done.7
  24.2 9.7 %conduct.1 = (f32[8,64]{1,0:T(8,128)}, f32[32,8,128]{2,1,0:T(8,128)S(1)}) custom-call(s32[2]{0:T(128)S(1)} %add_convert_fusion.flags_ref, s32[64]{0:T(128)S(1)} %copy-done.5, f32[64,1024]{1,0:T(8,128)S(1)} %bitcast.11, f32[80,1024]{1,0:T(8,128)S(1)} %collective-permute-done.up_ref.down_ref, f32[80,1024]{1,0:T(8,128)S(1)} %collective-permute-done.up_ref.down_ref, ...), custom_call_target="tpu_custom_call" | custom-call | flops 15728640 | bytes 786432 | tf_op jit(solution)/shard_map/conduct/pallas_call | solution.py:343
  33.9 13.7 %all_to_all.5.refs_1_ = f32[32,8,128]{2,1,0:T(8,128)S(1)} all-to-all(f32[32,8,128]{2,1,0:T(8,128)S(1)} %get-tuple-element.6), channel_id=1, replica_groups=mesh['mem'=16,'sp'=2] {'mem','sp'}, dimensions={0} | all-to-all | bytes 262144 | tf_op jit(solution)/shard_map/all_to_all | solution.py:381
  47.6 4.8 %solve.1.refs_0_ = bf16[16,128]{1,0:T(8,128)(2,1)S(1)} custom-call(s32[1]{0:T(128)} %bitcast.2.refs_0_, f32[32,8,128]{2,1,0:T(8,128)S(1)} %all_to_all.5.refs_1_), custom_call_target="tpu_custom_call" | custom-call | flops 4194304 | bytes 131072 | tf_op jit(solution)/shard_map/solve/pallas_call | solution.py:383
  52.4 0.4 apply.1
  52.8 0.6 %copy-done.1 = f32[64,512]{1,0:T(8,128)} copy-done((f32[64,512]{1,0:T(8,128)}, f32[64,512]{1,0:T(8,128)S(1)}, u32[]{:S(2)}) %copy-start.1) | copy-done | bytes 131096
  53.5 0.4 collective-permute-start.5
  53.9 3.8 %collective-permute-done.5.got_ref = bf16[64,512]{1,0:T(8,128)(2,1)S(1)} collective-permute-done((bf16[64,512]{1,0:T(8,128)(2,1)S(1)}, bf16[64,512]{1,0:T(8,128)(2,1)S(1)}, u32[]{:S(2)}, u32[]{:S(2)}) %collective-permute-start.5) | collective-permute-done | bytes 65568 | tf_op jit(solution)/shard_map/ppermute | solution.py:316
  57.7 0.6 %copy-done.8 = bf16[64,512]{1,0:T(8,128)(2,1)} copy-done((bf16[64,512]{1,0:T(8,128)(2,1)}, bf16[64,512]{1,0:T(8,128)(2,1)S(1)}, u32[]{:S(2)}) %copy-start.8) | copy-done | bytes 65560
  58.3 1.8 %merge.1 = f32[64,1024]{1,0:T(8,128)} custom-call(s32[1]{0:T(128)} %bitcast.odd_ref, f32[64,1024]{1,0:T(8,128)} %bitcast.9, f32[64,512]{1,0:T(8,128)} %copy-done.1, bf16[64,512]{1,0:T(8,128)(2,1)} %copy-done.8), custom_call_target="tpu_custom_call" | custom-call | tf_op jit(solution)/shard_map/merge/pallas_call | solution.py:426
  (18 shorter events, 0.1 us)
Async XLA Ops:
  1.6 5.2 %collective-permute-start.1 = (bf16[64,512]{1,0:T(8,128)(2,1)S(1)}, bf16[64,512]{1,0:T(8,128)(2,1)S(1)}, u32[]{:S(2)}, u32[]{:S(2)}) collective-permute-start(bf16[64,512]{1,0:T(8,128)(2,1)S(1)} %get-tuple-element.11), channel_id=1, source_target_pairs={{0,2},{2,0},{4,6},{6,4},{8,10},{10,8},{12,14},{14,12},{16,18},{18,... | collective-permute-start | bytes 196616 | tf_op jit(solution)/shard_map/ppermute | solution.py:316
  6.9 9.2 %copy-start = (f32[8,8,1024]{2,1,0:T(8,128)S(1)}, f32[8,8,1024]{2,1,0:T(8,128)}, u32[]{:S(2)}) copy-start(f32[8,8,1024]{2,1,0:T(8,128)} %param.7) | copy-start | bytes 786436
  6.9 9.2 %copy-start.2 = (f32[8,1024]{1,0:T(8,128)S(1)}, f32[8,1024]{1,0:T(8,128)}, u32[]{:S(2)}) copy-start(f32[8,1024]{1,0:T(8,128)} %supply_hbm.1) | copy-start | bytes 98308
  6.9 9.2 %copy-start.3 = (f32[8,1024]{1,0:T(8,128)S(1)}, f32[8,1024]{1,0:T(8,128)}, u32[]{:S(2)}) copy-start(f32[8,1024]{1,0:T(8,128)} %warmth_hbm.1) | copy-start | bytes 98308
  6.9 8.3 %collective-permute-start.2 = (bf16[128,512]{1,0:T(8,128)(2,1)S(1)}, bf16[128,512]{1,0:T(8,128)(2,1)S(1)}, u32[]{:S(2)}, u32[]{:S(2)}) collective-permute-start(bf16[128,512]{1,0:T(8,128)(2,1)S(1)} %pad_maximum_fusion.3), channel_id=1, source_target_pairs={{0,16},{2,18},{4,20},{6,22},{8,24},{10,26},{12,28},{14,30},{16,0},... | collective-permute-start | bytes 393224 | tf_op jit(solution)/shard_map/ppermute | solution.py:316
  15.3 6.4 %collective-permute-start.3 = (bf16[256,512]{1,0:T(8,128)(2,1)S(1)}, bf16[256,512]{1,0:T(8,128)(2,1)S(1)}, u32[]{:S(2)}, u32[]{:S(2)}) collective-permute-start(bf16[256,512]{1,0:T(8,128)(2,1)S(1)} %pad_maximum_fusion.2), channel_id=1, source_target_pairs={{0,8},{2,10},{4,12},{6,14},{8,0},{10,2},{12,4},{14,6},{16,24},{18,... | collective-permute-start | bytes 786440 | tf_op jit(solution)/shard_map/ppermute | solution.py:316
  16.1 7.4 %collective-permute-start = (f32[80,1024]{1,0:T(8,128)S(1)}, f32[80,1024]{1,0:T(8,128)S(1)}, u32[]{:S(2)}, u32[]{:S(2)}) collective-permute-start(f32[80,1024]{1,0:T(8,128)S(1)} %pad_maximum_fusion.1), channel_id=1, source_target_pairs={{0,1},{1,0},{2,3},{3,2},{4,5},{5,4},{6,7},{7,6},{8,9},{9,8},{10,11... | collective-permute-start | bytes 983048 | tf_op jit(solution)/shard_map/ppermute | solution.py:333
  21.8 30.6 %collective-permute-start.4 = (bf16[512,512]{1,0:T(8,128)(2,1)S(1)}, bf16[512,512]{1,0:T(8,128)(2,1)S(1)}, u32[]{:S(2)}, u32[]{:S(2)}) collective-permute-start(bf16[512,512]{1,0:T(8,128)(2,1)S(1)} %pad_maximum_fusion.refs_1_), channel_id=1, source_target_pairs={{0,4},{2,6},{4,0},{6,2},{8,12},{10,14},{12,8},{14,10},{16,20},{18,... | collective-permute-start | bytes 1572872 | tf_op jit(solution)/shard_map/ppermute | solution.py:316
  23.4 0.7 %copy-start.4 = (f32[8,64]{1,0:T(8,128)S(1)}, f32[8,64]{1,0:T(8,128)}, u32[]{:S(2)}) copy-start(f32[8,64]{1,0:T(8,128)} %draws_hbm.1) | copy-start | bytes 6148
  23.5 0.7 %copy-start.5 = (s32[64]{0:T(128)S(1)}, s32[64]{0:T(128)}, u32[]{:S(2)}) copy-start(s32[64]{0:T(128)} %columns_hbm.1) | copy-start | bytes 772
  23.5 0.7 %copy-start.6 = (f32[64]{0:T(128)S(1)}, f32[64]{0:T(128)}, u32[]{:S(2)}) copy-start(f32[64]{0:T(128)} %param.11) | copy-start | bytes 772
  23.5 0.7 %copy-start.7 = (f32[64]{0:T(128)S(1)}, f32[64]{0:T(128)}, u32[]{:S(2)}) copy-start(f32[64]{0:T(128)} %param.12) | copy-start | bytes 772
  52.8 0.7 %copy-start.1 = (f32[64,512]{1,0:T(8,128)}, f32[64,512]{1,0:T(8,128)S(1)}, u32[]{:S(2)}) copy-start(f32[64,512]{1,0:T(8,128)S(1)} %get-tuple-element.7.own_ref) | copy-start | bytes 393220
  53.5 4.3 %collective-permute-start.5 = (bf16[64,512]{1,0:T(8,128)(2,1)S(1)}, bf16[64,512]{1,0:T(8,128)(2,1)S(1)}, u32[]{:S(2)}, u32[]{:S(2)}) collective-permute-start(bf16[64,512]{1,0:T(8,128)(2,1)S(1)} %get-tuple-element.8), channel_id=1, source_target_pairs={{0,2},{2,0},{4,6},{6,4},{8,10},{10,8},{12,14},{14,12},{16,18},{18,... | collective-permute-start | bytes 196616 | tf_op jit(solution)/shard_map/ppermute | solution.py:316
  57.7 0.6 %copy-start.8 = (bf16[64,512]{1,0:T(8,128)(2,1)}, bf16[64,512]{1,0:T(8,128)(2,1)S(1)}, u32[]{:S(2)}) copy-start(bf16[64,512]{1,0:T(8,128)(2,1)S(1)} %collective-permute-done.5.got_ref) | copy-start | bytes 196612

commit v3 on v2

--- a/solution.py
+++ b/solution.py
@@ -92,32 +92,37 @@
     ]
     for copy in copies:
         copy.start()
-    for copy in copies:
-        copy.wait()
     members, width = predicted_ref.shape[0], small_ref.shape[1]
     tiles = width // LANES
     window = lines + 2 * STEPS
     lane = lax.broadcasted_iota(jnp.int32, (members, LANES), 1)
     first, last = lane == 0, lane == LANES - 1
 
-    def place(row, ref, small, base, line, count, inside):
+    above, below = flags_ref[0] > 0, flags_ref[1] > 0
+    sides = (
+        (0, up_ref, lines - STEPS, STEPS, above),
+        (STEPS, field_ref, 0, lines, None),
+        (STEPS + lines, down_ref, 0, STEPS, below),
+    )
+    for row, ref, line, count, inside in sides:
         coefficient = jnp.swapaxes(
             ref[0 : members * lines, :].reshape(members, lines, width), 0, 1
         )
         for step in range(count):
             part = coefficient[line + step]
+            if inside is not None:
+                part = jnp.where(inside, part, 0.0)
+            half_exp[row + step] = 0.5 * jnp.exp(part)
+    copies[0].wait()
+    copies[1].wait()
+    for row, ref, line, count, inside in sides:
+        small, base = (small_ref, 0) if inside is None else (ref, members * lines)
+        for step in range(count):
             heat = small[pl.ds(base + line + step, 1), :]
             if inside is not None:
-                part = jnp.where(inside, part, 0.0)
                 heat = jnp.where(inside, heat, 0.0)
-            half_exp[row + step] = 0.5 * jnp.exp(part)
             warmth[row + step] = jnp.broadcast_to(heat, (members, width))
         supply[pl.ds(row, count), :] = small[pl.ds(base + lines + line, count), :]
-
-    above, below = flags_ref[0] > 0, flags_ref[1] > 0
-    place(0, up_ref, up_ref, members * lines, lines - STEPS, STEPS, above)
-    place(STEPS, field_ref, small_ref, 0, 0, lines, None)
-    place(STEPS + lines, down_ref, down_ref, members * lines, 0, STEPS, below)
 
     def cut(value):
         return [value[:, k * LANES : (k + 1) * LANES] for k in range(tiles)]
@@ -166,8 +171,10 @@
                 )
             return t_next, c_next, down
 
-        lax.fori_loop(low, high, one_row, (t_here, c_here, flow_up))
-
+        lax.fori_loop(low, high, one_row, (t_here, c_here, flow_up), unroll=True)
+
+    for copy in copies[2:]:
+        copy.wait()
     probes = predicted_ref.shape[1]
     lane_probe = lax.broadcasted_iota(jnp.int32, (members, LANES), 1)
     picked = [zero for _ in range(4)]
@@ -322,10 +329,13 @@
     parts = [held, across(jnp.where(odd == 0, right, left), 1)]
     offsets = [0, 1]
     bit = owners // 2
-    while bit > 1:
+
+    def exchange(parts, offsets, bit):
         held = jnp.concatenate(parts, axis=0)
-        parts = [held, across(held, bit)]
-        offsets = offsets + [offset ^ bit for offset in offsets]
+        return [held, across(held, bit)], offsets + [offset ^ bit for offset in offsets]
+
+    if bit > 1:
+        parts, offsets = exchange(parts, offsets, bit)
         bit //= 2
 
     edges = jnp.concatenate([field_flat, starting_warmth, thermal_supply], axis=0)
@@ -378,6 +388,10 @@
         probe_error_sigma[None, :],
         perturb_draws,
     )
+    payload, *parts = lax.optimization_barrier((payload, *parts))
+    while bit > 1:
+        parts, offsets = exchange(parts, offsets, bit)
+        bit //= 2
     everyone = lax.all_to_all(payload, ("mem", "sp"), 0, 0, tiled=True)
     if order <= LANES:
         solved = pl.pallas_call(
@@ -428,6 +442,7 @@
         out_shape=jax.ShapeDtypeStruct((members * lines, width), jnp.float32),
         in_specs=[smem] + [vmem] * 3,
         out_specs=vmem,
+        compiler_params=pltpu.CompilerParams(vmem_limit_bytes=8 * 1024 * 1024),
         name="merge",
     )(odd[None], field_flat, own, got)
     return (revised.reshape(logarithmic_diffusivity.shape), predicted)

time: 60.3 us -> 49.9 us (0.83)
  Pallas kernels: 16.6 us -> 11.5 us
  waiting for transfers between devices: 16.8 us -> 12.6 us
  local copies, waits for them, and re-layouts: 1.96 us -> 0.71 us
  starting transfers between devices: 9.12 us -> 9.74 us
    ppermute x5, waiting for transfers between devices: 16.8 us -> 12.6 us  [across(): return lax.ppermute(value, 'mem', [(i, i ^ bit) for i in range(owners)])]
    pallas_call x1, Pallas kernels: 9.67 us -> 5.59 us  [body(): pl.pallas_call(conduct_kernel, out_shape=(jax.ShapeDtypeStruct((members,...]
    unnamed x18 -> x16, local copies, waits for them, and re-layouts: 1.96 us -> 0.69 us
    concatenate x1, other arithmetic: 0.02 us -> 1.06 us  [body(): jnp.concatenate([field_flat, starting_warmth, thermal_supply], axis=0)]
    pallas_call x1, Pallas kernels: 1.75 us -> 0.74 us  [body(): pl.pallas_call(merge_kernel, out_shape=jax.ShapeDtypeStruct((members * li...]
    convert_element_type x1, other arithmetic: 0.97 us -> 0.01 us  [body(): field_round = field_flat.astype(jnp.bfloat16)]
  transfers between devices with their start and end apart: 6 -> 6, of which waited for: 4 -> 3; matrix products, arithmetic and copies ran while one was open for 0% -> 0% of each run, Pallas kernels for 24% -> 21%
where the time goes in v3:
time: 49.9 us; the launch traced here: 49.7 us
  blocking collectives  13.2 us (26%)
  waiting for transfers between devices  12.6 us (25%)
  Pallas kernels  11.5 us (23%)
  starting transfers between devices  9.74 us (20%)
  other arithmetic  1.19 us (2%)
  between operations  0.75 us (2%)
  local copies, waits for them, and re-layouts  0.71 us (1%)
    all_to_all x1, blocking collectives, body(): everyone = lax.all_to_all(payload, ('mem', 'sp'), 0, 0, tiled=True)  13.2 us
    ppermute x5, waiting for transfers between devices, across(): return lax.ppermute(value, 'mem', [(i, i ^ bit) for i in range(owners)])  12.6 us
    ppermute x5, starting transfers between devices, across(): return lax.ppermute(value, 'mem', [(i, i ^ bit) for i in range(owners)])  9.22 us
    pallas_call x1, Pallas kernels, body(): pl.pallas_call(conduct_kernel, out_shape=(jax.ShapeDtypeStruct((members,...  5.59 us
    pallas_call x1, Pallas kernels, body(): pl.pallas_call(lambda *refs: solve_kernel(norm_scale, slabs, offsets, *re...  4.79 us
    concatenate x1, other arithmetic, body(): jnp.concatenate([field_flat, starting_warmth, thermal_supply], axis=0)  1.06 us
  transfers between devices with their start and end apart: 6, of which 3 were waited for; matrix products, arithmetic and copies ran while one was open for 0% of the time, Pallas kernels for 21%

profile of v3, /device:TPU:0, one launch (start us, length us, event | category | flops | bytes accessed | tf_op | source)
XLA Modules:
  0.0 49.7 jit_solution(17040052072162090624)
XLA Ops:
  0.6 0.0 copy-start
  0.6 1.1 %pad_maximum_fusion = f32[80,1024]{1,0:T(8,128)S(1)} fusion(f32[8,1024]{1,0:T(8,128)} %supply_hbm.1, f32[8,1024]{1,0:T(8,128)} %warmth_hbm.1, f32[64,1024]{1,0:T(8,128)} %bitcast.9), kind=kLoop, calls=%fused_computation | loop fusion | flops 163840 | bytes 655360 | tf_op jit(solution)/shard_map/concatenate | solution.py:341
  1.7 0.5 %collective-permute-start = (f32[80,1024]{1,0:T(8,128)S(1)}, f32[80,1024]{1,0:T(8,128)S(1)}, u32[]{:S(2)}, u32[]{:S(2)}) collective-permute-start(f32[80,1024]{1,0:T(8,128)S(1)} %pad_maximum_fusion), channel_id=1, source_target_pairs={{0,1},{1,0},{2,3},{3,2},{4,5},{5,4},{6,7},{7,6},{8,9},{9,8},{10,11... | collective-permute-start | bytes 983048 | tf_op jit(solution)/shard_map/ppermute | solution.py:343
  2.3 2.6 %collective-permute-start.1 = (bf16[64,512]{1,0:T(8,128)(2,1)S(1)}, bf16[64,512]{1,0:T(8,128)(2,1)S(1)}, u32[]{:S(2)}, u32[]{:S(2)}) collective-permute-start(bf16[64,512]{1,0:T(8,128)(2,1)S(1)} %get-tuple-element.17), channel_id=1, source_target_pairs={{0,2},{2,0},{4,6},{6,4},{8,10},{10,8},{12,14},{14,12},{16,18},{18,... | collective-permute-start | bytes 196616 | tf_op jit(solution)/shard_map/ppermute | solution.py:323
  4.8 2.7 %collective-permute-done.1 = bf16[64,512]{1,0:T(8,128)(2,1)S(1)} collective-permute-done((bf16[64,512]{1,0:T(8,128)(2,1)S(1)}, bf16[64,512]{1,0:T(8,128)(2,1)S(1)}, u32[]{:S(2)}, u32[]{:S(2)}) %collective-permute-start.1) | collective-permute-done | bytes 65568 | tf_op jit(solution)/shard_map/ppermute | solution.py:323
  7.6 2.9 %collective-permute-start.2 = (bf16[128,512]{1,0:T(8,128)(2,1)S(1)}, bf16[128,512]{1,0:T(8,128)(2,1)S(1)}, u32[]{:S(2)}, u32[]{:S(2)}) collective-permute-start(bf16[128,512]{1,0:T(8,128)(2,1)S(1)} %pad_maximum_fusion.2), channel_id=1, source_target_pairs={{0,16},{2,18},{4,20},{6,22},{8,24},{10,26},{12,28},{14,30},{16,0},... | collective-permute-start | bytes 393224 | tf_op jit(solution)/shard_map/ppermute | solution.py:323
  10.5 0.1 add_convert_fusion.flags_ref
  10.6 0.0 collective-permute-done.up_ref.down_ref
  10.6 0.6 %copy-done.3 = f32[8,64]{1,0:T(8,128)S(1)} copy-done((f32[8,64]{1,0:T(8,128)S(1)}, f32[8,64]{1,0:T(8,128)}, u32[]{:S(2)}) %copy-start.3) | copy-done | bytes 2072
  11.2 0.0 copy-done.4
  11.2 0.0 copy-done.5
  11.3 0.0 copy-done.6
  11.3 5.6 %conduct.1 = (f32[8,64]{1,0:T(8,128)}, f32[32,8,128]{2,1,0:T(8,128)S(1)}) custom-call(s32[2]{0:T(128)S(1)} %add_convert_fusion.flags_ref, s32[64]{0:T(128)S(1)} %copy-done.4, f32[64,1024]{1,0:T(8,128)S(1)} %bitcast.10, f32[80,1024]{1,0:T(8,128)S(1)} %collective-permute-done.up_ref.down_ref, f32[80,1024]{1,0:T(8,128)S(1)} %collective-permute-done.up_ref.down_ref, ...), custom_call_target="tpu_custom_call" | custom-call | flops 15728640 | bytes 786432 | tf_op jit(solution)/shard_map/conduct/pallas_call | solution.py:353
  16.9 0.0 collective-permute-done.2
  16.9 1.6 %collective-permute-start.3 = (bf16[256,512]{1,0:T(8,128)(2,1)S(1)}, bf16[256,512]{1,0:T(8,128)(2,1)S(1)}, u32[]{:S(2)}, u32[]{:S(2)}) collective-permute-start(bf16[256,512]{1,0:T(8,128)(2,1)S(1)} %pad_maximum_fusion.1), channel_id=1, source_target_pairs={{0,8},{2,10},{4,12},{6,14},{8,0},{10,2},{12,4},{14,6},{16,24},{18,... | collective-permute-start | bytes 786440 | tf_op jit(solution)/shard_map/ppermute | solution.py:323
  18.6 6.0 %collective-permute-done.3 = bf16[256,512]{1,0:T(8,128)(2,1)S(1)} collective-permute-done((bf16[256,512]{1,0:T(8,128)(2,1)S(1)}, bf16[256,512]{1,0:T(8,128)(2,1)S(1)}, u32[]{:S(2)}, u32[]{:S(2)}) %collective-permute-start.3) | collective-permute-done | bytes 262176 | tf_op jit(solution)/shard_map/ppermute | solution.py:323
  24.6 1.6 %collective-permute-start.4 = (bf16[512,512]{1,0:T(8,128)(2,1)S(1)}, bf16[512,512]{1,0:T(8,128)(2,1)S(1)}, u32[]{:S(2)}, u32[]{:S(2)}) collective-permute-start(bf16[512,512]{1,0:T(8,128)(2,1)S(1)} %constant_dynamic-update-slice_fusion.refs_1_), channel_id=1, source_target_pairs={{0,4},{2,6},{4,0},{6,2},{8,12},{10,14},{12,8},{14,10},{16,20},{18,... | collective-permute-start | bytes 1572872 | tf_op jit(solution)/shard_map/ppermute | solution.py:323
  26.2 13.2 %all_to_all.5.refs_1_ = f32[32,8,128]{2,1,0:T(8,128)S(1)} all-to-all(f32[32,8,128]{2,1,0:T(8,128)S(1)} %get-tuple-element.10), channel_id=1, replica_groups=mesh['mem'=16,'sp'=2] {'mem','sp'}, dimensions={0} | all-to-all | bytes 262144 | tf_op jit(solution)/shard_map/all_to_all | solution.py:395
  39.5 4.8 %solve.1.refs_0_ = bf16[16,128]{1,0:T(8,128)(2,1)S(1)} custom-call(s32[1]{0:T(128)} %bitcast.2.refs_0_, f32[32,8,128]{2,1,0:T(8,128)S(1)} %all_to_all.5.refs_1_), custom_call_target="tpu_custom_call" | custom-call | flops 4194304 | bytes 131072 | tf_op jit(solution)/shard_map/solve/pallas_call | solution.py:397
  44.2 0.0 collective-permute-done.4.refs_2_
  44.3 0.4 apply.1
  44.7 0.5 %collective-permute-start.5 = (bf16[64,512]{1,0:T(8,128)(2,1)S(1)}, bf16[64,512]{1,0:T(8,128)(2,1)S(1)}, u32[]{:S(2)}, u32[]{:S(2)}) collective-permute-start(bf16[64,512]{1,0:T(8,128)(2,1)S(1)} %get-tuple-element.14), channel_id=1, source_target_pairs={{0,2},{2,0},{4,6},{6,4},{8,10},{10,8},{12,14},{14,12},{16,18},{18,... | collective-permute-start | bytes 196616 | tf_op jit(solution)/shard_map/ppermute | solution.py:323
  45.2 3.8 %collective-permute-done.5.got_ref = bf16[64,512]{1,0:T(8,128)(2,1)S(1)} collective-permute-done((bf16[64,512]{1,0:T(8,128)(2,1)S(1)}, bf16[64,512]{1,0:T(8,128)(2,1)S(1)}, u32[]{:S(2)}, u32[]{:S(2)}) %collective-permute-start.5) | collective-permute-done | bytes 65568 | tf_op jit(solution)/shard_map/ppermute | solution.py:323
  49.0 0.7 %merge.1 = f32[64,1024]{1,0:T(8,128)} custom-call(s32[1]{0:T(128)} %bitcast.odd_ref, f32[64,1024]{1,0:T(8,128)S(1)} %bitcast.11, f32[64,512]{1,0:T(8,128)S(1)} %get-tuple-element.13.own_ref, bf16[64,512]{1,0:T(8,128)(2,1)S(1)} %collective-permute-done.5.got_ref), custom_call_target="tpu_custom_call" | custom-call | tf_op jit(solution)/shard_map/merge/pallas_call | solution.py:440
  (16 shorter events, 0.1 us)
Async XLA Ops:
  0.6 1.6 %copy-start = (f32[8,8,1024]{2,1,0:T(8,128)S(1)}, f32[8,8,1024]{2,1,0:T(8,128)}, u32[]{:S(2)}) copy-start(f32[8,8,1024]{2,1,0:T(8,128)} %param.7) | copy-start | bytes 786436
  1.7 8.9 %collective-permute-start = (f32[80,1024]{1,0:T(8,128)S(1)}, f32[80,1024]{1,0:T(8,128)S(1)}, u32[]{:S(2)}, u32[]{:S(2)}) collective-permute-start(f32[80,1024]{1,0:T(8,128)S(1)} %pad_maximum_fusion), channel_id=1, source_target_pairs={{0,1},{1,0},{2,3},{3,2},{4,5},{5,4},{6,7},{7,6},{8,9},{9,8},{10,11... | collective-permute-start | bytes 983048 | tf_op jit(solution)/shard_map/ppermute | solution.py:343
  2.3 5.3 %collective-permute-start.1 = (bf16[64,512]{1,0:T(8,128)(2,1)S(1)}, bf16[64,512]{1,0:T(8,128)(2,1)S(1)}, u32[]{:S(2)}, u32[]{:S(2)}) collective-permute-start(bf16[64,512]{1,0:T(8,128)(2,1)S(1)} %get-tuple-element.17), channel_id=1, source_target_pairs={{0,2},{2,0},{4,6},{6,4},{8,10},{10,8},{12,14},{14,12},{16,18},{18,... | collective-permute-start | bytes 196616 | tf_op jit(solution)/shard_map/ppermute | solution.py:323
  7.6 3.0 %copy-start.1 = (f32[8,1024]{1,0:T(8,128)S(1)}, f32[8,1024]{1,0:T(8,128)}, u32[]{:S(2)}) copy-start(f32[8,1024]{1,0:T(8,128)} %supply_hbm.1) | copy-start | bytes 98308
  7.6 3.0 %copy-start.2 = (f32[8,1024]{1,0:T(8,128)S(1)}, f32[8,1024]{1,0:T(8,128)}, u32[]{:S(2)}) copy-start(f32[8,1024]{1,0:T(8,128)} %warmth_hbm.1) | copy-start | bytes 98308
  7.6 9.3 %collective-permute-start.2 = (bf16[128,512]{1,0:T(8,128)(2,1)S(1)}, bf16[128,512]{1,0:T(8,128)(2,1)S(1)}, u32[]{:S(2)}, u32[]{:S(2)}) collective-permute-start(bf16[128,512]{1,0:T(8,128)(2,1)S(1)} %pad_maximum_fusion.2), channel_id=1, source_target_pairs={{0,16},{2,18},{4,20},{6,22},{8,24},{10,26},{12,28},{14,30},{16,0},... | collective-permute-start | bytes 393224 | tf_op jit(solution)/shard_map/ppermute | solution.py:323
  10.5 0.7 %copy-start.3 = (f32[8,64]{1,0:T(8,128)S(1)}, f32[8,64]{1,0:T(8,128)}, u32[]{:S(2)}) copy-start(f32[8,64]{1,0:T(8,128)} %draws_hbm.1) | copy-start | bytes 6148
  10.6 0.7 %copy-start.4 = (s32[64]{0:T(128)S(1)}, s32[64]{0:T(128)}, u32[]{:S(2)}) copy-start(s32[64]{0:T(128)} %columns_hbm.1) | copy-start | bytes 772
  10.6 0.7 %copy-start.5 = (f32[64]{0:T(128)S(1)}, f32[64]{0:T(128)}, u32[]{:S(2)}) copy-start(f32[64]{0:T(128)} %param.11) | copy-start | bytes 772
  10.6 0.7 %copy-start.6 = (f32[64]{0:T(128)S(1)}, f32[64]{0:T(128)}, u32[]{:S(2)}) copy-start(f32[64]{0:T(128)} %param.12) | copy-start | bytes 772
  16.9 7.7 %collective-permute-start.3 = (bf16[256,512]{1,0:T(8,128)(2,1)S(1)}, bf16[256,512]{1,0:T(8,128)(2,1)S(1)}, u32[]{:S(2)}, u32[]{:S(2)}) collective-permute-start(bf16[256,512]{1,0:T(8,128)(2,1)S(1)} %pad_maximum_fusion.1), channel_id=1, source_target_pairs={{0,8},{2,10},{4,12},{6,14},{8,0},{10,2},{12,4},{14,6},{16,24},{18,... | collective-permute-start | bytes 786440 | tf_op jit(solution)/shard_map/ppermute | solution.py:323
  24.6 19.6 %collective-permute-start.4 = (bf16[512,512]{1,0:T(8,128)(2,1)S(1)}, bf16[512,512]{1,0:T(8,128)(2,1)S(1)}, u32[]{:S(2)}, u32[]{:S(2)}) collective-permute-start(bf16[512,512]{1,0:T(8,128)(2,1)S(1)} %constant_dynamic-update-slice_fusion.refs_1_), channel_id=1, source_target_pairs={{0,4},{2,6},{4,0},{6,2},{8,12},{10,14},{12,8},{14,10},{16,20},{18,... | collective-permute-start | bytes 1572872 | tf_op jit(solution)/shard_map/ppermute | solution.py:323
  44.7 4.3 %collective-permute-start.5 = (bf16[64,512]{1,0:T(8,128)(2,1)S(1)}, bf16[64,512]{1,0:T(8,128)(2,1)S(1)}, u32[]{:S(2)}, u32[]{:S(2)}) collective-permute-start(bf16[64,512]{1,0:T(8,128)(2,1)S(1)} %get-tuple-element.14), channel_id=1, source_target_pairs={{0,2},{2,0},{4,6},{6,4},{8,10},{10,8},{12,14},{14,12},{16,18},{18,... | collective-permute-start | bytes 196616 | tf_op jit(solution)/shard_map/ppermute | solution.py:323

commit v4 on v3

--- a/solution.py
+++ b/solution.py
@@ -389,10 +389,19 @@
         perturb_draws,
     )
     payload, *parts = lax.optimization_barrier((payload, *parts))
-    while bit > 1:
+    while bit > 4:
         parts, offsets = exchange(parts, offsets, bit)
         bit //= 2
+    if bit == 4:
+        held = jnp.concatenate(parts, axis=0)
+        parts = [held, across(held, 4), across(held, 2)]
     everyone = lax.all_to_all(payload, ("mem", "sp"), 0, 0, tiled=True)
+    if bit == 4:
+        everyone, passed = lax.optimization_barrier((everyone, parts[1]))
+        parts.append(across(passed, 2))
+        offsets = [offset ^ turn for turn in (0, 4, 2, 6) for offset in offsets]
+    elif bit == 2:
+        parts, offsets = exchange(parts, offsets, bit)
     if order <= LANES:
         solved = pl.pallas_call(
             lambda *refs: solve_kernel(norm_scale, slabs, offsets, *refs),

time: 49.9 us -> 45.5 us (0.912)
  blocking collectives: 13.2 us -> 0 us
  starting transfers between devices: 9.74 us -> 15 us
  waiting for transfers between devices: 12.6 us -> 16 us
    all_to_all x1 -> x0, blocking collectives: 13.2 us -> none  [body(): everyone = lax.all_to_all(payload, ('mem', 'sp'), 0, 0, tiled=True)]
    all_to_all x0 -> x1, waiting for transfers between devices: none -> 6.49 us  [body(): everyone = lax.all_to_all(payload, ('mem', 'sp'), 0, 0, tiled=True)]
    all_to_all x0 -> x1, starting transfers between devices: none -> 4.41 us  [body(): everyone = lax.all_to_all(payload, ('mem', 'sp'), 0, 0, tiled=True)]
    ppermute x5 -> x6, waiting for transfers between devices: 12.6 us -> 9.49 us  [across(): return lax.ppermute(value, 'mem', [(i, i ^ bit) for i in range(owners)])]
    ppermute x5 -> x6, starting transfers between devices: 9.22 us -> 10.1 us  [across(): return lax.ppermute(value, 'mem', [(i, i ^ bit) for i in range(owners)])]
  transfers between devices with their start and end apart: 6 -> 8, of which waited for: 3 -> 4; matrix products, arithmetic and copies ran while one was open for 0% -> 0% of each run, Pallas kernels for 21% -> 23%
where the time goes in v4:
time: 45.5 us; the launch traced here: 45.3 us
  waiting for transfers between devices  16 us (35%)
  starting transfers between devices  15 us (33%)
  Pallas kernels  11.7 us (26%)
  other arithmetic  1.17 us (3%)
  between operations  0.75 us (2%)
  local copies, waits for them, and re-layouts  0.69 us (2%)
    ppermute x6, starting transfers between devices, across(): return lax.ppermute(value, 'mem', [(i, i ^ bit) for i in range(owners)])  10.1 us
    ppermute x6, waiting for transfers between devices, across(): return lax.ppermute(value, 'mem', [(i, i ^ bit) for i in range(owners)])  9.49 us
    all_to_all x1, waiting for transfers between devices, body(): everyone = lax.all_to_all(payload, ('mem', 'sp'), 0, 0, tiled=True)  6.49 us
    pallas_call x1, Pallas kernels, body(): pl.pallas_call(conduct_kernel, out_shape=(jax.ShapeDtypeStruct((members,...  5.73 us
    pallas_call x1, Pallas kernels, body(): pl.pallas_call(lambda *refs: solve_kernel(norm_scale, slabs, offsets, *re...  4.79 us
    all_to_all x1, starting transfers between devices, body(): everyone = lax.all_to_all(payload, ('mem', 'sp'), 0, 0, tiled=True)  4.41 us
    concatenate x1, other arithmetic, body(): jnp.concatenate([field_flat, starting_warmth, thermal_supply], axis=0)  1.06 us
  transfers between devices with their start and end apart: 8, of which 4 were waited for; matrix products, arithmetic and copies ran while one was open for 0% of the time, Pallas kernels for 23%

profile of v4, /device:TPU:0, one launch (start us, length us, event | category | flops | bytes accessed | tf_op | source)
XLA Modules:
  0.0 45.3 jit_solution(13975387537403117875)
XLA Ops:
  0.6 1.1 %pad_maximum_fusion = f32[80,1024]{1,0:T(8,128)S(1)} fusion(f32[8,1024]{1,0:T(8,128)} %supply_hbm.1, f32[8,1024]{1,0:T(8,128)} %warmth_hbm.1, f32[64,1024]{1,0:T(8,128)} %bitcast.9), kind=kLoop, calls=%fused_computation | loop fusion | flops 163840 | bytes 655360 | tf_op jit(solution)/shard_map/concatenate | solution.py:341
  1.7 0.5 %collective-permute-start = (f32[80,1024]{1,0:T(8,128)S(1)}, f32[80,1024]{1,0:T(8,128)S(1)}, u32[]{:S(2)}, u32[]{:S(2)}) collective-permute-start(f32[80,1024]{1,0:T(8,128)S(1)} %pad_maximum_fusion), channel_id=1, source_target_pairs={{0,1},{1,0},{2,3},{3,2},{4,5},{5,4},{6,7},{7,6},{8,9},{9,8},{10,11... | collective-permute-start | bytes 983048 | tf_op jit(solution)/shard_map/ppermute | solution.py:343
  2.3 2.6 %collective-permute-start.1 = (bf16[64,512]{1,0:T(8,128)(2,1)S(1)}, bf16[64,512]{1,0:T(8,128)(2,1)S(1)}, u32[]{:S(2)}, u32[]{:S(2)}) collective-permute-start(bf16[64,512]{1,0:T(8,128)(2,1)S(1)} %get-tuple-element.21), channel_id=1, source_target_pairs={{0,2},{2,0},{4,6},{6,4},{8,10},{10,8},{12,14},{14,12},{16,18},{18,... | collective-permute-start | bytes 196616 | tf_op jit(solution)/shard_map/ppermute | solution.py:323
  4.8 2.7 %collective-permute-done.1 = bf16[64,512]{1,0:T(8,128)(2,1)S(1)} collective-permute-done((bf16[64,512]{1,0:T(8,128)(2,1)S(1)}, bf16[64,512]{1,0:T(8,128)(2,1)S(1)}, u32[]{:S(2)}, u32[]{:S(2)}) %collective-permute-start.1) | collective-permute-done | bytes 65568 | tf_op jit(solution)/shard_map/ppermute | solution.py:323
  7.6 2.9 %collective-permute-start.2 = (bf16[128,512]{1,0:T(8,128)(2,1)S(1)}, bf16[128,512]{1,0:T(8,128)(2,1)S(1)}, u32[]{:S(2)}, u32[]{:S(2)}) collective-permute-start(bf16[128,512]{1,0:T(8,128)(2,1)S(1)} %pad_maximum_fusion.1), channel_id=1, source_target_pairs={{0,16},{2,18},{4,20},{6,22},{8,24},{10,26},{12,28},{14,30},{16,0},... | collective-permute-start | bytes 393224 | tf_op jit(solution)/shard_map/ppermute | solution.py:323
  10.5 0.1 add_convert_fusion.flags_ref
  10.6 0.0 collective-permute-done.up_ref.down_ref
  10.6 0.6 %copy-done.3 = f32[8,64]{1,0:T(8,128)S(1)} copy-done((f32[8,64]{1,0:T(8,128)S(1)}, f32[8,64]{1,0:T(8,128)}, u32[]{:S(2)}) %copy-start.3) | copy-done | bytes 2072
  11.2 0.0 copy-done.4
  11.2 0.0 copy-done.5
  11.3 0.0 copy-done.6
  11.3 5.7 %conduct.1 = (f32[8,64]{1,0:T(8,128)}, f32[32,8,128]{2,1,0:T(8,128)}) custom-call(s32[2]{0:T(128)S(1)} %add_convert_fusion.flags_ref, s32[64]{0:T(128)S(1)} %copy-done.4, f32[64,1024]{1,0:T(8,128)S(1)} %bitcast.10, f32[80,1024]{1,0:T(8,128)S(1)} %collective-permute-done.up_ref.down_ref, f32[80,1024]{1,0:T(8,128)S(1)} %collective-permute-done.up_ref.down_ref, ...), custom_call_target="tpu_custom_call" | custom-call | flops 15728640 | bytes 786432 | tf_op jit(solution)/shard_map/conduct/pallas_call | solution.py:353
  17.0 0.0 collective-permute-done.2
  17.1 1.6 %collective-permute-start.3 = (bf16[256,512]{1,0:T(8,128)(2,1)S(1)}, bf16[256,512]{1,0:T(8,128)(2,1)S(1)}, u32[]{:S(2)}, u32[]{:S(2)}) collective-permute-start(bf16[256,512]{1,0:T(8,128)(2,1)S(1)} %constant_dynamic-update-slice_fusion.refs_1_), channel_id=1, source_target_pairs={{0,8},{2,10},{4,12},{6,14},{8,0},{10,2},{12,4},{14,6},{16,24},{18,... | collective-permute-start | bytes 786440 | tf_op jit(solution)/shard_map/ppermute | solution.py:323
  18.7 4.4 %all-to-all-start = ((f32[32,8,128]{2,1,0:T(8,128)}), f32[32,8,128]{2,1,0:T(8,128)S(1)}, u32[]{:S(2)}, u32[]{:S(2)}) async-start(f32[32,8,128]{2,1,0:T(8,128)} %get-tuple-element.12), calls=%async_computation | async-start | bytes 262144 | tf_op jit(solution)/shard_map/all_to_all | solution.py:398
  23.1 1.8 %collective-permute-start.4 = (bf16[256,512]{1,0:T(8,128)(2,1)S(1)}, bf16[256,512]{1,0:T(8,128)(2,1)S(1)}, u32[]{:S(2)}, u32[]{:S(2)}) collective-permute-start(bf16[256,512]{1,0:T(8,128)(2,1)S(1)} %constant_dynamic-update-slice_fusion.refs_1_), channel_id=1, source_target_pairs={{0,4},{2,6},{4,0},{6,2},{8,12},{10,14},{12,8},{14,10},{16,20},{18,... | collective-permute-start | bytes 786440 | tf_op jit(solution)/shard_map/ppermute | solution.py:323
  25.0 6.5 %all-to-all-done.refs_1_ = f32[32,8,128]{2,1,0:T(8,128)S(1)} async-done(((f32[32,8,128]{2,1,0:T(8,128)}), f32[32,8,128]{2,1,0:T(8,128)S(1)}, u32[]{:S(2)}, u32[]{:S(2)}) %all-to-all-start) | async-done | bytes 131104 | tf_op jit(solution)/shard_map/all_to_all | solution.py:398
  31.5 0.7 %collective-permute-start.5 = (bf16[256,512]{1,0:T(8,128)(2,1)S(1)}, bf16[256,512]{1,0:T(8,128)(2,1)S(1)}, u32[]{:S(2)}, u32[]{:S(2)}) collective-permute-start(bf16[256,512]{1,0:T(8,128)(2,1)S(1)} %collective-permute-done.3.refs_2_), channel_id=1, source_target_pairs={{0,4},{2,6},{4,0},{6,2},{8,12},{10,14},{12,8},{14,10},{16,20},{18,... | collective-permute-start | bytes 786440 | tf_op jit(solution)/shard_map/ppermute | solution.py:323
  32.1 4.8 %solve.1.refs_0_ = bf16[16,128]{1,0:T(8,128)(2,1)S(1)} custom-call(s32[1]{0:T(128)} %bitcast.2.refs_0_, f32[32,8,128]{2,1,0:T(8,128)S(1)} %all-to-all-done.refs_1_), custom_call_target="tpu_custom_call" | custom-call | flops 4194304 | bytes 131072 | tf_op jit(solution)/shard_map/solve/pallas_call | solution.py:406
  36.9 2.9 %collective-permute-done.5.refs_4_ = bf16[256,512]{1,0:T(8,128)(2,1)S(1)} collective-permute-done((bf16[256,512]{1,0:T(8,128)(2,1)S(1)}, bf16[256,512]{1,0:T(8,128)(2,1)S(1)}, u32[]{:S(2)}, u32[]{:S(2)}) %collective-permute-start.5) | collective-permute-done | bytes 262176 | tf_op jit(solution)/shard_map/ppermute | solution.py:323
  39.8 0.4 apply.1
  40.2 0.4 collective-permute-start.6
  40.6 3.9 %collective-permute-done.6.got_ref = bf16[64,512]{1,0:T(8,128)(2,1)S(1)} collective-permute-done((bf16[64,512]{1,0:T(8,128)(2,1)S(1)}, bf16[64,512]{1,0:T(8,128)(2,1)S(1)}, u32[]{:S(2)}, u32[]{:S(2)}) %collective-permute-start.6) | collective-permute-done | bytes 65568 | tf_op jit(solution)/shard_map/ppermute | solution.py:323
  44.5 0.7 %merge.1 = f32[64,1024]{1,0:T(8,128)} custom-call(s32[1]{0:T(128)} %bitcast.odd_ref, f32[64,1024]{1,0:T(8,128)S(1)} %bitcast.11, f32[64,512]{1,0:T(8,128)S(1)} %get-tuple-element.17.own_ref, bf16[64,512]{1,0:T(8,128)(2,1)S(1)} %collective-permute-done.6.got_ref), custom_call_target="tpu_custom_call" | custom-call | tf_op jit(solution)/shard_map/merge/pallas_call | solution.py:449
  (17 shorter events, 0.1 us)
Async XLA Ops:
  0.6 1.6 %copy-start = (f32[8,8,1024]{2,1,0:T(8,128)S(1)}, f32[8,8,1024]{2,1,0:T(8,128)}, u32[]{:S(2)}) copy-start(f32[8,8,1024]{2,1,0:T(8,128)} %param.7) | copy-start | bytes 786436
  1.7 8.9 %collective-permute-start = (f32[80,1024]{1,0:T(8,128)S(1)}, f32[80,1024]{1,0:T(8,128)S(1)}, u32[]{:S(2)}, u32[]{:S(2)}) collective-permute-start(f32[80,1024]{1,0:T(8,128)S(1)} %pad_maximum_fusion), channel_id=1, source_target_pairs={{0,1},{1,0},{2,3},{3,2},{4,5},{5,4},{6,7},{7,6},{8,9},{9,8},{10,11... | collective-permute-start | bytes 983048 | tf_op jit(solution)/shard_map/ppermute | solution.py:343
  2.3 5.3 %collective-permute-start.1 = (bf16[64,512]{1,0:T(8,128)(2,1)S(1)}, bf16[64,512]{1,0:T(8,128)(2,1)S(1)}, u32[]{:S(2)}, u32[]{:S(2)}) collective-permute-start(bf16[64,512]{1,0:T(8,128)(2,1)S(1)} %get-tuple-element.21), channel_id=1, source_target_pairs={{0,2},{2,0},{4,6},{6,4},{8,10},{10,8},{12,14},{14,12},{16,18},{18,... | collective-permute-start | bytes 196616 | tf_op jit(solution)/shard_map/ppermute | solution.py:323
  7.6 3.0 %copy-start.1 = (f32[8,1024]{1,0:T(8,128)S(1)}, f32[8,1024]{1,0:T(8,128)}, u32[]{:S(2)}) copy-start(f32[8,1024]{1,0:T(8,128)} %supply_hbm.1) | copy-start | bytes 98308
  7.6 3.0 %copy-start.2 = (f32[8,1024]{1,0:T(8,128)S(1)}, f32[8,1024]{1,0:T(8,128)}, u32[]{:S(2)}) copy-start(f32[8,1024]{1,0:T(8,128)} %warmth_hbm.1) | copy-start | bytes 98308
  7.6 9.4 %collective-permute-start.2 = (bf16[128,512]{1,0:T(8,128)(2,1)S(1)}, bf16[128,512]{1,0:T(8,128)(2,1)S(1)}, u32[]{:S(2)}, u32[]{:S(2)}) collective-permute-start(bf16[128,512]{1,0:T(8,128)(2,1)S(1)} %pad_maximum_fusion.1), channel_id=1, source_target_pairs={{0,16},{2,18},{4,20},{6,22},{8,24},{10,26},{12,28},{14,30},{16,0},... | collective-permute-start | bytes 393224 | tf_op jit(solution)/shard_map/ppermute | solution.py:323
  10.5 0.7 %copy-start.3 = (f32[8,64]{1,0:T(8,128)S(1)}, f32[8,64]{1,0:T(8,128)}, u32[]{:S(2)}) copy-start(f32[8,64]{1,0:T(8,128)} %draws_hbm.1) | copy-start | bytes 6148
  10.6 0.7 %copy-start.4 = (s32[64]{0:T(128)S(1)}, s32[64]{0:T(128)}, u32[]{:S(2)}) copy-start(s32[64]{0:T(128)} %columns_hbm.1) | copy-start | bytes 772
  10.6 0.7 %copy-start.5 = (f32[64]{0:T(128)S(1)}, f32[64]{0:T(128)}, u32[]{:S(2)}) copy-start(f32[64]{0:T(128)} %param.11) | copy-start | bytes 772
  10.6 0.7 %copy-start.6 = (f32[64]{0:T(128)S(1)}, f32[64]{0:T(128)}, u32[]{:S(2)}) copy-start(f32[64]{0:T(128)} %param.12) | copy-start | bytes 772
  17.1 14.4 %collective-permute-start.3 = (bf16[256,512]{1,0:T(8,128)(2,1)S(1)}, bf16[256,512]{1,0:T(8,128)(2,1)S(1)}, u32[]{:S(2)}, u32[]{:S(2)}) collective-permute-start(bf16[256,512]{1,0:T(8,128)(2,1)S(1)} %constant_dynamic-update-slice_fusion.refs_1_), channel_id=1, source_target_pairs={{0,8},{2,10},{4,12},{6,14},{8,0},{10,2},{12,4},{14,6},{16,24},{18,... | collective-permute-start | bytes 786440 | tf_op jit(solution)/shard_map/ppermute | solution.py:323
  18.7 12.7 %all-to-all-start = ((f32[32,8,128]{2,1,0:T(8,128)}), f32[32,8,128]{2,1,0:T(8,128)S(1)}, u32[]{:S(2)}, u32[]{:S(2)}) async-start(f32[32,8,128]{2,1,0:T(8,128)} %get-tuple-element.12), calls=%async_computation | async-start | bytes 262144 | tf_op jit(solution)/shard_map/all_to_all | solution.py:398
  23.1 13.8 %collective-permute-start.4 = (bf16[256,512]{1,0:T(8,128)(2,1)S(1)}, bf16[256,512]{1,0:T(8,128)(2,1)S(1)}, u32[]{:S(2)}, u32[]{:S(2)}) collective-permute-start(bf16[256,512]{1,0:T(8,128)(2,1)S(1)} %constant_dynamic-update-slice_fusion.refs_1_), channel_id=1, source_target_pairs={{0,4},{2,6},{4,0},{6,2},{8,12},{10,14},{12,8},{14,10},{16,20},{18,... | collective-permute-start | bytes 786440 | tf_op jit(solution)/shard_map/ppermute | solution.py:323
  31.5 8.3 %collective-permute-start.5 = (bf16[256,512]{1,0:T(8,128)(2,1)S(1)}, bf16[256,512]{1,0:T(8,128)(2,1)S(1)}, u32[]{:S(2)}, u32[]{:S(2)}) collective-permute-start(bf16[256,512]{1,0:T(8,128)(2,1)S(1)} %collective-permute-done.3.refs_2_), channel_id=1, source_target_pairs={{0,4},{2,6},{4,0},{6,2},{8,12},{10,14},{12,8},{14,10},{16,20},{18,... | collective-permute-start | bytes 786440 | tf_op jit(solution)/shard_map/ppermute | solution.py:323
  40.2 4.3 %collective-permute-start.6 = (bf16[64,512]{1,0:T(8,128)(2,1)S(1)}, bf16[64,512]{1,0:T(8,128)(2,1)S(1)}, u32[]{:S(2)}, u32[]{:S(2)}) collective-permute-start(bf16[64,512]{1,0:T(8,128)(2,1)S(1)} %get-tuple-element.18), channel_id=1, source_target_pairs={{0,2},{2,0},{4,6},{6,4},{8,10},{10,8},{12,14},{14,12},{16,18},{18,... | collective-permute-start | bytes 196616 | tf_op jit(solution)/shard_map/ppermute | solution.py:323

commit v5 on v3

--- a/solution.py
+++ b/solution.py
@@ -195,7 +195,7 @@
         payload_ref[device] = payload
 
 
-def solve_kernel(norm_scale, slabs, offsets, place_ref, payload_ref, solved_ref):
+def solve_kernel(norm_scale, slabs, offsets, turns, place_ref, payload_ref, solved_ref):
     members, probes = payload_ref.shape[1], payload_ref.shape[2] // 2
     order = len(offsets) * members
     mine = place_ref[0]
@@ -208,7 +208,9 @@
         normal = jnp.concatenate([block[:, :probes] for block in blocks], axis=0)
         center = jnp.sum(normal, axis=0, keepdims=True) * (1.0 / order)
         scaled = (center - normal) * norm_scale
-        misfit = jnp.concatenate([block[:, probes:] for block in blocks[:2]], axis=0)
+        misfit = jnp.concatenate(
+            [blocks[offsets.index(turn)][:, probes:] for turn in turns], axis=0
+        )
         one = lax.dot_general(
             scaled, scaled, dims, precision=lax.Precision.HIGHEST, preferred_element_type=jnp.float32
         )
@@ -225,7 +227,7 @@
         + jnp.where(lane_id == row_id + k * ROWS, damping, 0.0)
         for k in range(blocks)
     ]
-    tableau += [cross[k : k + ROWS, :] for k in range(0, 2 * members, ROWS)]
+    tableau += [cross[k : k + ROWS, :] for k in range(0, len(turns) * members, ROWS)]
 
     def lanes_of(value, at):
         return jnp.broadcast_to(value[:, at : at + 1], (ROWS, order))
@@ -258,7 +260,8 @@
 
 
 def apply_kernel(norm_scale, lines, solved_ref, *refs):
-    part_refs, own_ref, give_ref = refs[:-2], refs[-2], refs[-1]
+    outs = refs[len(refs) // 2 :]
+    part_refs = refs[: len(refs) // 2]
     solved = solved_ref[...]
     pair, order = solved.shape
     wide = order * lines
@@ -286,17 +289,19 @@
         change = part if change is None else change + part
         start += deep
     change = change * norm_scale
-    rows = own_ref.shape[0]
-    own_ref[...] = change[:rows]
-    give_ref[...] = change[rows:].astype(give_ref.dtype)
-
-
-def merge_kernel(odd_ref, field_ref, own_ref, got_ref, out_ref):
-    own, got = own_ref[...], got_ref[...].astype(jnp.float32)
-    half = own.shape[1]
-    even = odd_ref[0] == 0
-    out_ref[:, :half] = field_ref[:, :half] + jnp.where(even, own, got)
-    out_ref[:, half:] = field_ref[:, half:] + jnp.where(even, got, own)
+    rows = outs[0].shape[0]
+    for turn, ref in enumerate(outs):
+        ref[...] = change[turn * rows : (turn + 1) * rows].astype(ref.dtype)
+
+
+def merge_kernel(place_ref, field_ref, *refs):
+    pieces, out_ref = refs[:-1], refs[-1]
+    share = pieces[0].shape[1]
+    mine = jnp.bitwise_and(place_ref[0], len(pieces) - 1)
+    for turn, piece in enumerate(pieces):
+        start = pl.multiple_of(jnp.bitwise_xor(mine, turn) * share, LANES)
+        columns = pl.ds(start, share)
+        out_ref[:, columns] = field_ref[:, columns] + piece[...].astype(jnp.float32)
 
 
 def body(
@@ -316,27 +321,25 @@
     slab = lax.axis_index("sp")
 
     mine = lax.axis_index("mem").astype(jnp.int32)
-    odd = mine & 1
-    half = width // 2
+    turns = range(math.gcd(owners, 4))
+    share = width // len(turns)
 
     def across(value, bit):
         return lax.ppermute(value, "mem", [(i, i ^ bit) for i in range(owners)])
 
     field_flat = logarithmic_diffusivity.reshape(members * lines, width)
     field_round = field_flat.astype(jnp.bfloat16)
-    left, right = field_round[:, :half], field_round[:, half:]
-    held = jnp.where(odd == 0, left, right)
-    parts = [held, across(jnp.where(odd == 0, right, left), 1)]
-    offsets = [0, 1]
-    bit = owners // 2
+    parts, offsets = [field_round], [0]
+    bits = []
+    while len(turns) << len(bits) < owners:
+        bits.insert(0, len(turns) << len(bits))
 
     def exchange(parts, offsets, bit):
         held = jnp.concatenate(parts, axis=0)
         return [held, across(held, bit)], offsets + [offset ^ bit for offset in offsets]
 
-    if bit > 1:
+    for bit in bits[:1]:
         parts, offsets = exchange(parts, offsets, bit)
-        bit //= 2
 
     edges = jnp.concatenate([field_flat, starting_warmth, thermal_supply], axis=0)
     if slabs == 2:
@@ -389,14 +392,21 @@
         perturb_draws,
     )
     payload, *parts = lax.optimization_barrier((payload, *parts))
-    while bit > 1:
+    for bit in bits[1:]:
         parts, offsets = exchange(parts, offsets, bit)
-        bit //= 2
     everyone = lax.all_to_all(payload, ("mem", "sp"), 0, 0, tiled=True)
+    everyone, *parts = lax.optimization_barrier((everyone, *parts))
+    held = jnp.concatenate(parts, axis=0)
+    parts = []
+    for turn in turns:
+        columns = ((mine ^ turn) & (len(turns) - 1)) * share
+        piece = lax.dynamic_slice_in_dim(held, columns, share, 1)
+        parts.append(across(piece, turn) if turn else piece)
+    offsets = [offset ^ turn for turn in turns for offset in offsets]
     if order <= LANES:
         solved = pl.pallas_call(
-            lambda *refs: solve_kernel(norm_scale, slabs, offsets, *refs),
-            out_shape=jax.ShapeDtypeStruct((2 * members, order), jnp.bfloat16),
+            lambda *refs: solve_kernel(norm_scale, slabs, offsets, turns, *refs),
+            out_shape=jax.ShapeDtypeStruct((len(turns) * members, order), jnp.bfloat16),
             in_specs=[smem, vmem],
             out_specs=vmem,
             compiler_params=pltpu.CompilerParams(vmem_limit_bytes=16 * 1024 * 1024),
@@ -411,7 +421,9 @@
         owner = mine ^ jnp.array(offsets, jnp.int32)
         split = everyone.reshape(owners, slabs, members, 2, probes)[owner]
         split = split.transpose(3, 0, 2, 1, 4).reshape(2, order, slabs * probes)
-        normal, misfit = split[0], split[1, : 2 * members]
+        normal = split[0]
+        misfit = split[1].reshape(owners, members, -1)
+        misfit = jnp.concatenate([misfit[offsets.index(turn)] for turn in turns], axis=0)
         scaled = (jnp.mean(normal, axis=0, keepdims=True) - normal) * norm_scale
         gram_matrix = jnp.dot(
             scaled, scaled.T, precision=lax.Precision.HIGHEST, preferred_element_type=jnp.float32
@@ -420,31 +432,32 @@
             scaled, misfit.T, precision=lax.Precision.HIGHEST, preferred_element_type=jnp.float32
         )
         solved = eliminate(gram_matrix, cross_term).T.astype(jnp.bfloat16)
-    own, give = pl.pallas_call(
+    rows = members * lines
+    pieces = pl.pallas_call(
         lambda *refs: apply_kernel(norm_scale, lines, *refs),
-        out_shape=(
-            jax.ShapeDtypeStruct((members * lines, half), jnp.float32),
-            jax.ShapeDtypeStruct((members * lines, half), jnp.bfloat16),
-        ),
+        out_shape=[
+            jax.ShapeDtypeStruct((rows, share), jnp.bfloat16 if turn else jnp.float32)
+            for turn in turns
+        ],
         in_specs=[vmem] * (1 + len(parts)),
-        out_specs=(vmem, vmem),
+        out_specs=[vmem] * len(turns),
         compiler_params=pltpu.CompilerParams(vmem_limit_bytes=40 * 1024 * 1024),
         cost_estimate=pl.CostEstimate(
-            flops=4 * members * lines * order * lines * half,
-            bytes_accessed=2 * order * lines * half,
+            flops=2 * rows * order * lines * width,
+            bytes_accessed=2 * order * lines * share,
             transcendentals=0,
         ),
         name="apply",
     )(solved, *parts)
-    got = across(give, 1)
+    pieces = [across(piece, turn) if turn else piece for turn, piece in zip(turns, pieces)]
     revised = pl.pallas_call(
         merge_kernel,
-        out_shape=jax.ShapeDtypeStruct((members * lines, width), jnp.float32),
-        in_specs=[smem] + [vmem] * 3,
+        out_shape=jax.ShapeDtypeStruct((rows, width), jnp.float32),
+        in_specs=[smem] + [vmem] * (1 + len(turns)),
         out_specs=vmem,
         compiler_params=pltpu.CompilerParams(vmem_limit_bytes=8 * 1024 * 1024),
         name="merge",
-    )(odd[None], field_flat, own, got)
+    )(mine[None], field_flat, *pieces)
     return (revised.reshape(logarithmic_diffusivity.shape), predicted)
 
 

time: 49.9 us -> 44.5 us (0.89)
  blocking collectives: 13.2 us -> 0 us
  starting transfers between devices: 9.74 us -> 17.7 us
    all_to_all x1 -> x0, blocking collectives: 13.2 us -> none  [body(): everyone = lax.all_to_all(payload, ('mem', 'sp'), 0, 0, tiled=True)]
    ppermute x5 -> x8, waiting for transfers between devices: 12.6 us -> 4.33 us  [across(): return lax.ppermute(value, 'mem', [(i, i ^ bit) for i in range(owners)])]
    all_to_all x0 -> x1, waiting for transfers between devices: none -> 8.22 us  [body(): everyone = lax.all_to_all(payload, ('mem', 'sp'), 0, 0, tiled=True)]
    all_to_all x0 -> x1, starting transfers between devices: none -> 5.2 us  [body(): everyone = lax.all_to_all(payload, ('mem', 'sp'), 0, 0, tiled=True)]
    ppermute x5 -> x8, starting transfers between devices: 9.22 us -> 12 us  [across(): return lax.ppermute(value, 'mem', [(i, i ^ bit) for i in range(owners)])]
  transfers between devices with their start and end apart: 6 -> 10, of which waited for: 3 -> 6; matrix products, arithmetic and copies ran while one was open for 0% -> 0% of each run, Pallas kernels for 21% -> 23%
where the time goes in v5:
time: 44.5 us; the launch traced here: 44.3 us
  starting transfers between devices  17.7 us (40%)
  waiting for transfers between devices  12.6 us (28%)
  Pallas kernels  11.3 us (25%)
  other arithmetic  1.15 us (3%)
  local copies, waits for them, and re-layouts  0.82 us (2%)
  between operations  0.77 us (2%)
    ppermute x8, starting transfers between devices, across(): return lax.ppermute(value, 'mem', [(i, i ^ bit) for i in range(owners)])  12 us
    all_to_all x1, waiting for transfers between devices, body(): everyone = lax.all_to_all(payload, ('mem', 'sp'), 0, 0, tiled=True)  8.22 us
    pallas_call x1, Pallas kernels, body(): pl.pallas_call(conduct_kernel, out_shape=(jax.ShapeDtypeStruct((members,...  5.73 us
    all_to_all x1, starting transfers between devices, body(): everyone = lax.all_to_all(payload, ('mem', 'sp'), 0, 0, tiled=True)  5.2 us
    pallas_call x1, Pallas kernels, body(): pl.pallas_call(lambda *refs: solve_kernel(norm_scale, slabs, offsets, tur...  4.44 us
    ppermute x8, waiting for transfers between devices, across(): return lax.ppermute(value, 'mem', [(i, i ^ bit) for i in range(owners)])  4.33 us
    concatenate x1, other arithmetic, body(): jnp.concatenate([field_flat, starting_warmth, thermal_supply], axis=0)  1.06 us
  transfers between devices with their start and end apart: 10, of which 6 were waited for; matrix products, arithmetic and copies ran while one was open for 0% of the time, Pallas kernels for 23%

profile of v5, /device:TPU:0, one launch (start us, length us, event | category | flops | bytes accessed | tf_op | source)
XLA Modules:
  0.0 44.3 jit_solution(17994151786241554898)
XLA Ops:
  0.6 1.1 %pad_maximum_fusion = f32[80,1024]{1,0:T(8,128)S(1)} fusion(f32[8,1024]{1,0:T(8,128)} %supply_hbm.1, f32[8,1024]{1,0:T(8,128)} %warmth_hbm.1, f32[64,1024]{1,0:T(8,128)} %bitcast.8), kind=kLoop, calls=%fused_computation | loop fusion | flops 163840 | bytes 655360 | tf_op jit(solution)/shard_map/concatenate | solution.py:344
  1.7 0.5 %collective-permute-start = (f32[80,1024]{1,0:T(8,128)S(1)}, f32[80,1024]{1,0:T(8,128)S(1)}, u32[]{:S(2)}, u32[]{:S(2)}) collective-permute-start(f32[80,1024]{1,0:T(8,128)S(1)} %pad_maximum_fusion), channel_id=1, source_target_pairs={{0,1},{1,0},{2,3},{3,2},{4,5},{5,4},{6,7},{7,6},{8,9},{9,8},{10,11... | collective-permute-start | bytes 983048 | tf_op jit(solution)/shard_map/ppermute | solution.py:346
  2.3 3.7 %collective-permute-start.1 = (bf16[64,1024]{1,0:T(8,128)(2,1)S(1)}, bf16[64,1024]{1,0:T(8,128)(2,1)S(1)}, u32[]{:S(2)}, u32[]{:S(2)}) collective-permute-start(bf16[64,1024]{1,0:T(8,128)(2,1)S(1)} %bitcast_convert_fusion), channel_id=1, source_target_pairs={{0,16},{2,18},{4,20},{6,22},{8,24},{10,26},{12,28},{14,30},{16,0},... | collective-permute-start | bytes 393224 | tf_op jit(solution)/shard_map/ppermute | solution.py:328
  5.9 0.1 add_convert_fusion.flags_ref
  6.0 0.6 %copy-done.3 = f32[8,64]{1,0:T(8,128)S(1)} copy-done((f32[8,64]{1,0:T(8,128)S(1)}, f32[8,64]{1,0:T(8,128)}, u32[]{:S(2)}) %copy-start.3) | copy-done | bytes 2072
  6.7 5.7 %conduct.1 = (f32[8,64]{1,0:T(8,128)}, f32[32,8,128]{2,1,0:T(8,128)}) custom-call(s32[2]{0:T(128)S(1)} %add_convert_fusion.flags_ref, s32[64]{0:T(128)S(1)} %copy-done.4, f32[64,1024]{1,0:T(8,128)S(1)} %bitcast.9, f32[80,1024]{1,0:T(8,128)S(1)} %collective-permute-done.up_ref.down_ref, f32[80,1024]{1,0:T(8,128)S(1)} %collective-permute-done.up_ref.down_ref, ...), custom_call_target="tpu_custom_call" | custom-call | flops 15728640 | bytes 786432 | tf_op jit(solution)/shard_map/conduct/pallas_call | solution.py:356
  12.4 0.4 %collective-permute-done.1 = bf16[64,1024]{1,0:T(8,128)(2,1)S(1)} collective-permute-done((bf16[64,1024]{1,0:T(8,128)(2,1)S(1)}, bf16[64,1024]{1,0:T(8,128)(2,1)S(1)}, u32[]{:S(2)}, u32[]{:S(2)}) %collective-permute-start.1) | collective-permute-done | bytes 131104 | tf_op jit(solution)/shard_map/ppermute | solution.py:328
  12.9 1.2 %collective-permute-start.2 = (bf16[128,1024]{1,0:T(8,128)(2,1)S(1)}, bf16[128,1024]{1,0:T(8,128)(2,1)S(1)}, u32[]{:S(2)}, u32[]{:S(2)}) collective-permute-start(bf16[128,1024]{1,0:T(8,128)(2,1)S(1)} %constant_dynamic-update-slice_fusion), channel_id=1, source_target_pairs={{0,8},{2,10},{4,12},{6,14},{8,0},{10,2},{12,4},{14,6},{16,24},{18,... | collective-permute-start | bytes 786440 | tf_op jit(solution)/shard_map/ppermute | solution.py:328
  14.1 5.2 %all-to-all-start = ((f32[32,8,128]{2,1,0:T(8,128)}), f32[32,8,128]{2,1,0:T(8,128)S(1)}, u32[]{:S(2)}, u32[]{:S(2)}) async-start(f32[32,8,128]{2,1,0:T(8,128)} %get-tuple-element.15), calls=%async_computation | async-start | bytes 262144 | tf_op jit(solution)/shard_map/all_to_all | solution.py:397
  19.4 8.2 %all-to-all-done.refs_1_ = f32[32,8,128]{2,1,0:T(8,128)S(1)} async-done(((f32[32,8,128]{2,1,0:T(8,128)}), f32[32,8,128]{2,1,0:T(8,128)S(1)}, u32[]{:S(2)}, u32[]{:S(2)}) %all-to-all-start) | async-done | bytes 131104 | tf_op jit(solution)/shard_map/all_to_all | solution.py:397
  27.6 0.1 constant_dynamic-slice_fusion
  27.7 0.5 %collective-permute-start.3 = (bf16[256,256]{1,0:T(8,128)(2,1)S(1)}, bf16[256,256]{1,0:T(8,128)(2,1)S(1)}, u32[]{:S(2)}, u32[]{:S(2)}) collective-permute-start(bf16[256,256]{1,0:T(8,128)(2,1)S(1)} %get-tuple-element.28), channel_id=1, source_target_pairs={{0,2},{2,0},{4,6},{6,4},{8,10},{10,8},{12,14},{14,12},{16,18},{18,... | collective-permute-start | bytes 393224 | tf_op jit(solution)/shard_map/ppermute | solution.py:328
  28.2 1.0 %collective-permute-start.4 = (bf16[256,256]{1,0:T(8,128)(2,1)S(1)}, bf16[256,256]{1,0:T(8,128)(2,1)S(1)}, u32[]{:S(2)}, u32[]{:S(2)}) collective-permute-start(bf16[256,256]{1,0:T(8,128)(2,1)S(1)} %get-tuple-element.27), channel_id=1, source_target_pairs={{0,4},{2,6},{4,0},{6,2},{8,12},{10,14},{12,8},{14,10},{16,20},{18,... | collective-permute-start | bytes 393224 | tf_op jit(solution)/shard_map/ppermute | solution.py:328
  29.2 2.1 %collective-permute-start.5 = (bf16[256,256]{1,0:T(8,128)(2,1)S(1)}, bf16[256,256]{1,0:T(8,128)(2,1)S(1)}, u32[]{:S(2)}, u32[]{:S(2)}) collective-permute-start(bf16[256,256]{1,0:T(8,128)(2,1)S(1)} %get-tuple-element.26), channel_id=1, source_target_pairs={{0,6},{2,4},{4,2},{6,0},{8,14},{10,12},{12,10},{14,8},{16,22},{18,... | collective-permute-start | bytes 393224 | tf_op jit(solution)/shard_map/ppermute | solution.py:328
  31.3 4.4 %solve.1.refs_0_ = bf16[32,128]{1,0:T(8,128)(2,1)S(1)} custom-call(s32[1]{0:T(128)} %bitcast.refs_0_.place_ref, f32[32,8,128]{2,1,0:T(8,128)S(1)} %all-to-all-done.refs_1_), custom_call_target="tpu_custom_call" | custom-call | flops 4194304 | bytes 131072 | tf_op jit(solution)/shard_map/solve/pallas_call | solution.py:407
  35.7 0.6 %collective-permute-done.4.refs_3_ = bf16[256,256]{1,0:T(8,128)(2,1)S(1)} collective-permute-done((bf16[256,256]{1,0:T(8,128)(2,1)S(1)}, bf16[256,256]{1,0:T(8,128)(2,1)S(1)}, u32[]{:S(2)}, u32[]{:S(2)}) %collective-permute-start.4) | collective-permute-done | bytes 131104 | tf_op jit(solution)/shard_map/ppermute | solution.py:328
  36.3 0.4 apply.1
  36.7 1.7 %collective-permute-start.6 = (bf16[64,256]{1,0:T(8,128)(2,1)S(1)}, bf16[64,256]{1,0:T(8,128)(2,1)S(1)}, u32[]{:S(2)}, u32[]{:S(2)}) collective-permute-start(bf16[64,256]{1,0:T(8,128)(2,1)S(1)} %get-tuple-element.22), channel_id=1, source_target_pairs={{0,2},{2,0},{4,6},{6,4},{8,10},{10,8},{12,14},{14,12},{16,18},{18,... | collective-permute-start | bytes 98312 | tf_op jit(solution)/shard_map/ppermute | solution.py:328
  38.4 0.3 collective-permute-start.7
  38.8 1.5 %collective-permute-start.8 = (bf16[64,256]{1,0:T(8,128)(2,1)S(1)}, bf16[64,256]{1,0:T(8,128)(2,1)S(1)}, u32[]{:S(2)}, u32[]{:S(2)}) collective-permute-start(bf16[64,256]{1,0:T(8,128)(2,1)S(1)} %get-tuple-element.24), channel_id=1, source_target_pairs={{0,6},{2,4},{4,2},{6,0},{8,14},{10,12},{12,10},{14,8},{16,22},{18,... | collective-permute-start | bytes 98312 | tf_op jit(solution)/shard_map/ppermute | solution.py:328
  40.3 0.4 collective-permute-done.6.refs_1_
  40.7 1.7 %collective-permute-done.7.refs_2_ = bf16[64,256]{1,0:T(8,128)(2,1)S(1)} collective-permute-done((bf16[64,256]{1,0:T(8,128)(2,1)S(1)}, bf16[64,256]{1,0:T(8,128)(2,1)S(1)}, u32[]{:S(2)}, u32[]{:S(2)}) %collective-permute-start.7) | collective-permute-done | bytes 32800 | tf_op jit(solution)/shard_map/ppermute | solution.py:328
  42.3 1.2 %collective-permute-done.8.refs_3_ = bf16[64,256]{1,0:T(8,128)(2,1)S(1)} collective-permute-done((bf16[64,256]{1,0:T(8,128)(2,1)S(1)}, bf16[64,256]{1,0:T(8,128)(2,1)S(1)}, u32[]{:S(2)}, u32[]{:S(2)}) %collective-permute-start.8) | collective-permute-done | bytes 32800 | tf_op jit(solution)/shard_map/ppermute | solution.py:328
  43.6 0.7 %merge.1 = f32[64,1024]{1,0:T(8,128)} custom-call(s32[1]{0:T(128)} %bitcast.refs_0_.place_ref, f32[64,1024]{1,0:T(8,128)S(1)} %bitcast.10, f32[64,256]{1,0:T(8,128)S(1)} %get-tuple-element.21.refs_0_, bf16[64,256]{1,0:T(8,128)(2,1)S(1)} %collective-permute-done.6.refs_1_, bf16[64,256]{1,0:T(8,128)(2,1)S(1)} %collective-permute-done.7.refs_2_, ...), custom_call_target="tpu_custom_call" | custom-call | tf_op jit(solution)/shard_map/merge/pallas_call | solution.py:453
  (22 shorter events, 0.2 us)
Async XLA Ops:
  0.6 1.6 %copy-start = (f32[8,8,1024]{2,1,0:T(8,128)S(1)}, f32[8,8,1024]{2,1,0:T(8,128)}, u32[]{:S(2)}) copy-start(f32[8,8,1024]{2,1,0:T(8,128)} %param.7) | copy-start | bytes 786436
  1.7 4.3 %copy-start.1 = (f32[8,1024]{1,0:T(8,128)S(1)}, f32[8,1024]{1,0:T(8,128)}, u32[]{:S(2)}) copy-start(f32[8,1024]{1,0:T(8,128)} %supply_hbm.1) | copy-start | bytes 98308
  1.7 4.3 %copy-start.2 = (f32[8,1024]{1,0:T(8,128)S(1)}, f32[8,1024]{1,0:T(8,128)}, u32[]{:S(2)}) copy-start(f32[8,1024]{1,0:T(8,128)} %warmth_hbm.1) | copy-start | bytes 98308
  1.7 4.3 %collective-permute-start = (f32[80,1024]{1,0:T(8,128)S(1)}, f32[80,1024]{1,0:T(8,128)S(1)}, u32[]{:S(2)}, u32[]{:S(2)}) collective-permute-start(f32[80,1024]{1,0:T(8,128)S(1)} %pad_maximum_fusion), channel_id=1, source_target_pairs={{0,1},{1,0},{2,3},{3,2},{4,5},{5,4},{6,7},{7,6},{8,9},{9,8},{10,11... | collective-permute-start | bytes 983048 | tf_op jit(solution)/shard_map/ppermute | solution.py:346
  2.3 10.6 %collective-permute-start.1 = (bf16[64,1024]{1,0:T(8,128)(2,1)S(1)}, bf16[64,1024]{1,0:T(8,128)(2,1)S(1)}, u32[]{:S(2)}, u32[]{:S(2)}) collective-permute-start(bf16[64,1024]{1,0:T(8,128)(2,1)S(1)} %bitcast_convert_fusion), channel_id=1, source_target_pairs={{0,16},{2,18},{4,20},{6,22},{8,24},{10,26},{12,28},{14,30},{16,0},... | collective-permute-start | bytes 393224 | tf_op jit(solution)/shard_map/ppermute | solution.py:328
  5.9 0.7 %copy-start.3 = (f32[8,64]{1,0:T(8,128)S(1)}, f32[8,64]{1,0:T(8,128)}, u32[]{:S(2)}) copy-start(f32[8,64]{1,0:T(8,128)} %draws_hbm.1) | copy-start | bytes 6148
  6.0 0.7 %copy-start.4 = (s32[64]{0:T(128)S(1)}, s32[64]{0:T(128)}, u32[]{:S(2)}) copy-start(s32[64]{0:T(128)} %columns_hbm.1) | copy-start | bytes 772
  6.0 0.7 %copy-start.5 = (f32[64]{0:T(128)S(1)}, f32[64]{0:T(128)}, u32[]{:S(2)}) copy-start(f32[64]{0:T(128)} %param.11) | copy-start | bytes 772
  6.0 0.7 %copy-start.6 = (f32[64]{0:T(128)S(1)}, f32[64]{0:T(128)}, u32[]{:S(2)}) copy-start(f32[64]{0:T(128)} %param.12) | copy-start | bytes 772
  12.9 14.7 %collective-permute-start.2 = (bf16[128,1024]{1,0:T(8,128)(2,1)S(1)}, bf16[128,1024]{1,0:T(8,128)(2,1)S(1)}, u32[]{:S(2)}, u32[]{:S(2)}) collective-permute-start(bf16[128,1024]{1,0:T(8,128)(2,1)S(1)} %constant_dynamic-update-slice_fusion), channel_id=1, source_target_pairs={{0,8},{2,10},{4,12},{6,14},{8,0},{10,2},{12,4},{14,6},{16,24},{18,... | collective-permute-start | bytes 786440 | tf_op jit(solution)/shard_map/ppermute | solution.py:328
  14.1 13.4 %all-to-all-start = ((f32[32,8,128]{2,1,0:T(8,128)}), f32[32,8,128]{2,1,0:T(8,128)S(1)}, u32[]{:S(2)}, u32[]{:S(2)}) async-start(f32[32,8,128]{2,1,0:T(8,128)} %get-tuple-element.15), calls=%async_computation | async-start | bytes 262144 | tf_op jit(solution)/shard_map/all_to_all | solution.py:397
  27.7 8.0 %collective-permute-start.3 = (bf16[256,256]{1,0:T(8,128)(2,1)S(1)}, bf16[256,256]{1,0:T(8,128)(2,1)S(1)}, u32[]{:S(2)}, u32[]{:S(2)}) collective-permute-start(bf16[256,256]{1,0:T(8,128)(2,1)S(1)} %get-tuple-element.28), channel_id=1, source_target_pairs={{0,2},{2,0},{4,6},{6,4},{8,10},{10,8},{12,14},{14,12},{16,18},{18,... | collective-permute-start | bytes 393224 | tf_op jit(solution)/shard_map/ppermute | solution.py:328
  28.2 8.1 %collective-permute-start.4 = (bf16[256,256]{1,0:T(8,128)(2,1)S(1)}, bf16[256,256]{1,0:T(8,128)(2,1)S(1)}, u32[]{:S(2)}, u32[]{:S(2)}) collective-permute-start(bf16[256,256]{1,0:T(8,128)(2,1)S(1)} %get-tuple-element.27), channel_id=1, source_target_pairs={{0,4},{2,6},{4,0},{6,2},{8,12},{10,14},{12,8},{14,10},{16,20},{18,... | collective-permute-start | bytes 393224 | tf_op jit(solution)/shard_map/ppermute | solution.py:328
  29.2 7.1 %collective-permute-start.5 = (bf16[256,256]{1,0:T(8,128)(2,1)S(1)}, bf16[256,256]{1,0:T(8,128)(2,1)S(1)}, u32[]{:S(2)}, u32[]{:S(2)}) collective-permute-start(bf16[256,256]{1,0:T(8,128)(2,1)S(1)} %get-tuple-element.26), channel_id=1, source_target_pairs={{0,6},{2,4},{4,2},{6,0},{8,14},{10,12},{12,10},{14,8},{16,22},{18,... | collective-permute-start | bytes 393224 | tf_op jit(solution)/shard_map/ppermute | solution.py:328
  36.7 4.0 %collective-permute-start.6 = (bf16[64,256]{1,0:T(8,128)(2,1)S(1)}, bf16[64,256]{1,0:T(8,128)(2,1)S(1)}, u32[]{:S(2)}, u32[]{:S(2)}) collective-permute-start(bf16[64,256]{1,0:T(8,128)(2,1)S(1)} %get-tuple-element.22), channel_id=1, source_target_pairs={{0,2},{2,0},{4,6},{6,4},{8,10},{10,8},{12,14},{14,12},{16,18},{18,... | collective-permute-start | bytes 98312 | tf_op jit(solution)/shard_map/ppermute | solution.py:328
  38.4 3.9 %collective-permute-start.7 = (bf16[64,256]{1,0:T(8,128)(2,1)S(1)}, bf16[64,256]{1,0:T(8,128)(2,1)S(1)}, u32[]{:S(2)}, u32[]{:S(2)}) collective-permute-start(bf16[64,256]{1,0:T(8,128)(2,1)S(1)} %get-tuple-element.23), channel_id=1, source_target_pairs={{0,4},{2,6},{4,0},{6,2},{8,12},{10,14},{12,8},{14,10},{16,20},{18,... | collective-permute-start | bytes 98312 | tf_op jit(solution)/shard_map/ppermute | solution.py:328
  38.8 4.8 %collective-permute-start.8 = (bf16[64,256]{1,0:T(8,128)(2,1)S(1)}, bf16[64,256]{1,0:T(8,128)(2,1)S(1)}, u32[]{:S(2)}, u32[]{:S(2)}) collective-permute-start(bf16[64,256]{1,0:T(8,128)(2,1)S(1)} %get-tuple-element.24), channel_id=1, source_target_pairs={{0,6},{2,4},{4,2},{6,0},{8,14},{10,12},{12,10},{14,8},{16,22},{18,... | collective-permute-start | bytes 98312 | tf_op jit(solution)/shard_map/ppermute | solution.py:328

commit v6 on v5

--- a/solution.py
+++ b/solution.py
@@ -59,8 +59,8 @@
     field_ref,
     up_ref,
     down_ref,
-    warmth_hbm,
-    supply_hbm,
+    start_ref,
+    source_ref,
     recorded_hbm,
     sigma_hbm,
     draws_hbm,
@@ -70,19 +70,16 @@
     half_exp,
     supply,
     columns_ref,
-    small_ref,
     recorded_ref,
     sigma_ref,
     draws_ref,
     sems,
 ):
-    lines = warmth_hbm.shape[0]
+    lines = start_ref.shape[0]
     copies = [
         pltpu.make_async_copy(source, target, sems.at[k])
         for k, (source, target) in enumerate(
             (
-                (warmth_hbm, small_ref.at[pl.ds(0, lines)]),
-                (supply_hbm, small_ref.at[pl.ds(lines, lines)]),
                 (columns_hbm, columns_ref),
                 (recorded_hbm, recorded_ref),
                 (sigma_hbm, sigma_ref),
@@ -92,7 +89,7 @@
     ]
     for copy in copies:
         copy.start()
-    members, width = predicted_ref.shape[0], small_ref.shape[1]
+    members, width = predicted_ref.shape[0], start_ref.shape[1]
     tiles = width // LANES
     window = lines + 2 * STEPS
     lane = lax.broadcasted_iota(jnp.int32, (members, LANES), 1)
@@ -104,25 +101,29 @@
         (STEPS, field_ref, 0, lines, None),
         (STEPS + lines, down_ref, 0, STEPS, below),
     )
+    def by_rows(ref):
+        return jnp.swapaxes(ref[0 : members * lines, :].reshape(members, lines, width), 0, 1)
+
+    turned = {id(ref): by_rows(ref) for ref in (field_ref, up_ref, down_ref)}
     for row, ref, line, count, inside in sides:
-        coefficient = jnp.swapaxes(
-            ref[0 : members * lines, :].reshape(members, lines, width), 0, 1
-        )
+        coefficient = turned[id(ref)]
         for step in range(count):
             part = coefficient[line + step]
             if inside is not None:
                 part = jnp.where(inside, part, 0.0)
             half_exp[row + step] = 0.5 * jnp.exp(part)
-    copies[0].wait()
-    copies[1].wait()
     for row, ref, line, count, inside in sides:
-        small, base = (small_ref, 0) if inside is None else (ref, members * lines)
         for step in range(count):
-            heat = small[pl.ds(base + line + step, 1), :]
-            if inside is not None:
-                heat = jnp.where(inside, heat, 0.0)
+            if inside is None:
+                heat = start_ref[pl.ds(line + step, 1), :]
+            else:
+                heat = jnp.where(inside, ref[pl.ds(members * lines + line + step, 1), :], 0.0)
             warmth[row + step] = jnp.broadcast_to(heat, (members, width))
-        supply[pl.ds(row, count), :] = small[pl.ds(base + lines + line, count), :]
+        if inside is None:
+            supply[pl.ds(row, count), :] = source_ref[...]
+        else:
+            base = (members + 1) * lines + line
+            supply[pl.ds(row, count), :] = ref[pl.ds(base, count), :]
 
     def cut(value):
         return [value[:, k * LANES : (k + 1) * LANES] for k in range(tiles)]
@@ -173,7 +174,7 @@
 
         lax.fori_loop(low, high, one_row, (t_here, c_here, flow_up), unroll=True)
 
-    for copy in copies[2:]:
+    for copy in copies:
         copy.wait()
     probes = predicted_ref.shape[1]
     lane_probe = lax.broadcasted_iota(jnp.int32, (members, LANES), 1)
@@ -261,7 +262,7 @@
 
 def apply_kernel(norm_scale, lines, solved_ref, *refs):
     outs = refs[len(refs) // 2 :]
-    part_refs = refs[: len(refs) // 2]
+    part_refs = refs[: len(refs) // 2][::-1]
     solved = solved_ref[...]
     pair, order = solved.shape
     wide = order * lines
@@ -295,7 +296,7 @@
 
 
 def merge_kernel(place_ref, field_ref, *refs):
-    pieces, out_ref = refs[:-1], refs[-1]
+    pieces, out_ref = refs[:-1][::-1], refs[-1]
     share = pieces[0].shape[1]
     mine = jnp.bitwise_and(place_ref[0], len(pieces) - 1)
     for turn, piece in enumerate(pieces):
@@ -353,24 +354,31 @@
     anywhere = pl.BlockSpec(memory_space=pl.ANY)
     window = lines + 2 * STEPS
     devices = owners * slabs
+    beside = [up] if slabs == 2 else [up, down]
+
+    def kernel(flags_ref, columns_hbm, field_ref, *refs):
+        neighbours, rest = refs[: len(beside)], refs[len(beside) :]
+        conduct_kernel(
+            flags_ref, columns_hbm, field_ref, neighbours[0], neighbours[-1], *rest
+        )
+
     predicted, payload = pl.pallas_call(
-        conduct_kernel,
+        kernel,
         out_shape=(
             jax.ShapeDtypeStruct((members, probes), jnp.float32),
             jax.ShapeDtypeStruct((devices, members, 2 * probes), jnp.float32),
         ),
-        in_specs=[smem, anywhere] + [vmem] * 3 + [anywhere] * 5,
+        in_specs=[smem, anywhere] + [vmem] * (3 + len(beside)) + [anywhere] * 3,
         out_specs=(vmem, vmem),
         scratch_shapes=[
             pltpu.VMEM((window, members, width), jnp.float32),
             pltpu.VMEM((window, members, width), jnp.float32),
             pltpu.VMEM((window, width), jnp.float32),
             pltpu.SMEM((probes,), jnp.int32),
-            pltpu.VMEM((2 * lines, width), jnp.float32),
             pltpu.VMEM((1, probes), jnp.float32),
             pltpu.VMEM((1, probes), jnp.float32),
             pltpu.VMEM((members, probes), jnp.float32),
-            pltpu.SemaphoreType.DMA((6,)),
+            pltpu.SemaphoreType.DMA((4,)),
         ],
         compiler_params=pltpu.CompilerParams(vmem_limit_bytes=24 * 1024 * 1024),
         cost_estimate=pl.CostEstimate(
@@ -383,8 +391,7 @@
         flags,
         probe_positions,
         field_flat,
-        up,
-        down,
+        *beside,
         starting_warmth,
         thermal_supply,
         recorded_temps[None, :],
@@ -395,13 +402,12 @@
     for bit in bits[1:]:
         parts, offsets = exchange(parts, offsets, bit)
     everyone = lax.all_to_all(payload, ("mem", "sp"), 0, 0, tiled=True)
-    everyone, *parts = lax.optimization_barrier((everyone, *parts))
     held = jnp.concatenate(parts, axis=0)
     parts = []
-    for turn in turns:
+    for turn in reversed(turns):
         columns = ((mine ^ turn) & (len(turns) - 1)) * share
         piece = lax.dynamic_slice_in_dim(held, columns, share, 1)
-        parts.append(across(piece, turn) if turn else piece)
+        parts.insert(0, across(piece, turn) if turn else piece)
     offsets = [offset ^ turn for turn in turns for offset in offsets]
     if order <= LANES:
         solved = pl.pallas_call(
@@ -448,8 +454,10 @@
             transcendentals=0,
         ),
         name="apply",
-    )(solved, *parts)
-    pieces = [across(piece, turn) if turn else piece for turn, piece in zip(turns, pieces)]
+    )(solved, *parts[::-1])
+    pieces = [
+        across(pieces[turn], turn) if turn else pieces[turn] for turn in reversed(turns)
+    ][::-1]
     revised = pl.pallas_call(
         merge_kernel,
         out_shape=jax.ShapeDtypeStruct((rows, width), jnp.float32),
@@ -457,7 +465,7 @@
         out_specs=vmem,
         compiler_params=pltpu.CompilerParams(vmem_limit_bytes=8 * 1024 * 1024),
         name="merge",
-    )(mine[None], field_flat, *pieces)
+    )(mine[None], field_flat, *pieces[::-1])
     return (revised.reshape(logarithmic_diffusivity.shape), predicted)
 
 

time: 44.5 us -> 39.3 us (0.88)
  waiting for transfers between devices: 12.6 us -> 7.59 us
    all_to_all x1, waiting for transfers between devices: 8.22 us -> 2.81 us  [body(): everyone = lax.all_to_all(payload, ('mem', 'sp'), 0, 0, tiled=True)]
  transfers between devices with their start and end apart: 10 -> 10, of which waited for: 6 -> 6; matrix products, arithmetic and copies ran while one was open for 0% -> 1% of each run, Pallas kernels for 23% -> 25%
where the time goes in v6:
time: 39.3 us; the launch traced here: 39.1 us
  starting transfers between devices  17.7 us (45%)
  Pallas kernels  11 us (28%)
  waiting for transfers between devices  7.59 us (19%)
  other arithmetic  1.16 us (3%)
  local copies, waits for them, and re-layouts  0.8 us (2%)
  between operations  0.77 us (2%)
    ppermute x8, starting transfers between devices, across(): return lax.ppermute(value, 'mem', [(i, i ^ bit) for i in range(owners)])  11.7 us
    all_to_all x1, starting transfers between devices, body(): everyone = lax.all_to_all(payload, ('mem', 'sp'), 0, 0, tiled=True)  5.48 us
    pallas_call x1, Pallas kernels, body(): pl.pallas_call(kernel, out_shape=(jax.ShapeDtypeStruct((members, probes),...  5.46 us
    ppermute x8, waiting for transfers between devices, across(): return lax.ppermute(value, 'mem', [(i, i ^ bit) for i in range(owners)])  4.78 us
    pallas_call x1, Pallas kernels, body(): pl.pallas_call(lambda *refs: solve_kernel(norm_scale, slabs, offsets, tur...  4.44 us
    all_to_all x1, waiting for transfers between devices, body(): everyone = lax.all_to_all(payload, ('mem', 'sp'), 0, 0, tiled=True)  2.81 us
    concatenate x1, other arithmetic, body(): jnp.concatenate([field_flat, starting_warmth, thermal_supply], axis=0)  1.06 us
  transfers between devices with their start and end apart: 10, of which 6 were waited for; matrix products, arithmetic and copies ran while one was open for 1% of the time, Pallas kernels for 25%

profile of v6, /device:TPU:0, one launch (start us, length us, event | category | flops | bytes accessed | tf_op | source)
XLA Modules:
  0.0 39.1 jit_solution(1828586336186169072)
XLA Ops:
  0.6 1.1 %pad_maximum_fusion = f32[80,1024]{1,0:T(8,128)S(1)} fusion(f32[8,1024]{1,0:T(8,128)} %refs_2_.1, f32[8,1024]{1,0:T(8,128)} %refs_1_.1, f32[64,1024]{1,0:T(8,128)} %bitcast.8), kind=kLoop, calls=%fused_computation | loop fusion | flops 163840 | bytes 655360 | tf_op jit(solution)/shard_map/concatenate | solution.py:345
  1.7 0.5 %collective-permute-start = (f32[80,1024]{1,0:T(8,128)S(1)}, f32[80,1024]{1,0:T(8,128)S(1)}, u32[]{:S(2)}, u32[]{:S(2)}) collective-permute-start(f32[80,1024]{1,0:T(8,128)S(1)} %pad_maximum_fusion), channel_id=1, source_target_pairs={{0,1},{1,0},{2,3},{3,2},{4,5},{5,4},{6,7},{7,6},{8,9},{9,8},{10,11... | collective-permute-start | bytes 983048 | tf_op jit(solution)/shard_map/ppermute | solution.py:347
  2.3 3.7 %collective-permute-start.1 = (bf16[64,1024]{1,0:T(8,128)(2,1)S(1)}, bf16[64,1024]{1,0:T(8,128)(2,1)S(1)}, u32[]{:S(2)}, u32[]{:S(2)}) collective-permute-start(bf16[64,1024]{1,0:T(8,128)(2,1)S(1)} %bitcast_convert_fusion), channel_id=1, source_target_pairs={{0,16},{2,18},{4,20},{6,22},{8,24},{10,26},{12,28},{14,30},{16,0},... | collective-permute-start | bytes 393224 | tf_op jit(solution)/shard_map/ppermute | solution.py:329
  5.9 0.1 add_convert_fusion.flags_ref
  6.0 0.6 %copy-done.3 = f32[8,64]{1,0:T(8,128)S(1)} copy-done((f32[8,64]{1,0:T(8,128)S(1)}, f32[8,64]{1,0:T(8,128)}, u32[]{:S(2)}) %copy-start.3) | copy-done | bytes 2072
  6.7 5.5 %conduct.1 = (f32[8,64]{1,0:T(8,128)}, f32[32,8,128]{2,1,0:T(8,128)}) custom-call(s32[2]{0:T(128)S(1)} %add_convert_fusion.flags_ref, s32[64]{0:T(128)S(1)} %copy-done.4, f32[64,1024]{1,0:T(8,128)S(1)} %bitcast.9, f32[80,1024]{1,0:T(8,128)S(1)} %collective-permute-done.refs_0_, f32[8,1024]{1,0:T(8,128)S(1)} %copy-done.2, f32[8,1024]{1,0:T(8,128)S(1)} %copy-done.1, ...), custom_call_target="tpu_custom_call" | custom-call | flops 15728640 | bytes 786432 | tf_op jit(solution)/shard_map/conduct/pallas_call | solution.py:365
  12.2 0.7 %collective-permute-done.1 = bf16[64,1024]{1,0:T(8,128)(2,1)S(1)} collective-permute-done((bf16[64,1024]{1,0:T(8,128)(2,1)S(1)}, bf16[64,1024]{1,0:T(8,128)(2,1)S(1)}, u32[]{:S(2)}, u32[]{:S(2)}) %collective-permute-start.1) | collective-permute-done | bytes 131104 | tf_op jit(solution)/shard_map/ppermute | solution.py:329
  12.9 0.9 %collective-permute-start.2 = (bf16[128,1024]{1,0:T(8,128)(2,1)S(1)}, bf16[128,1024]{1,0:T(8,128)(2,1)S(1)}, u32[]{:S(2)}, u32[]{:S(2)}) collective-permute-start(bf16[128,1024]{1,0:T(8,128)(2,1)S(1)} %pad_maximum_fusion.1), channel_id=1, source_target_pairs={{0,8},{2,10},{4,12},{6,14},{8,0},{10,2},{12,4},{14,6},{16,24},{18,... | collective-permute-start | bytes 786440 | tf_op jit(solution)/shard_map/ppermute | solution.py:329
  13.9 5.5 %all-to-all-start = ((f32[32,8,128]{2,1,0:T(8,128)}), f32[32,8,128]{2,1,0:T(8,128)S(1)}, u32[]{:S(2)}, u32[]{:S(2)}) async-start(f32[32,8,128]{2,1,0:T(8,128)} %get-tuple-element.12), calls=%async_computation | async-start | bytes 262144 | tf_op jit(solution)/shard_map/all_to_all | solution.py:404
  19.4 1.7 %collective-permute-done.2 = bf16[128,1024]{1,0:T(8,128)(2,1)S(1)} collective-permute-done((bf16[128,1024]{1,0:T(8,128)(2,1)S(1)}, bf16[128,1024]{1,0:T(8,128)(2,1)S(1)}, u32[]{:S(2)}, u32[]{:S(2)}) %collective-permute-start.2) | collective-permute-done | bytes 262176 | tf_op jit(solution)/shard_map/ppermute | solution.py:329
  21.1 0.1 constant_dynamic-slice_fusion
  21.2 2.4 %collective-permute-start.3 = (bf16[256,256]{1,0:T(8,128)(2,1)S(1)}, bf16[256,256]{1,0:T(8,128)(2,1)S(1)}, u32[]{:S(2)}, u32[]{:S(2)}) collective-permute-start(bf16[256,256]{1,0:T(8,128)(2,1)S(1)} %get-tuple-element.23), channel_id=1, source_target_pairs={{0,6},{2,4},{4,2},{6,0},{8,14},{10,12},{12,10},{14,8},{16,22},{18,... | collective-permute-start | bytes 393224 | tf_op jit(solution)/shard_map/ppermute | solution.py:329
  23.6 0.5 %collective-permute-start.4 = (bf16[256,256]{1,0:T(8,128)(2,1)S(1)}, bf16[256,256]{1,0:T(8,128)(2,1)S(1)}, u32[]{:S(2)}, u32[]{:S(2)}) collective-permute-start(bf16[256,256]{1,0:T(8,128)(2,1)S(1)} %get-tuple-element.22), channel_id=1, source_target_pairs={{0,4},{2,6},{4,0},{6,2},{8,12},{10,14},{12,8},{14,10},{16,20},{18,... | collective-permute-start | bytes 393224 | tf_op jit(solution)/shard_map/ppermute | solution.py:329
  24.1 0.7 %collective-permute-start.5 = (bf16[256,256]{1,0:T(8,128)(2,1)S(1)}, bf16[256,256]{1,0:T(8,128)(2,1)S(1)}, u32[]{:S(2)}, u32[]{:S(2)}) collective-permute-start(bf16[256,256]{1,0:T(8,128)(2,1)S(1)} %get-tuple-element.21), channel_id=1, source_target_pairs={{0,2},{2,0},{4,6},{6,4},{8,10},{10,8},{12,14},{14,12},{16,18},{18,... | collective-permute-start | bytes 393224 | tf_op jit(solution)/shard_map/ppermute | solution.py:329
  24.8 2.8 %all-to-all-done.refs_1_ = f32[32,8,128]{2,1,0:T(8,128)S(1)} async-done(((f32[32,8,128]{2,1,0:T(8,128)}), f32[32,8,128]{2,1,0:T(8,128)S(1)}, u32[]{:S(2)}, u32[]{:S(2)}) %all-to-all-start) | async-done | bytes 131104 | tf_op jit(solution)/shard_map/all_to_all | solution.py:404
  27.6 4.4 %solve.1.refs_0_ = bf16[32,128]{1,0:T(8,128)(2,1)S(1)} custom-call(s32[1]{0:T(128)} %bitcast.refs_0_.place_ref, f32[32,8,128]{2,1,0:T(8,128)S(1)} %all-to-all-done.refs_1_), custom_call_target="tpu_custom_call" | custom-call | flops 4194304 | bytes 131072 | tf_op jit(solution)/shard_map/solve/pallas_call | solution.py:413
  32.0 0.4 %apply.1 = (f32[64,256]{1,0:T(8,128)S(1)}, bf16[64,256]{1,0:T(8,128)(2,1)S(1)}, bf16[64,256]{1,0:T(8,128)(2,1)S(1)}, bf16[64,256]{1,0:T(8,128)(2,1)S(1)}) custom-call(bf16[32,128]{1,0:T(8,128)(2,1)S(1)} %solve.1.refs_0_, bf16[256,256]{1,0:T(8,128)(2,1)S(1)} %collective-permute-done.3.refs_1_, bf16[256,256]{1,0:T(8,128)(2,1)S(1)} %collective-permute-done.4.refs_2_, ...), custom_call_target="tpu_custom_call" | custom-call | flops 134217728 | bytes 524288 | tf_op jit(solution)/shard_map/apply/pallas_call | solution.py:442
  32.4 0.9 %collective-permute-start.6 = (bf16[64,256]{1,0:T(8,128)(2,1)S(1)}, bf16[64,256]{1,0:T(8,128)(2,1)S(1)}, u32[]{:S(2)}, u32[]{:S(2)}) collective-permute-start(bf16[64,256]{1,0:T(8,128)(2,1)S(1)} %get-tuple-element.15), channel_id=1, source_target_pairs={{0,6},{2,4},{4,2},{6,0},{8,14},{10,12},{12,10},{14,8},{16,22},{18,... | collective-permute-start | bytes 98312 | tf_op jit(solution)/shard_map/ppermute | solution.py:329
  33.4 1.0 %collective-permute-start.7 = (bf16[64,256]{1,0:T(8,128)(2,1)S(1)}, bf16[64,256]{1,0:T(8,128)(2,1)S(1)}, u32[]{:S(2)}, u32[]{:S(2)}) collective-permute-start(bf16[64,256]{1,0:T(8,128)(2,1)S(1)} %get-tuple-element.16), channel_id=1, source_target_pairs={{0,4},{2,6},{4,0},{6,2},{8,12},{10,14},{12,8},{14,10},{16,20},{18,... | collective-permute-start | bytes 98312 | tf_op jit(solution)/shard_map/ppermute | solution.py:329
  34.4 1.6 %collective-permute-start.8 = (bf16[64,256]{1,0:T(8,128)(2,1)S(1)}, bf16[64,256]{1,0:T(8,128)(2,1)S(1)}, u32[]{:S(2)}, u32[]{:S(2)}) collective-permute-start(bf16[64,256]{1,0:T(8,128)(2,1)S(1)} %get-tuple-element.17), channel_id=1, source_target_pairs={{0,2},{2,0},{4,6},{6,4},{8,10},{10,8},{12,14},{14,12},{16,18},{18,... | collective-permute-start | bytes 98312 | tf_op jit(solution)/shard_map/ppermute | solution.py:329
  36.0 1.6 %collective-permute-done.6.refs_0_ = bf16[64,256]{1,0:T(8,128)(2,1)S(1)} collective-permute-done((bf16[64,256]{1,0:T(8,128)(2,1)S(1)}, bf16[64,256]{1,0:T(8,128)(2,1)S(1)}, u32[]{:S(2)}, u32[]{:S(2)}) %collective-permute-start.6) | collective-permute-done | bytes 32800 | tf_op jit(solution)/shard_map/ppermute | solution.py:329
  37.6 0.1 collective-permute-done.7.refs_1_
  37.6 0.7 %collective-permute-done.8.refs_2_ = bf16[64,256]{1,0:T(8,128)(2,1)S(1)} collective-permute-done((bf16[64,256]{1,0:T(8,128)(2,1)S(1)}, bf16[64,256]{1,0:T(8,128)(2,1)S(1)}, u32[]{:S(2)}, u32[]{:S(2)}) %collective-permute-start.8) | collective-permute-done | bytes 32800 | tf_op jit(solution)/shard_map/ppermute | solution.py:329
  38.3 0.7 %merge.1 = f32[64,1024]{1,0:T(8,128)} custom-call(s32[1]{0:T(128)} %bitcast.refs_0_.place_ref, f32[64,1024]{1,0:T(8,128)S(1)} %bitcast.10, bf16[64,256]{1,0:T(8,128)(2,1)S(1)} %collective-permute-done.6.refs_0_, bf16[64,256]{1,0:T(8,128)(2,1)S(1)} %collective-permute-done.7.refs_1_, bf16[64,256]{1,0:T(8,128)(2,1)S(1)} %collective-permute-done.8.refs_2_, ...), custom_call_target="tpu_custom_call" | custom-call | tf_op jit(solution)/shard_map/merge/pallas_call | solution.py:461
  (22 shorter events, 0.2 us)
Async XLA Ops:
  0.6 1.6 %copy-start = (f32[8,8,1024]{2,1,0:T(8,128)S(1)}, f32[8,8,1024]{2,1,0:T(8,128)}, u32[]{:S(2)}) copy-start(f32[8,8,1024]{2,1,0:T(8,128)} %param.7) | copy-start | bytes 786436
  1.7 4.3 %copy-start.1 = (f32[8,1024]{1,0:T(8,128)S(1)}, f32[8,1024]{1,0:T(8,128)}, u32[]{:S(2)}) copy-start(f32[8,1024]{1,0:T(8,128)} %refs_2_.1) | copy-start | bytes 98308
  1.7 4.3 %copy-start.2 = (f32[8,1024]{1,0:T(8,128)S(1)}, f32[8,1024]{1,0:T(8,128)}, u32[]{:S(2)}) copy-start(f32[8,1024]{1,0:T(8,128)} %refs_1_.1) | copy-start | bytes 98308
  1.7 4.3 %collective-permute-start = (f32[80,1024]{1,0:T(8,128)S(1)}, f32[80,1024]{1,0:T(8,128)S(1)}, u32[]{:S(2)}, u32[]{:S(2)}) collective-permute-start(f32[80,1024]{1,0:T(8,128)S(1)} %pad_maximum_fusion), channel_id=1, source_target_pairs={{0,1},{1,0},{2,3},{3,2},{4,5},{5,4},{6,7},{7,6},{8,9},{9,8},{10,11... | collective-permute-start | bytes 983048 | tf_op jit(solution)/shard_map/ppermute | solution.py:347
  2.3 10.6 %collective-permute-start.1 = (bf16[64,1024]{1,0:T(8,128)(2,1)S(1)}, bf16[64,1024]{1,0:T(8,128)(2,1)S(1)}, u32[]{:S(2)}, u32[]{:S(2)}) collective-permute-start(bf16[64,1024]{1,0:T(8,128)(2,1)S(1)} %bitcast_convert_fusion), channel_id=1, source_target_pairs={{0,16},{2,18},{4,20},{6,22},{8,24},{10,26},{12,28},{14,30},{16,0},... | collective-permute-start | bytes 393224 | tf_op jit(solution)/shard_map/ppermute | solution.py:329
  5.9 0.7 %copy-start.3 = (f32[8,64]{1,0:T(8,128)S(1)}, f32[8,64]{1,0:T(8,128)}, u32[]{:S(2)}) copy-start(f32[8,64]{1,0:T(8,128)} %refs_5_.1) | copy-start | bytes 6148
  6.0 0.7 %copy-start.4 = (s32[64]{0:T(128)S(1)}, s32[64]{0:T(128)}, u32[]{:S(2)}) copy-start(s32[64]{0:T(128)} %columns_hbm.1) | copy-start | bytes 772
  6.0 0.7 %copy-start.5 = (f32[64]{0:T(128)S(1)}, f32[64]{0:T(128)}, u32[]{:S(2)}) copy-start(f32[64]{0:T(128)} %param.11) | copy-start | bytes 772
  6.0 0.7 %copy-start.6 = (f32[64]{0:T(128)S(1)}, f32[64]{0:T(128)}, u32[]{:S(2)}) copy-start(f32[64]{0:T(128)} %param.12) | copy-start | bytes 772
  12.9 8.2 %collective-permute-start.2 = (bf16[128,1024]{1,0:T(8,128)(2,1)S(1)}, bf16[128,1024]{1,0:T(8,128)(2,1)S(1)}, u32[]{:S(2)}, u32[]{:S(2)}) collective-permute-start(bf16[128,1024]{1,0:T(8,128)(2,1)S(1)} %pad_maximum_fusion.1), channel_id=1, source_target_pairs={{0,8},{2,10},{4,12},{6,14},{8,0},{10,2},{12,4},{14,6},{16,24},{18,... | collective-permute-start | bytes 786440 | tf_op jit(solution)/shard_map/ppermute | solution.py:329
  13.9 13.7 %all-to-all-start = ((f32[32,8,128]{2,1,0:T(8,128)}), f32[32,8,128]{2,1,0:T(8,128)S(1)}, u32[]{:S(2)}, u32[]{:S(2)}) async-start(f32[32,8,128]{2,1,0:T(8,128)} %get-tuple-element.12), calls=%async_computation | async-start | bytes 262144 | tf_op jit(solution)/shard_map/all_to_all | solution.py:404
  21.2 10.8 %collective-permute-start.3 = (bf16[256,256]{1,0:T(8,128)(2,1)S(1)}, bf16[256,256]{1,0:T(8,128)(2,1)S(1)}, u32[]{:S(2)}, u32[]{:S(2)}) collective-permute-start(bf16[256,256]{1,0:T(8,128)(2,1)S(1)} %get-tuple-element.23), channel_id=1, source_target_pairs={{0,6},{2,4},{4,2},{6,0},{8,14},{10,12},{12,10},{14,8},{16,22},{18,... | collective-permute-start | bytes 393224 | tf_op jit(solution)/shard_map/ppermute | solution.py:329
  23.6 8.5 %collective-permute-start.4 = (bf16[256,256]{1,0:T(8,128)(2,1)S(1)}, bf16[256,256]{1,0:T(8,128)(2,1)S(1)}, u32[]{:S(2)}, u32[]{:S(2)}) collective-permute-start(bf16[256,256]{1,0:T(8,128)(2,1)S(1)} %get-tuple-element.22), channel_id=1, source_target_pairs={{0,4},{2,6},{4,0},{6,2},{8,12},{10,14},{12,8},{14,10},{16,20},{18,... | collective-permute-start | bytes 393224 | tf_op jit(solution)/shard_map/ppermute | solution.py:329
  24.1 8.0 %collective-permute-start.5 = (bf16[256,256]{1,0:T(8,128)(2,1)S(1)}, bf16[256,256]{1,0:T(8,128)(2,1)S(1)}, u32[]{:S(2)}, u32[]{:S(2)}) collective-permute-start(bf16[256,256]{1,0:T(8,128)(2,1)S(1)} %get-tuple-element.21), channel_id=1, source_target_pairs={{0,2},{2,0},{4,6},{6,4},{8,10},{10,8},{12,14},{14,12},{16,18},{18,... | collective-permute-start | bytes 393224 | tf_op jit(solution)/shard_map/ppermute | solution.py:329
  32.4 5.1 %collective-permute-start.6 = (bf16[64,256]{1,0:T(8,128)(2,1)S(1)}, bf16[64,256]{1,0:T(8,128)(2,1)S(1)}, u32[]{:S(2)}, u32[]{:S(2)}) collective-permute-start(bf16[64,256]{1,0:T(8,128)(2,1)S(1)} %get-tuple-element.15), channel_id=1, source_target_pairs={{0,6},{2,4},{4,2},{6,0},{8,14},{10,12},{12,10},{14,8},{16,22},{18,... | collective-permute-start | bytes 98312 | tf_op jit(solution)/shard_map/ppermute | solution.py:329
  33.4 4.3 %collective-permute-start.7 = (bf16[64,256]{1,0:T(8,128)(2,1)S(1)}, bf16[64,256]{1,0:T(8,128)(2,1)S(1)}, u32[]{:S(2)}, u32[]{:S(2)}) collective-permute-start(bf16[64,256]{1,0:T(8,128)(2,1)S(1)} %get-tuple-element.16), channel_id=1, source_target_pairs={{0,4},{2,6},{4,0},{6,2},{8,12},{10,14},{12,8},{14,10},{16,20},{18,... | collective-permute-start | bytes 98312 | tf_op jit(solution)/shard_map/ppermute | solution.py:329
  34.4 3.9 %collective-permute-start.8 = (bf16[64,256]{1,0:T(8,128)(2,1)S(1)}, bf16[64,256]{1,0:T(8,128)(2,1)S(1)}, u32[]{:S(2)}, u32[]{:S(2)}) collective-permute-start(bf16[64,256]{1,0:T(8,128)(2,1)S(1)} %get-tuple-element.17), channel_id=1, source_target_pairs={{0,2},{2,0},{4,6},{6,4},{8,10},{10,8},{12,14},{14,12},{16,18},{18,... | collective-permute-start | bytes 98312 | tf_op jit(solution)/shard_map/ppermute | solution.py:329

commit v7 on v6

--- a/solution.py
+++ b/solution.py
@@ -54,7 +54,6 @@
 
 
 def conduct_kernel(
-    flags_ref,
     columns_hbm,
     field_ref,
     up_ref,
@@ -95,7 +94,8 @@
     lane = lax.broadcasted_iota(jnp.int32, (members, LANES), 1)
     first, last = lane == 0, lane == LANES - 1
 
-    above, below = flags_ref[0] > 0, flags_ref[1] > 0
+    slab = lax.axis_index("sp")
+    above, below = slab > 0, slab < lax.axis_size("sp") - 1
     sides = (
         (0, up_ref, lines - STEPS, STEPS, above),
         (STEPS, field_ref, 0, lines, None),
@@ -157,8 +157,8 @@
                 right.append((c[k] + c_right) * (t_right - t[k]))
             back = [pltpu.roll(x, 1, 1) for x in right]
             outside = jnp.logical_or(
-                jnp.logical_and(row < STEPS, flags_ref[0] <= 0),
-                jnp.logical_and(row >= STEPS + lines, flags_ref[1] <= 0),
+                jnp.logical_and(row < STEPS, jnp.logical_not(above)),
+                jnp.logical_and(row >= STEPS + lines, jnp.logical_not(below)),
             )
             keep = jnp.where(outside, 0.0, 1.0)
             source = supply[pl.ds(row, 1), :]
@@ -196,10 +196,10 @@
         payload_ref[device] = payload
 
 
-def solve_kernel(norm_scale, slabs, offsets, turns, place_ref, payload_ref, solved_ref):
+def solve_kernel(norm_scale, slabs, offsets, turns, payload_ref, solved_ref):
     members, probes = payload_ref.shape[1], payload_ref.shape[2] // 2
     order = len(offsets) * members
-    mine = place_ref[0]
+    mine = lax.axis_index("mem")
     dims = (((1,), (1,)), ((), ()))
     gram, cross = None, None
     for slab in range(slabs):
@@ -295,10 +295,10 @@
         ref[...] = change[turn * rows : (turn + 1) * rows].astype(ref.dtype)
 
 
-def merge_kernel(place_ref, field_ref, *refs):
+def merge_kernel(field_ref, *refs):
     pieces, out_ref = refs[:-1][::-1], refs[-1]
     share = pieces[0].shape[1]
-    mine = jnp.bitwise_and(place_ref[0], len(pieces) - 1)
+    mine = jnp.bitwise_and(lax.axis_index("mem"), len(pieces) - 1)
     for turn, piece in enumerate(pieces):
         start = pl.multiple_of(jnp.bitwise_xor(mine, turn) * share, LANES)
         columns = pl.ds(start, share)
@@ -319,7 +319,6 @@
     order = members * owners
     norm_scale = 1.0 / math.sqrt(order - 1)
     probes = probe_positions.shape[0]
-    slab = lax.axis_index("sp")
 
     mine = lax.axis_index("mem").astype(jnp.int32)
     turns = range(math.gcd(owners, 4))
@@ -339,16 +338,17 @@
         held = jnp.concatenate(parts, axis=0)
         return [held, across(held, bit)], offsets + [offset ^ bit for offset in offsets]
 
-    for bit in bits[:1]:
-        parts, offsets = exchange(parts, offsets, bit)
-
-    edges = jnp.concatenate([field_flat, starting_warmth, thermal_supply], axis=0)
+    for bit in bits[:2]:
+        offsets = offsets + [offset ^ bit for offset in reversed(offsets)]
+    parts = [across(field_round, offset) if offset else field_round for offset in offsets]
+
+    start_tied, parts[0] = lax.optimization_barrier((starting_warmth, parts[0]))
+    edges = jnp.concatenate([field_flat, start_tied, thermal_supply], axis=0)
     if slabs == 2:
         up = down = lax.ppermute(edges, "sp", [(0, 1), (1, 0)])
     else:
         up = lax.ppermute(edges, "sp", [(i, i + 1) for i in range(slabs - 1)])
         down = lax.ppermute(edges, "sp", [(i + 1, i) for i in range(slabs - 1)])
-    flags = jnp.stack([slab > 0, slab < slabs - 1]).astype(jnp.int32)
     vmem = pl.BlockSpec(memory_space=pltpu.VMEM)
     smem = pl.BlockSpec(memory_space=pltpu.SMEM)
     anywhere = pl.BlockSpec(memory_space=pl.ANY)
@@ -356,11 +356,9 @@
     devices = owners * slabs
     beside = [up] if slabs == 2 else [up, down]
 
-    def kernel(flags_ref, columns_hbm, field_ref, *refs):
+    def kernel(columns_hbm, field_ref, *refs):
         neighbours, rest = refs[: len(beside)], refs[len(beside) :]
-        conduct_kernel(
-            flags_ref, columns_hbm, field_ref, neighbours[0], neighbours[-1], *rest
-        )
+        conduct_kernel(columns_hbm, field_ref, neighbours[0], neighbours[-1], *rest)
 
     predicted, payload = pl.pallas_call(
         kernel,
@@ -368,7 +366,7 @@
             jax.ShapeDtypeStruct((members, probes), jnp.float32),
             jax.ShapeDtypeStruct((devices, members, 2 * probes), jnp.float32),
         ),
-        in_specs=[smem, anywhere] + [vmem] * (3 + len(beside)) + [anywhere] * 3,
+        in_specs=[anywhere] + [vmem] * (3 + len(beside)) + [anywhere] * 3,
         out_specs=(vmem, vmem),
         scratch_shapes=[
             pltpu.VMEM((window, members, width), jnp.float32),
@@ -388,7 +386,6 @@
         ),
         name="conduct",
     )(
-        flags,
         probe_positions,
         field_flat,
         *beside,
@@ -398,8 +395,8 @@
         probe_error_sigma[None, :],
         perturb_draws,
     )
-    payload, *parts = lax.optimization_barrier((payload, *parts))
-    for bit in bits[1:]:
+    _, *parts = lax.optimization_barrier((payload, *parts))
+    for bit in bits[2:]:
         parts, offsets = exchange(parts, offsets, bit)
     everyone = lax.all_to_all(payload, ("mem", "sp"), 0, 0, tiled=True)
     held = jnp.concatenate(parts, axis=0)
@@ -413,7 +410,7 @@
         solved = pl.pallas_call(
             lambda *refs: solve_kernel(norm_scale, slabs, offsets, turns, *refs),
             out_shape=jax.ShapeDtypeStruct((len(turns) * members, order), jnp.bfloat16),
-            in_specs=[smem, vmem],
+            in_specs=[vmem],
             out_specs=vmem,
             compiler_params=pltpu.CompilerParams(vmem_limit_bytes=16 * 1024 * 1024),
             cost_estimate=pl.CostEstimate(
@@ -422,7 +419,7 @@
                 transcendentals=0,
             ),
             name="solve",
-        )(mine[None], everyone)
+        )(everyone)
     else:
         owner = mine ^ jnp.array(offsets, jnp.int32)
         split = everyone.reshape(owners, slabs, members, 2, probes)[owner]
@@ -461,11 +458,11 @@
     revised = pl.pallas_call(
         merge_kernel,
         out_shape=jax.ShapeDtypeStruct((rows, width), jnp.float32),
-        in_specs=[smem] + [vmem] * (1 + len(turns)),
+        in_specs=[vmem] * (1 + len(turns)),
         out_specs=vmem,
         compiler_params=pltpu.CompilerParams(vmem_limit_bytes=8 * 1024 * 1024),
         name="merge",
-    )(mine[None], field_flat, *pieces[::-1])
+    )(field_flat, *pieces[::-1])
     return (revised.reshape(logarithmic_diffusivity.shape), predicted)
 
 

time: 39.3 us -> 38.4 us (0.977)
  waiting for transfers between devices: 7.59 us -> 6.96 us
  Pallas kernels: 11 us -> 10.5 us
    ppermute x8 -> x9, waiting for transfers between devices: 4.78 us -> 2.48 us  [across(): return lax.ppermute(value, 'mem', [(i, i ^ bit) for i in range(owners)])]
    all_to_all x1, waiting for transfers between devices: 2.81 us -> 4.48 us  [body(): everyone = lax.all_to_all(payload, ('mem', 'sp'), 0, 0, tiled=True)]
    concatenate x2 -> x1, other arithmetic: 1.07 us -> 0.02 us  [body(): edges = jnp.concatenate([field_flat, start_tied, thermal_supply], axis=0)]
    convert_element_type x1, other arithmetic: 0.01 us -> 1.01 us  [body(): field_round = field_flat.astype(jnp.bfloat16)]
    ppermute x8 -> x9, starting transfers between devices: 11.7 us -> 12.3 us  [across(): return lax.ppermute(value, 'mem', [(i, i ^ bit) for i in range(owners)])]
    pallas_call x1, Pallas kernels: 5.46 us -> 4.94 us  [body(): pl.pallas_call(kernel, out_shape=(jax.ShapeDtypeStruct((members, probes),...]
  transfers between devices with their start and end apart: 10 -> 11, of which waited for: 6 -> 4; matrix products, arithmetic and copies ran while one was open for 1% -> 0% of each run, Pallas kernels for 25% -> 24%
where the time goes in v7:
time: 38.4 us; the launch traced here: 38.2 us
  starting transfers between devices  18 us (47%)
  Pallas kernels  10.5 us (27%)
  waiting for transfers between devices  6.96 us (18%)
  other arithmetic  1.03 us (3%)
  local copies, waits for them, and re-layouts  0.82 us (2%)
  between operations  0.82 us (2%)
    ppermute x9, starting transfers between devices, across(): return lax.ppermute(value, 'mem', [(i, i ^ bit) for i in range(owners)])  12.3 us
    all_to_all x1, starting transfers between devices, body(): everyone = lax.all_to_all(payload, ('mem', 'sp'), 0, 0, tiled=True)  5.18 us
    pallas_call x1, Pallas kernels, body(): pl.pallas_call(kernel, out_shape=(jax.ShapeDtypeStruct((members, probes),...  4.94 us
    all_to_all x1, waiting for transfers between devices, body(): everyone = lax.all_to_all(payload, ('mem', 'sp'), 0, 0, tiled=True)  4.48 us
    pallas_call x1, Pallas kernels, body(): pl.pallas_call(lambda *refs: solve_kernel(norm_scale, slabs, offsets, tur...  4.4 us
    ppermute x9, waiting for transfers between devices, across(): return lax.ppermute(value, 'mem', [(i, i ^ bit) for i in range(owners)])  2.48 us
    convert_element_type x1, other arithmetic, body(): field_round = field_flat.astype(jnp.bfloat16)  1.01 us
  transfers between devices with their start and end apart: 11, of which 4 were waited for; matrix products, arithmetic and copies ran while one was open for 0% of the time, Pallas kernels for 24%

profile of v7, /device:TPU:0, one launch (start us, length us, event | category | flops | bytes accessed | tf_op | source)
XLA Modules:
  0.0 38.2 jit_solution(7852474636530291992)
XLA Ops:
  0.7 1.0 %bitcast_convert_fusion = bf16[64,1024]{1,0:T(8,128)(2,1)S(1)} fusion(f32[8,8,1024]{2,1,0:T(8,128)} %param.7), kind=kLoop, calls=%fused_computation.9 | loop fusion | flops 65536 | bytes 393216 | tf_op jit(solution)/shard_map/convert_element_type | solution.py:331
  1.7 0.5 %collective-permute-start = (f32[80,1024]{1,0:T(8,128)S(1)}, f32[80,1024]{1,0:T(8,128)S(1)}, u32[]{:S(2)}, u32[]{:S(2)}) collective-permute-start(f32[80,1024]{1,0:T(8,128)S(1)} %pad_maximum_fusion), channel_id=1, source_target_pairs={{0,1},{1,0},{2,3},{3,2},{4,5},{5,4},{6,7},{7,6},{8,9},{9,8},{10,11... | collective-permute-start | bytes 983048 | tf_op jit(solution)/shard_map/ppermute | solution.py:348
  2.3 3.7 %collective-permute-start.1 = (bf16[64,1024]{1,0:T(8,128)(2,1)S(1)}, bf16[64,1024]{1,0:T(8,128)(2,1)S(1)}, u32[]{:S(2)}, u32[]{:S(2)}) collective-permute-start(bf16[64,1024]{1,0:T(8,128)(2,1)S(1)} %bitcast_convert_fusion), channel_id=1, source_target_pairs={{0,16},{2,18},{4,20},{6,22},{8,24},{10,26},{12,28},{14,30},{16,0},... | collective-permute-start | bytes 393224 | tf_op jit(solution)/shard_map/ppermute | solution.py:328
  5.9 1.3 %collective-permute-start.2 = (bf16[64,1024]{1,0:T(8,128)(2,1)S(1)}, bf16[64,1024]{1,0:T(8,128)(2,1)S(1)}, u32[]{:S(2)}, u32[]{:S(2)}) collective-permute-start(bf16[64,1024]{1,0:T(8,128)(2,1)S(1)} %bitcast_convert_fusion), channel_id=1, source_target_pairs={{0,24},{2,26},{4,28},{6,30},{8,16},{10,18},{12,20},{14,22},{16,8},... | collective-permute-start | bytes 393224 | tf_op jit(solution)/shard_map/ppermute | solution.py:328
  7.3 0.2 collective-permute-start.3
  7.5 0.0 copy-start.6
  7.5 0.7 %copy-done.3 = f32[8,64]{1,0:T(8,128)S(1)} copy-done((f32[8,64]{1,0:T(8,128)S(1)}, f32[8,64]{1,0:T(8,128)}, u32[]{:S(2)}) %copy-start.3) | copy-done | bytes 2072
  8.2 0.0 copy-done.6
  8.2 4.9 %conduct.1 = (f32[8,64]{1,0:T(8,128)}, f32[32,8,128]{2,1,0:T(8,128)}) custom-call(s32[64]{0:T(128)S(1)} %copy-done.4, f32[64,1024]{1,0:T(8,128)S(1)} %bitcast.6, f32[80,1024]{1,0:T(8,128)S(1)} %collective-permute-done.refs_0_, f32[8,1024]{1,0:T(8,128)S(1)} %copy-done.2, f32[8,1024]{1,0:T(8,128)S(1)} %copy-done.1, f32[1,64]{1,0:T(1,128)S(1)} %bitcast.8, ...), custom_call_target="tpu_custom_call" | custom-call | flops 15728640 | bytes 786432 | tf_op jit(solution)/shard_map/conduct/pallas_call | solution.py:363
  13.2 5.2 %all-to-all-start = ((f32[32,8,128]{2,1,0:T(8,128)}), f32[32,8,128]{2,1,0:T(8,128)S(1)}, u32[]{:S(2)}, u32[]{:S(2)}) async-start(f32[32,8,128]{2,1,0:T(8,128)} %get-tuple-element.15), calls=%async_computation | async-start | bytes 262144 | tf_op jit(solution)/shard_map/all_to_all | solution.py:401
  18.4 0.1 constant_dynamic-slice_fusion
  18.5 2.7 %collective-permute-start.4 = (bf16[256,256]{1,0:T(8,128)(2,1)S(1)}, bf16[256,256]{1,0:T(8,128)(2,1)S(1)}, u32[]{:S(2)}, u32[]{:S(2)}) collective-permute-start(bf16[256,256]{1,0:T(8,128)(2,1)S(1)} %get-tuple-element.29), channel_id=1, source_target_pairs={{0,6},{2,4},{4,2},{6,0},{8,14},{10,12},{12,10},{14,8},{16,22},{18,... | collective-permute-start | bytes 393224 | tf_op jit(solution)/shard_map/ppermute | solution.py:328
  21.3 0.6 %collective-permute-start.5 = (bf16[256,256]{1,0:T(8,128)(2,1)S(1)}, bf16[256,256]{1,0:T(8,128)(2,1)S(1)}, u32[]{:S(2)}, u32[]{:S(2)}) collective-permute-start(bf16[256,256]{1,0:T(8,128)(2,1)S(1)} %get-tuple-element.28), channel_id=1, source_target_pairs={{0,4},{2,6},{4,0},{6,2},{8,12},{10,14},{12,8},{14,10},{16,20},{18,... | collective-permute-start | bytes 393224 | tf_op jit(solution)/shard_map/ppermute | solution.py:328
  21.8 0.3 collective-permute-start.6
  22.1 4.5 %all-to-all-done.refs_0_ = f32[32,8,128]{2,1,0:T(8,128)S(1)} async-done(((f32[32,8,128]{2,1,0:T(8,128)}), f32[32,8,128]{2,1,0:T(8,128)S(1)}, u32[]{:S(2)}, u32[]{:S(2)}) %all-to-all-start) | async-done | bytes 131104 | tf_op jit(solution)/shard_map/all_to_all | solution.py:401
  26.6 4.4 %solve.1.refs_0_ = bf16[32,128]{1,0:T(8,128)(2,1)S(1)} custom-call(f32[32,8,128]{2,1,0:T(8,128)S(1)} %all-to-all-done.refs_0_), custom_call_target="tpu_custom_call" | custom-call | flops 4194304 | bytes 131072 | tf_op jit(solution)/shard_map/solve/pallas_call | solution.py:410
  31.0 0.4 %apply.1 = (f32[64,256]{1,0:T(8,128)S(1)}, bf16[64,256]{1,0:T(8,128)(2,1)S(1)}, bf16[64,256]{1,0:T(8,128)(2,1)S(1)}, bf16[64,256]{1,0:T(8,128)(2,1)S(1)}) custom-call(bf16[32,128]{1,0:T(8,128)(2,1)S(1)} %solve.1.refs_0_, bf16[256,256]{1,0:T(8,128)(2,1)S(1)} %collective-permute-done.4.refs_1_, bf16[256,256]{1,0:T(8,128)(2,1)S(1)} %collective-permute-done.5.refs_2_, ...), custom_call_target="tpu_custom_call" | custom-call | flops 134217728 | bytes 524288 | tf_op jit(solution)/shard_map/apply/pallas_call | solution.py:439
  31.4 0.9 %collective-permute-start.7 = (bf16[64,256]{1,0:T(8,128)(2,1)S(1)}, bf16[64,256]{1,0:T(8,128)(2,1)S(1)}, u32[]{:S(2)}, u32[]{:S(2)}) collective-permute-start(bf16[64,256]{1,0:T(8,128)(2,1)S(1)} %get-tuple-element.21), channel_id=1, source_target_pairs={{0,6},{2,4},{4,2},{6,0},{8,14},{10,12},{12,10},{14,8},{16,22},{18,... | collective-permute-start | bytes 98312 | tf_op jit(solution)/shard_map/ppermute | solution.py:328
  32.3 1.2 %collective-permute-start.8 = (bf16[64,256]{1,0:T(8,128)(2,1)S(1)}, bf16[64,256]{1,0:T(8,128)(2,1)S(1)}, u32[]{:S(2)}, u32[]{:S(2)}) collective-permute-start(bf16[64,256]{1,0:T(8,128)(2,1)S(1)} %get-tuple-element.22), channel_id=1, source_target_pairs={{0,4},{2,6},{4,0},{6,2},{8,12},{10,14},{12,8},{14,10},{16,20},{18,... | collective-permute-start | bytes 98312 | tf_op jit(solution)/shard_map/ppermute | solution.py:328
  33.5 1.4 %collective-permute-start.9 = (bf16[64,256]{1,0:T(8,128)(2,1)S(1)}, bf16[64,256]{1,0:T(8,128)(2,1)S(1)}, u32[]{:S(2)}, u32[]{:S(2)}) collective-permute-start(bf16[64,256]{1,0:T(8,128)(2,1)S(1)} %get-tuple-element.23), channel_id=1, source_target_pairs={{0,2},{2,0},{4,6},{6,4},{8,10},{10,8},{12,14},{14,12},{16,18},{18,... | collective-permute-start | bytes 98312 | tf_op jit(solution)/shard_map/ppermute | solution.py:328
  35.0 1.6 %collective-permute-done.7.refs_0_ = bf16[64,256]{1,0:T(8,128)(2,1)S(1)} collective-permute-done((bf16[64,256]{1,0:T(8,128)(2,1)S(1)}, bf16[64,256]{1,0:T(8,128)(2,1)S(1)}, u32[]{:S(2)}, u32[]{:S(2)}) %collective-permute-start.7) | collective-permute-done | bytes 32800 | tf_op jit(solution)/shard_map/ppermute | solution.py:328
  36.5 0.1 collective-permute-done.8.refs_1_
  36.6 0.8 %collective-permute-done.9.refs_2_ = bf16[64,256]{1,0:T(8,128)(2,1)S(1)} collective-permute-done((bf16[64,256]{1,0:T(8,128)(2,1)S(1)}, bf16[64,256]{1,0:T(8,128)(2,1)S(1)}, u32[]{:S(2)}, u32[]{:S(2)}) %collective-permute-start.9) | collective-permute-done | bytes 32800 | tf_op jit(solution)/shard_map/ppermute | solution.py:328
  37.4 0.7 %merge.1 = f32[64,1024]{1,0:T(8,128)} custom-call(f32[64,1024]{1,0:T(8,128)S(1)} %bitcast.7, bf16[64,256]{1,0:T(8,128)(2,1)S(1)} %collective-permute-done.7.refs_0_, bf16[64,256]{1,0:T(8,128)(2,1)S(1)} %collective-permute-done.8.refs_1_, bf16[64,256]{1,0:T(8,128)(2,1)S(1)} %collective-permute-done.9.refs_2_, f32[64,256]{1,0:T(8,128)S(1)} %get-tuple-element.24.refs_3_), custom_call_target="tpu_custom_call" | custom-call | tf_op jit(solution)/shard_map/merge/pallas_call | solution.py:458
  (23 shorter events, 0.1 us)
Async XLA Ops:
  0.6 1.0 %copy-start = (f32[8,8,1024]{2,1,0:T(8,128)S(1)}, f32[8,8,1024]{2,1,0:T(8,128)}, u32[]{:S(2)}) copy-start(f32[8,8,1024]{2,1,0:T(8,128)} %param.7) | copy-start | bytes 786436
  0.6 1.0 %copy-start.2 = (f32[8,1024]{1,0:T(8,128)S(1)}, f32[8,1024]{1,0:T(8,128)}, u32[]{:S(2)}) copy-start(f32[8,1024]{1,0:T(8,128)} %refs_1_.1) | copy-start | bytes 98308
  0.6 1.0 %copy-start.1 = (f32[8,1024]{1,0:T(8,128)S(1)}, f32[8,1024]{1,0:T(8,128)}, u32[]{:S(2)}) copy-start(f32[8,1024]{1,0:T(8,128)} %refs_2_.1) | copy-start | bytes 98308
  1.7 5.8 %collective-permute-start = (f32[80,1024]{1,0:T(8,128)S(1)}, f32[80,1024]{1,0:T(8,128)S(1)}, u32[]{:S(2)}, u32[]{:S(2)}) collective-permute-start(f32[80,1024]{1,0:T(8,128)S(1)} %pad_maximum_fusion), channel_id=1, source_target_pairs={{0,1},{1,0},{2,3},{3,2},{4,5},{5,4},{6,7},{7,6},{8,9},{9,8},{10,11... | collective-permute-start | bytes 983048 | tf_op jit(solution)/shard_map/ppermute | solution.py:348
  2.3 16.1 %collective-permute-start.1 = (bf16[64,1024]{1,0:T(8,128)(2,1)S(1)}, bf16[64,1024]{1,0:T(8,128)(2,1)S(1)}, u32[]{:S(2)}, u32[]{:S(2)}) collective-permute-start(bf16[64,1024]{1,0:T(8,128)(2,1)S(1)} %bitcast_convert_fusion), channel_id=1, source_target_pairs={{0,16},{2,18},{4,20},{6,22},{8,24},{10,26},{12,28},{14,30},{16,0},... | collective-permute-start | bytes 393224 | tf_op jit(solution)/shard_map/ppermute | solution.py:328
  5.9 12.4 %collective-permute-start.2 = (bf16[64,1024]{1,0:T(8,128)(2,1)S(1)}, bf16[64,1024]{1,0:T(8,128)(2,1)S(1)}, u32[]{:S(2)}, u32[]{:S(2)}) collective-permute-start(bf16[64,1024]{1,0:T(8,128)(2,1)S(1)} %bitcast_convert_fusion), channel_id=1, source_target_pairs={{0,24},{2,26},{4,28},{6,30},{8,16},{10,18},{12,20},{14,22},{16,8},... | collective-permute-start | bytes 393224 | tf_op jit(solution)/shard_map/ppermute | solution.py:328
  7.3 11.1 %collective-permute-start.3 = (bf16[64,1024]{1,0:T(8,128)(2,1)S(1)}, bf16[64,1024]{1,0:T(8,128)(2,1)S(1)}, u32[]{:S(2)}, u32[]{:S(2)}) collective-permute-start(bf16[64,1024]{1,0:T(8,128)(2,1)S(1)} %bitcast_convert_fusion), channel_id=1, source_target_pairs={{0,8},{2,10},{4,12},{6,14},{8,0},{10,2},{12,4},{14,6},{16,24},{18,... | collective-permute-start | bytes 393224 | tf_op jit(solution)/shard_map/ppermute | solution.py:328
  7.5 0.7 %copy-start.3 = (f32[8,64]{1,0:T(8,128)S(1)}, f32[8,64]{1,0:T(8,128)}, u32[]{:S(2)}) copy-start(f32[8,64]{1,0:T(8,128)} %refs_5_.1) | copy-start | bytes 6148
  7.5 0.7 %copy-start.4 = (s32[64]{0:T(128)S(1)}, s32[64]{0:T(128)}, u32[]{:S(2)}) copy-start(s32[64]{0:T(128)} %columns_hbm.1) | copy-start | bytes 772
  7.5 0.7 %copy-start.5 = (f32[64]{0:T(128)S(1)}, f32[64]{0:T(128)}, u32[]{:S(2)}) copy-start(f32[64]{0:T(128)} %param.11) | copy-start | bytes 772
  7.5 0.7 %copy-start.6 = (f32[64]{0:T(128)S(1)}, f32[64]{0:T(128)}, u32[]{:S(2)}) copy-start(f32[64]{0:T(128)} %param.12) | copy-start | bytes 772
  13.2 13.4 %all-to-all-start = ((f32[32,8,128]{2,1,0:T(8,128)}), f32[32,8,128]{2,1,0:T(8,128)S(1)}, u32[]{:S(2)}, u32[]{:S(2)}) async-start(f32[32,8,128]{2,1,0:T(8,128)} %get-tuple-element.15), calls=%async_computation | async-start | bytes 262144 | tf_op jit(solution)/shard_map/all_to_all | solution.py:401
  18.5 12.4 %collective-permute-start.4 = (bf16[256,256]{1,0:T(8,128)(2,1)S(1)}, bf16[256,256]{1,0:T(8,128)(2,1)S(1)}, u32[]{:S(2)}, u32[]{:S(2)}) collective-permute-start(bf16[256,256]{1,0:T(8,128)(2,1)S(1)} %get-tuple-element.29), channel_id=1, source_target_pairs={{0,6},{2,4},{4,2},{6,0},{8,14},{10,12},{12,10},{14,8},{16,22},{18,... | collective-permute-start | bytes 393224 | tf_op jit(solution)/shard_map/ppermute | solution.py:328
  21.3 9.7 %collective-permute-start.5 = (bf16[256,256]{1,0:T(8,128)(2,1)S(1)}, bf16[256,256]{1,0:T(8,128)(2,1)S(1)}, u32[]{:S(2)}, u32[]{:S(2)}) collective-permute-start(bf16[256,256]{1,0:T(8,128)(2,1)S(1)} %get-tuple-element.28), channel_id=1, source_target_pairs={{0,4},{2,6},{4,0},{6,2},{8,12},{10,14},{12,8},{14,10},{16,20},{18,... | collective-permute-start | bytes 393224 | tf_op jit(solution)/shard_map/ppermute | solution.py:328
  21.8 9.2 %collective-permute-start.6 = (bf16[256,256]{1,0:T(8,128)(2,1)S(1)}, bf16[256,256]{1,0:T(8,128)(2,1)S(1)}, u32[]{:S(2)}, u32[]{:S(2)}) collective-permute-start(bf16[256,256]{1,0:T(8,128)(2,1)S(1)} %get-tuple-element.27), channel_id=1, source_target_pairs={{0,2},{2,0},{4,6},{6,4},{8,10},{10,8},{12,14},{14,12},{16,18},{18,... | collective-permute-start | bytes 393224 | tf_op jit(solution)/shard_map/ppermute | solution.py:328
  31.4 5.1 %collective-permute-start.7 = (bf16[64,256]{1,0:T(8,128)(2,1)S(1)}, bf16[64,256]{1,0:T(8,128)(2,1)S(1)}, u32[]{:S(2)}, u32[]{:S(2)}) collective-permute-start(bf16[64,256]{1,0:T(8,128)(2,1)S(1)} %get-tuple-element.21), channel_id=1, source_target_pairs={{0,6},{2,4},{4,2},{6,0},{8,14},{10,12},{12,10},{14,8},{16,22},{18,... | collective-permute-start | bytes 98312 | tf_op jit(solution)/shard_map/ppermute | solution.py:328
  32.3 4.3 %collective-permute-start.8 = (bf16[64,256]{1,0:T(8,128)(2,1)S(1)}, bf16[64,256]{1,0:T(8,128)(2,1)S(1)}, u32[]{:S(2)}, u32[]{:S(2)}) collective-permute-start(bf16[64,256]{1,0:T(8,128)(2,1)S(1)} %get-tuple-element.22), channel_id=1, source_target_pairs={{0,4},{2,6},{4,0},{6,2},{8,12},{10,14},{12,8},{14,10},{16,20},{18,... | collective-permute-start | bytes 98312 | tf_op jit(solution)/shard_map/ppermute | solution.py:328
  33.5 3.9 %collective-permute-start.9 = (bf16[64,256]{1,0:T(8,128)(2,1)S(1)}, bf16[64,256]{1,0:T(8,128)(2,1)S(1)}, u32[]{:S(2)}, u32[]{:S(2)}) collective-permute-start(bf16[64,256]{1,0:T(8,128)(2,1)S(1)} %get-tuple-element.23), channel_id=1, source_target_pairs={{0,2},{2,0},{4,6},{6,4},{8,10},{10,8},{12,14},{14,12},{16,18},{18,... | collective-permute-start | bytes 98312 | tf_op jit(solution)/shard_map/ppermute | solution.py:328

commit v8 on v7

--- a/solution.py
+++ b/solution.py
@@ -90,40 +90,62 @@
         copy.start()
     members, width = predicted_ref.shape[0], start_ref.shape[1]
     tiles = width // LANES
-    window = lines + 2 * STEPS
+    top = 0 if up_ref is None else STEPS
+    window = top + lines + STEPS
     lane = lax.broadcasted_iota(jnp.int32, (members, LANES), 1)
     first, last = lane == 0, lane == LANES - 1
 
     slab = lax.axis_index("sp")
-    above, below = slab > 0, slab < lax.axis_size("sp") - 1
-    sides = (
-        (0, up_ref, lines - STEPS, STEPS, above),
-        (STEPS, field_ref, 0, lines, None),
-        (STEPS + lines, down_ref, 0, STEPS, below),
-    )
     def by_rows(ref):
         return jnp.swapaxes(ref[0 : members * lines, :].reshape(members, lines, width), 0, 1)
 
-    turned = {id(ref): by_rows(ref) for ref in (field_ref, up_ref, down_ref)}
-    for row, ref, line, count, inside in sides:
-        coefficient = turned[id(ref)]
-        for step in range(count):
-            part = coefficient[line + step]
-            if inside is not None:
-                part = jnp.where(inside, part, 0.0)
-            half_exp[row + step] = 0.5 * jnp.exp(part)
-    for row, ref, line, count, inside in sides:
-        for step in range(count):
+    def turn(line):
+        return jnp.where(slab > 0, lines - 1 - line, line)
+
+    if top:
+        above, below = slab > 0, slab < lax.axis_size("sp") - 1
+        sides = (
+            (0, up_ref, lines - STEPS, STEPS, above),
+            (STEPS, field_ref, 0, lines, None),
+            (STEPS + lines, down_ref, 0, STEPS, below),
+        )
+        turned = {id(ref): by_rows(ref) for ref in (field_ref, up_ref, down_ref)}
+        for row, ref, line, count, inside in sides:
+            coefficient = turned[id(ref)]
+            for step in range(count):
+                part = coefficient[line + step]
+                if inside is not None:
+                    part = jnp.where(inside, part, 0.0)
+                half_exp[row + step] = 0.5 * jnp.exp(part)
+        for row, ref, line, count, inside in sides:
+            for step in range(count):
+                if inside is None:
+                    heat = start_ref[pl.ds(line + step, 1), :]
+                else:
+                    heat = jnp.where(inside, ref[pl.ds(members * lines + line + step, 1), :], 0.0)
+                warmth[row + step] = jnp.broadcast_to(heat, (members, width))
             if inside is None:
-                heat = start_ref[pl.ds(line + step, 1), :]
+                supply[pl.ds(row, count), :] = source_ref[...]
             else:
-                heat = jnp.where(inside, ref[pl.ds(members * lines + line + step, 1), :], 0.0)
-            warmth[row + step] = jnp.broadcast_to(heat, (members, width))
-        if inside is None:
-            supply[pl.ds(row, count), :] = source_ref[...]
-        else:
-            base = (members + 1) * lines + line
-            supply[pl.ds(row, count), :] = ref[pl.ds(base, count), :]
+                base = (members + 1) * lines + line
+                supply[pl.ds(row, count), :] = ref[pl.ds(base, count), :]
+    else:
+        own, other = by_rows(field_ref), by_rows(down_ref)
+        for line in range(lines):
+            half_exp[turn(line)] = 0.5 * jnp.exp(own[line])
+        for step in range(STEPS):
+            part = jnp.where(slab > 0, other[lines - 1 - step], other[step])
+            half_exp[lines + step] = 0.5 * jnp.exp(part)
+        for row in range(lines + STEPS):
+            if row < lines:
+                heat = start_ref[pl.ds(turn(row), 1), :]
+                source = source_ref[pl.ds(turn(row), 1), :]
+            else:
+                line = members * lines + turn(row - lines)
+                heat = down_ref[pl.ds(line, 1), :]
+                source = down_ref[pl.ds(line + lines, 1), :]
+            warmth[row] = jnp.broadcast_to(heat, (members, width))
+            supply[pl.ds(row, 1), :] = source
 
     def cut(value):
         return [value[:, k * LANES : (k + 1) * LANES] for k in range(tiles)]
@@ -136,9 +158,12 @@
     zero = jnp.zeros((members, LANES), jnp.float32)
 
     for step in range(STEPS):
-        low, high = step + 1, window - 1 - step
-        t_up = cut(warmth[low - 1])
-        c_up = conductivity(low - 1, t_up)
+        low, high = step + 1 if top else 0, window - 1 - step
+        if top:
+            t_up = cut(warmth[low - 1])
+            c_up = conductivity(low - 1, t_up)
+        else:
+            t_up, c_up = [zero] * tiles, [half_one] * tiles
         t_here = cut(warmth[low])
         c_here = conductivity(low, t_here)
         flow_up = [(a + b) * (y - x) for a, b, x, y in zip(c_up, c_here, t_up, t_here)]
@@ -156,20 +181,21 @@
                 c_right = jnp.where(last, c_roll[k + 1], c_roll[k])
                 right.append((c[k] + c_right) * (t_right - t[k]))
             back = [pltpu.roll(x, 1, 1) for x in right]
-            outside = jnp.logical_or(
-                jnp.logical_and(row < STEPS, jnp.logical_not(above)),
-                jnp.logical_and(row >= STEPS + lines, jnp.logical_not(below)),
-            )
-            keep = jnp.where(outside, 0.0, 1.0)
+            keep = 1.0
+            if top:
+                outside = jnp.logical_or(
+                    jnp.logical_and(row < STEPS, jnp.logical_not(above)),
+                    jnp.logical_and(row >= STEPS + lines, jnp.logical_not(below)),
+                )
+                keep = jnp.where(outside, 0.0, 1.0)
             source = supply[pl.ds(row, 1), :]
             for k in range(tiles):
                 edge = (c[0] + 0.5) * t[0] if k == 0 else back[k - 1]
                 left = jnp.where(first, edge, back[k])
                 inflow = (down[k] - up[k]) + (right[k] - left)
                 heat = source[:, k * LANES : (k + 1) * LANES]
-                warmth[row, :, k * LANES : (k + 1) * LANES] = keep * (
-                    t[k] + time_step * (inflow + heat)
-                )
+                fresh = t[k] + time_step * (inflow + heat)
+                warmth[row, :, k * LANES : (k + 1) * LANES] = keep * fresh if top else fresh
             return t_next, c_next, down
 
         lax.fori_loop(low, high, one_row, (t_here, c_here, flow_up), unroll=True)
@@ -182,9 +208,11 @@
     for probe in range(probes):
         line = probe * lines // probes
         column = columns_ref[probe] - line * width
-        tile = column // LANES
-        shift = lax.rem(probe - lax.rem(column, LANES) + LANES, LANES)
-        values = warmth[STEPS + line, :, pl.ds(pl.multiple_of(tile * LANES, LANES), LANES)]
+        offset = jnp.bitwise_and(column, LANES - 1)
+        shift = jnp.bitwise_and(probe - offset, LANES - 1)
+        start = pl.multiple_of(column - offset, LANES)
+        place = STEPS + line if top else turn(line)
+        values = warmth[place, :, pl.ds(start, LANES)]
         moved = pltpu.roll(values, shift, 1)
         picked[probe % 4] = jnp.where(lane_probe == probe, moved, picked[probe % 4])
     total = (picked[0] + picked[1]) + (picked[2] + picked[3])
@@ -358,7 +386,8 @@
 
     def kernel(columns_hbm, field_ref, *refs):
         neighbours, rest = refs[: len(beside)], refs[len(beside) :]
-        conduct_kernel(columns_hbm, field_ref, neighbours[0], neighbours[-1], *rest)
+        above = neighbours[0] if len(beside) == 2 else None
+        conduct_kernel(columns_hbm, field_ref, above, neighbours[-1], *rest)
 
     predicted, payload = pl.pallas_call(
         kernel,

time: 38.4 us -> 37.6 us (0.979)
  Pallas kernels: 10.5 us -> 9.72 us
    pallas_call x1, Pallas kernels: 4.94 us -> 4.17 us  [body(): pl.pallas_call(kernel, out_shape=(jax.ShapeDtypeStruct((members, probes),...]
  transfers between devices with their start and end apart: 11 -> 11, of which waited for: 4 -> 4; matrix products, arithmetic and copies ran while one was open for 0% -> 0% of each run, Pallas kernels for 24% -> 23%
where the time goes in v8:
time: 37.6 us; the launch traced here: 37.4 us
  starting transfers between devices  18 us (48%)
  Pallas kernels  9.72 us (26%)
  waiting for transfers between devices  6.96 us (19%)
  other arithmetic  1.03 us (3%)
  local copies, waits for them, and re-layouts  0.82 us (2%)
  between operations  0.82 us (2%)
    ppermute x9, starting transfers between devices, across(): return lax.ppermute(value, 'mem', [(i, i ^ bit) for i in range(owners)])  12.3 us
    all_to_all x1, starting transfers between devices, body(): everyone = lax.all_to_all(payload, ('mem', 'sp'), 0, 0, tiled=True)  5.18 us
    all_to_all x1, waiting for transfers between devices, body(): everyone = lax.all_to_all(payload, ('mem', 'sp'), 0, 0, tiled=True)  4.48 us
    pallas_call x1, Pallas kernels, body(): pl.pallas_call(lambda *refs: solve_kernel(norm_scale, slabs, offsets, tur...  4.4 us
    pallas_call x1, Pallas kernels, body(): pl.pallas_call(kernel, out_shape=(jax.ShapeDtypeStruct((members, probes),...  4.17 us
    ppermute x9, waiting for transfers between devices, across(): return lax.ppermute(value, 'mem', [(i, i ^ bit) for i in range(owners)])  2.48 us
    convert_element_type x1, other arithmetic, body(): field_round = field_flat.astype(jnp.bfloat16)  1.01 us
  transfers between devices with their start and end apart: 11, of which 4 were waited for; matrix products, arithmetic and copies ran while one was open for 0% of the time, Pallas kernels for 23%

profile of v8, /device:TPU:0, one launch (start us, length us, event | category | flops | bytes accessed | tf_op | source)
XLA Modules:
  0.0 37.4 jit_solution(12112228659558398368)
XLA Ops:
  0.7 1.0 %bitcast_convert_fusion = bf16[64,1024]{1,0:T(8,128)(2,1)S(1)} fusion(f32[8,8,1024]{2,1,0:T(8,128)} %param.7), kind=kLoop, calls=%fused_computation.9 | loop fusion | flops 65536 | bytes 393216 | tf_op jit(solution)/shard_map/convert_element_type | solution.py:359
  1.7 0.5 %collective-permute-start = (f32[80,1024]{1,0:T(8,128)S(1)}, f32[80,1024]{1,0:T(8,128)S(1)}, u32[]{:S(2)}, u32[]{:S(2)}) collective-permute-start(f32[80,1024]{1,0:T(8,128)S(1)} %pad_maximum_fusion), channel_id=1, source_target_pairs={{0,1},{1,0},{2,3},{3,2},{4,5},{5,4},{6,7},{7,6},{8,9},{9,8},{10,11... | collective-permute-start | bytes 983048 | tf_op jit(solution)/shard_map/ppermute | solution.py:376
  2.3 3.7 %collective-permute-start.1 = (bf16[64,1024]{1,0:T(8,128)(2,1)S(1)}, bf16[64,1024]{1,0:T(8,128)(2,1)S(1)}, u32[]{:S(2)}, u32[]{:S(2)}) collective-permute-start(bf16[64,1024]{1,0:T(8,128)(2,1)S(1)} %bitcast_convert_fusion), channel_id=1, source_target_pairs={{0,16},{2,18},{4,20},{6,22},{8,24},{10,26},{12,28},{14,30},{16,0},... | collective-permute-start | bytes 393224 | tf_op jit(solution)/shard_map/ppermute | solution.py:356
  5.9 1.3 %collective-permute-start.2 = (bf16[64,1024]{1,0:T(8,128)(2,1)S(1)}, bf16[64,1024]{1,0:T(8,128)(2,1)S(1)}, u32[]{:S(2)}, u32[]{:S(2)}) collective-permute-start(bf16[64,1024]{1,0:T(8,128)(2,1)S(1)} %bitcast_convert_fusion), channel_id=1, source_target_pairs={{0,24},{2,26},{4,28},{6,30},{8,16},{10,18},{12,20},{14,22},{16,8},... | collective-permute-start | bytes 393224 | tf_op jit(solution)/shard_map/ppermute | solution.py:356
  7.3 0.2 collective-permute-start.3
  7.5 0.0 copy-start.6
  7.5 0.7 %copy-done.3 = f32[8,64]{1,0:T(8,128)S(1)} copy-done((f32[8,64]{1,0:T(8,128)S(1)}, f32[8,64]{1,0:T(8,128)}, u32[]{:S(2)}) %copy-start.3) | copy-done | bytes 2072
  8.2 0.0 copy-done.6
  8.2 4.2 %conduct.1 = (f32[8,64]{1,0:T(8,128)}, f32[32,8,128]{2,1,0:T(8,128)}) custom-call(s32[64]{0:T(128)S(1)} %copy-done.4, f32[64,1024]{1,0:T(8,128)S(1)} %bitcast.6, f32[80,1024]{1,0:T(8,128)S(1)} %collective-permute-done.refs_0_, f32[8,1024]{1,0:T(8,128)S(1)} %copy-done.2, f32[8,1024]{1,0:T(8,128)S(1)} %copy-done.1, f32[1,64]{1,0:T(1,128)S(1)} %bitcast.8, ...), custom_call_target="tpu_custom_call" | custom-call | flops 15728640 | bytes 786432 | tf_op jit(solution)/shard_map/conduct/pallas_call | solution.py:392
  12.4 5.2 %all-to-all-start = ((f32[32,8,128]{2,1,0:T(8,128)}), f32[32,8,128]{2,1,0:T(8,128)S(1)}, u32[]{:S(2)}, u32[]{:S(2)}) async-start(f32[32,8,128]{2,1,0:T(8,128)} %get-tuple-element.15), calls=%async_computation | async-start | bytes 262144 | tf_op jit(solution)/shard_map/all_to_all | solution.py:430
  17.7 0.1 constant_dynamic-slice_fusion
  17.8 2.7 %collective-permute-start.4 = (bf16[256,256]{1,0:T(8,128)(2,1)S(1)}, bf16[256,256]{1,0:T(8,128)(2,1)S(1)}, u32[]{:S(2)}, u32[]{:S(2)}) collective-permute-start(bf16[256,256]{1,0:T(8,128)(2,1)S(1)} %get-tuple-element.29), channel_id=1, source_target_pairs={{0,6},{2,4},{4,2},{6,0},{8,14},{10,12},{12,10},{14,8},{16,22},{18,... | collective-permute-start | bytes 393224 | tf_op jit(solution)/shard_map/ppermute | solution.py:356
  20.5 0.6 %collective-permute-start.5 = (bf16[256,256]{1,0:T(8,128)(2,1)S(1)}, bf16[256,256]{1,0:T(8,128)(2,1)S(1)}, u32[]{:S(2)}, u32[]{:S(2)}) collective-permute-start(bf16[256,256]{1,0:T(8,128)(2,1)S(1)} %get-tuple-element.28), channel_id=1, source_target_pairs={{0,4},{2,6},{4,0},{6,2},{8,12},{10,14},{12,8},{14,10},{16,20},{18,... | collective-permute-start | bytes 393224 | tf_op jit(solution)/shard_map/ppermute | solution.py:356
  21.1 0.3 collective-permute-start.6
  21.3 4.5 %all-to-all-done.refs_0_ = f32[32,8,128]{2,1,0:T(8,128)S(1)} async-done(((f32[32,8,128]{2,1,0:T(8,128)}), f32[32,8,128]{2,1,0:T(8,128)S(1)}, u32[]{:S(2)}, u32[]{:S(2)}) %all-to-all-start) | async-done | bytes 131104 | tf_op jit(solution)/shard_map/all_to_all | solution.py:430
  25.8 4.4 %solve.1.refs_0_ = bf16[32,128]{1,0:T(8,128)(2,1)S(1)} custom-call(f32[32,8,128]{2,1,0:T(8,128)S(1)} %all-to-all-done.refs_0_), custom_call_target="tpu_custom_call" | custom-call | flops 4194304 | bytes 131072 | tf_op jit(solution)/shard_map/solve/pallas_call | solution.py:439
  30.2 0.4 %apply.1 = (f32[64,256]{1,0:T(8,128)S(1)}, bf16[64,256]{1,0:T(8,128)(2,1)S(1)}, bf16[64,256]{1,0:T(8,128)(2,1)S(1)}, bf16[64,256]{1,0:T(8,128)(2,1)S(1)}) custom-call(bf16[32,128]{1,0:T(8,128)(2,1)S(1)} %solve.1.refs_0_, bf16[256,256]{1,0:T(8,128)(2,1)S(1)} %collective-permute-done.4.refs_1_, bf16[256,256]{1,0:T(8,128)(2,1)S(1)} %collective-permute-done.5.refs_2_, ...), custom_call_target="tpu_custom_call" | custom-call | flops 134217728 | bytes 524288 | tf_op jit(solution)/shard_map/apply/pallas_call | solution.py:468
  30.6 0.9 %collective-permute-start.7 = (bf16[64,256]{1,0:T(8,128)(2,1)S(1)}, bf16[64,256]{1,0:T(8,128)(2,1)S(1)}, u32[]{:S(2)}, u32[]{:S(2)}) collective-permute-start(bf16[64,256]{1,0:T(8,128)(2,1)S(1)} %get-tuple-element.21), channel_id=1, source_target_pairs={{0,6},{2,4},{4,2},{6,0},{8,14},{10,12},{12,10},{14,8},{16,22},{18,... | collective-permute-start | bytes 98312 | tf_op jit(solution)/shard_map/ppermute | solution.py:356
  31.6 1.2 %collective-permute-start.8 = (bf16[64,256]{1,0:T(8,128)(2,1)S(1)}, bf16[64,256]{1,0:T(8,128)(2,1)S(1)}, u32[]{:S(2)}, u32[]{:S(2)}) collective-permute-start(bf16[64,256]{1,0:T(8,128)(2,1)S(1)} %get-tuple-element.22), channel_id=1, source_target_pairs={{0,4},{2,6},{4,0},{6,2},{8,12},{10,14},{12,8},{14,10},{16,20},{18,... | collective-permute-start | bytes 98312 | tf_op jit(solution)/shard_map/ppermute | solution.py:356
  32.7 1.4 %collective-permute-start.9 = (bf16[64,256]{1,0:T(8,128)(2,1)S(1)}, bf16[64,256]{1,0:T(8,128)(2,1)S(1)}, u32[]{:S(2)}, u32[]{:S(2)}) collective-permute-start(bf16[64,256]{1,0:T(8,128)(2,1)S(1)} %get-tuple-element.23), channel_id=1, source_target_pairs={{0,2},{2,0},{4,6},{6,4},{8,10},{10,8},{12,14},{14,12},{16,18},{18,... | collective-permute-start | bytes 98312 | tf_op jit(solution)/shard_map/ppermute | solution.py:356
  34.2 1.6 %collective-permute-done.7.refs_0_ = bf16[64,256]{1,0:T(8,128)(2,1)S(1)} collective-permute-done((bf16[64,256]{1,0:T(8,128)(2,1)S(1)}, bf16[64,256]{1,0:T(8,128)(2,1)S(1)}, u32[]{:S(2)}, u32[]{:S(2)}) %collective-permute-start.7) | collective-permute-done | bytes 32800 | tf_op jit(solution)/shard_map/ppermute | solution.py:356
  35.8 0.1 collective-permute-done.8.refs_1_
  35.8 0.8 %collective-permute-done.9.refs_2_ = bf16[64,256]{1,0:T(8,128)(2,1)S(1)} collective-permute-done((bf16[64,256]{1,0:T(8,128)(2,1)S(1)}, bf16[64,256]{1,0:T(8,128)(2,1)S(1)}, u32[]{:S(2)}, u32[]{:S(2)}) %collective-permute-start.9) | collective-permute-done | bytes 32800 | tf_op jit(solution)/shard_map/ppermute | solution.py:356
  36.7 0.7 %merge.1 = f32[64,1024]{1,0:T(8,128)} custom-call(f32[64,1024]{1,0:T(8,128)S(1)} %bitcast.7, bf16[64,256]{1,0:T(8,128)(2,1)S(1)} %collective-permute-done.7.refs_0_, bf16[64,256]{1,0:T(8,128)(2,1)S(1)} %collective-permute-done.8.refs_1_, bf16[64,256]{1,0:T(8,128)(2,1)S(1)} %collective-permute-done.9.refs_2_, f32[64,256]{1,0:T(8,128)S(1)} %get-tuple-element.24.refs_3_), custom_call_target="tpu_custom_call" | custom-call | tf_op jit(solution)/shard_map/merge/pallas_call | solution.py:487
  (23 shorter events, 0.1 us)
Async XLA Ops:
  0.6 1.0 %copy-start = (f32[8,8,1024]{2,1,0:T(8,128)S(1)}, f32[8,8,1024]{2,1,0:T(8,128)}, u32[]{:S(2)}) copy-start(f32[8,8,1024]{2,1,0:T(8,128)} %param.7) | copy-start | bytes 786436
  0.6 1.0 %copy-start.2 = (f32[8,1024]{1,0:T(8,128)S(1)}, f32[8,1024]{1,0:T(8,128)}, u32[]{:S(2)}) copy-start(f32[8,1024]{1,0:T(8,128)} %refs_1_.1) | copy-start | bytes 98308
  0.6 1.0 %copy-start.1 = (f32[8,1024]{1,0:T(8,128)S(1)}, f32[8,1024]{1,0:T(8,128)}, u32[]{:S(2)}) copy-start(f32[8,1024]{1,0:T(8,128)} %refs_2_.1) | copy-start | bytes 98308
  1.7 5.8 %collective-permute-start = (f32[80,1024]{1,0:T(8,128)S(1)}, f32[80,1024]{1,0:T(8,128)S(1)}, u32[]{:S(2)}, u32[]{:S(2)}) collective-permute-start(f32[80,1024]{1,0:T(8,128)S(1)} %pad_maximum_fusion), channel_id=1, source_target_pairs={{0,1},{1,0},{2,3},{3,2},{4,5},{5,4},{6,7},{7,6},{8,9},{9,8},{10,11... | collective-permute-start | bytes 983048 | tf_op jit(solution)/shard_map/ppermute | solution.py:376
  2.3 15.3 %collective-permute-start.1 = (bf16[64,1024]{1,0:T(8,128)(2,1)S(1)}, bf16[64,1024]{1,0:T(8,128)(2,1)S(1)}, u32[]{:S(2)}, u32[]{:S(2)}) collective-permute-start(bf16[64,1024]{1,0:T(8,128)(2,1)S(1)} %bitcast_convert_fusion), channel_id=1, source_target_pairs={{0,16},{2,18},{4,20},{6,22},{8,24},{10,26},{12,28},{14,30},{16,0},... | collective-permute-start | bytes 393224 | tf_op jit(solution)/shard_map/ppermute | solution.py:356
  5.9 11.7 %collective-permute-start.2 = (bf16[64,1024]{1,0:T(8,128)(2,1)S(1)}, bf16[64,1024]{1,0:T(8,128)(2,1)S(1)}, u32[]{:S(2)}, u32[]{:S(2)}) collective-permute-start(bf16[64,1024]{1,0:T(8,128)(2,1)S(1)} %bitcast_convert_fusion), channel_id=1, source_target_pairs={{0,24},{2,26},{4,28},{6,30},{8,16},{10,18},{12,20},{14,22},{16,8},... | collective-permute-start | bytes 393224 | tf_op jit(solution)/shard_map/ppermute | solution.py:356
  7.3 10.3 %collective-permute-start.3 = (bf16[64,1024]{1,0:T(8,128)(2,1)S(1)}, bf16[64,1024]{1,0:T(8,128)(2,1)S(1)}, u32[]{:S(2)}, u32[]{:S(2)}) collective-permute-start(bf16[64,1024]{1,0:T(8,128)(2,1)S(1)} %bitcast_convert_fusion), channel_id=1, source_target_pairs={{0,8},{2,10},{4,12},{6,14},{8,0},{10,2},{12,4},{14,6},{16,24},{18,... | collective-permute-start | bytes 393224 | tf_op jit(solution)/shard_map/ppermute | solution.py:356
  7.5 0.7 %copy-start.3 = (f32[8,64]{1,0:T(8,128)S(1)}, f32[8,64]{1,0:T(8,128)}, u32[]{:S(2)}) copy-start(f32[8,64]{1,0:T(8,128)} %refs_5_.1) | copy-start | bytes 6148
  7.5 0.7 %copy-start.4 = (s32[64]{0:T(128)S(1)}, s32[64]{0:T(128)}, u32[]{:S(2)}) copy-start(s32[64]{0:T(128)} %columns_hbm.1) | copy-start | bytes 772
  7.5 0.7 %copy-start.5 = (f32[64]{0:T(128)S(1)}, f32[64]{0:T(128)}, u32[]{:S(2)}) copy-start(f32[64]{0:T(128)} %param.11) | copy-start | bytes 772
  7.5 0.7 %copy-start.6 = (f32[64]{0:T(128)S(1)}, f32[64]{0:T(128)}, u32[]{:S(2)}) copy-start(f32[64]{0:T(128)} %param.12) | copy-start | bytes 772
  12.4 13.4 %all-to-all-start = ((f32[32,8,128]{2,1,0:T(8,128)}), f32[32,8,128]{2,1,0:T(8,128)S(1)}, u32[]{:S(2)}, u32[]{:S(2)}) async-start(f32[32,8,128]{2,1,0:T(8,128)} %get-tuple-element.15), calls=%async_computation | async-start | bytes 262144 | tf_op jit(solution)/shard_map/all_to_all | solution.py:430
  17.8 12.4 %collective-permute-start.4 = (bf16[256,256]{1,0:T(8,128)(2,1)S(1)}, bf16[256,256]{1,0:T(8,128)(2,1)S(1)}, u32[]{:S(2)}, u32[]{:S(2)}) collective-permute-start(bf16[256,256]{1,0:T(8,128)(2,1)S(1)} %get-tuple-element.29), channel_id=1, source_target_pairs={{0,6},{2,4},{4,2},{6,0},{8,14},{10,12},{12,10},{14,8},{16,22},{18,... | collective-permute-start | bytes 393224 | tf_op jit(solution)/shard_map/ppermute | solution.py:356
  20.5 9.7 %collective-permute-start.5 = (bf16[256,256]{1,0:T(8,128)(2,1)S(1)}, bf16[256,256]{1,0:T(8,128)(2,1)S(1)}, u32[]{:S(2)}, u32[]{:S(2)}) collective-permute-start(bf16[256,256]{1,0:T(8,128)(2,1)S(1)} %get-tuple-element.28), channel_id=1, source_target_pairs={{0,4},{2,6},{4,0},{6,2},{8,12},{10,14},{12,8},{14,10},{16,20},{18,... | collective-permute-start | bytes 393224 | tf_op jit(solution)/shard_map/ppermute | solution.py:356
  21.1 9.2 %collective-permute-start.6 = (bf16[256,256]{1,0:T(8,128)(2,1)S(1)}, bf16[256,256]{1,0:T(8,128)(2,1)S(1)}, u32[]{:S(2)}, u32[]{:S(2)}) collective-permute-start(bf16[256,256]{1,0:T(8,128)(2,1)S(1)} %get-tuple-element.27), channel_id=1, source_target_pairs={{0,2},{2,0},{4,6},{6,4},{8,10},{10,8},{12,14},{14,12},{16,18},{18,... | collective-permute-start | bytes 393224 | tf_op jit(solution)/shard_map/ppermute | solution.py:356
  30.6 5.1 %collective-permute-start.7 = (bf16[64,256]{1,0:T(8,128)(2,1)S(1)}, bf16[64,256]{1,0:T(8,128)(2,1)S(1)}, u32[]{:S(2)}, u32[]{:S(2)}) collective-permute-start(bf16[64,256]{1,0:T(8,128)(2,1)S(1)} %get-tuple-element.21), channel_id=1, source_target_pairs={{0,6},{2,4},{4,2},{6,0},{8,14},{10,12},{12,10},{14,8},{16,22},{18,... | collective-permute-start | bytes 98312 | tf_op jit(solution)/shard_map/ppermute | solution.py:356
  31.6 4.3 %collective-permute-start.8 = (bf16[64,256]{1,0:T(8,128)(2,1)S(1)}, bf16[64,256]{1,0:T(8,128)(2,1)S(1)}, u32[]{:S(2)}, u32[]{:S(2)}) collective-permute-start(bf16[64,256]{1,0:T(8,128)(2,1)S(1)} %get-tuple-element.22), channel_id=1, source_target_pairs={{0,4},{2,6},{4,0},{6,2},{8,12},{10,14},{12,8},{14,10},{16,20},{18,... | collective-permute-start | bytes 98312 | tf_op jit(solution)/shard_map/ppermute | solution.py:356
  32.7 3.9 %collective-permute-start.9 = (bf16[64,256]{1,0:T(8,128)(2,1)S(1)}, bf16[64,256]{1,0:T(8,128)(2,1)S(1)}, u32[]{:S(2)}, u32[]{:S(2)}) collective-permute-start(bf16[64,256]{1,0:T(8,128)(2,1)S(1)} %get-tuple-element.23), channel_id=1, source_target_pairs={{0,2},{2,0},{4,6},{6,4},{8,10},{10,8},{12,14},{14,12},{16,18},{18,... | collective-permute-start | bytes 98312 | tf_op jit(solution)/shard_map/ppermute | solution.py:356

commit v9 on v8

--- a/solution.py
+++ b/solution.py
@@ -229,25 +229,26 @@
     order = len(offsets) * members
     mine = lax.axis_index("mem")
     dims = (((1,), (1,)), ((), ()))
-    gram, cross = None, None
+    normals, misfits = [], []
     for slab in range(slabs):
         blocks = [
             payload_ref[jnp.bitwise_xor(mine, offset) * slabs + slab] for offset in offsets
         ]
-        normal = jnp.concatenate([block[:, :probes] for block in blocks], axis=0)
-        center = jnp.sum(normal, axis=0, keepdims=True) * (1.0 / order)
-        scaled = (center - normal) * norm_scale
-        misfit = jnp.concatenate(
-            [blocks[offsets.index(turn)][:, probes:] for turn in turns], axis=0
-        )
-        one = lax.dot_general(
-            scaled, scaled, dims, precision=lax.Precision.HIGHEST, preferred_element_type=jnp.float32
-        )
-        two = lax.dot_general(
-            misfit, scaled, dims, precision=lax.Precision.HIGHEST, preferred_element_type=jnp.float32
-        )
-        gram = one if gram is None else gram + one
-        cross = two if cross is None else cross + two
+        normals.append(jnp.concatenate([block[:, :probes] for block in blocks], axis=0))
+        misfits += [
+            jnp.concatenate([blocks[offsets.index(turn)][:, probes:] for turn in turns], axis=0)
+        ]
+    normal, misfit = jnp.concatenate(normals, axis=1), jnp.concatenate(misfits, axis=1)
+    center = jnp.sum(normal, axis=0, keepdims=True) * (1.0 / order)
+    scaled = (center - normal) * norm_scale
+    both = lax.dot_general(
+        jnp.concatenate([scaled, misfit], axis=0),
+        scaled,
+        dims,
+        precision=lax.Precision.HIGHEST,
+        preferred_element_type=jnp.float32,
+    )
+    gram, cross = both[:order], both[order:]
     row_id = lax.broadcasted_iota(jnp.int32, (ROWS, order), 0)
     lane_id = lax.broadcasted_iota(jnp.int32, (ROWS, order), 1)
     blocks = order // ROWS

time: 37.6 us -> 37.4 us (level)
  transfers between devices with their start and end apart: 11 -> 11, of which waited for: 4 -> 4; matrix products, arithmetic and copies ran while one was open for 0% -> 0% of each run, Pallas kernels for 23% -> 22%
where the time goes in v9:
time: 37.4 us; the launch traced here: 37.2 us
  starting transfers between devices  18 us (48%)
  Pallas kernels  9.49 us (25%)
  waiting for transfers between devices  6.96 us (19%)
  other arithmetic  1.03 us (3%)
  local copies, waits for them, and re-layouts  0.82 us (2%)
  between operations  0.82 us (2%)
    ppermute x9, starting transfers between devices, across(): return lax.ppermute(value, 'mem', [(i, i ^ bit) for i in range(owners)])  12.3 us
    all_to_all x1, starting transfers between devices, body(): everyone = lax.all_to_all(payload, ('mem', 'sp'), 0, 0, tiled=True)  5.18 us
    all_to_all x1, waiting for transfers between devices, body(): everyone = lax.all_to_all(payload, ('mem', 'sp'), 0, 0, tiled=True)  4.48 us
    pallas_call x1, Pallas kernels, body(): pl.pallas_call(lambda *refs: solve_kernel(norm_scale, slabs, offsets, tur...  4.17 us
    pallas_call x1, Pallas kernels, body(): pl.pallas_call(kernel, out_shape=(jax.ShapeDtypeStruct((members, probes),...  4.17 us
    ppermute x9, waiting for transfers between devices, across(): return lax.ppermute(value, 'mem', [(i, i ^ bit) for i in range(owners)])  2.48 us
    convert_element_type x1, other arithmetic, body(): field_round = field_flat.astype(jnp.bfloat16)  1.01 us
  transfers between devices with their start and end apart: 11, of which 4 were waited for; matrix products, arithmetic and copies ran while one was open for 0% of the time, Pallas kernels for 22%

profile of v9, /device:TPU:0, one launch (start us, length us, event | category | flops | bytes accessed | tf_op | source)
XLA Modules:
  0.0 37.2 jit_solution(14410942761040721375)
XLA Ops:
  0.7 1.0 %bitcast_convert_fusion = bf16[64,1024]{1,0:T(8,128)(2,1)S(1)} fusion(f32[8,8,1024]{2,1,0:T(8,128)} %param.7), kind=kLoop, calls=%fused_computation.9 | loop fusion | flops 65536 | bytes 393216 | tf_op jit(solution)/shard_map/convert_element_type | solution.py:360
  1.7 0.5 %collective-permute-start = (f32[80,1024]{1,0:T(8,128)S(1)}, f32[80,1024]{1,0:T(8,128)S(1)}, u32[]{:S(2)}, u32[]{:S(2)}) collective-permute-start(f32[80,1024]{1,0:T(8,128)S(1)} %pad_maximum_fusion), channel_id=1, source_target_pairs={{0,1},{1,0},{2,3},{3,2},{4,5},{5,4},{6,7},{7,6},{8,9},{9,8},{10,11... | collective-permute-start | bytes 983048 | tf_op jit(solution)/shard_map/ppermute | solution.py:377
  2.3 3.7 %collective-permute-start.1 = (bf16[64,1024]{1,0:T(8,128)(2,1)S(1)}, bf16[64,1024]{1,0:T(8,128)(2,1)S(1)}, u32[]{:S(2)}, u32[]{:S(2)}) collective-permute-start(bf16[64,1024]{1,0:T(8,128)(2,1)S(1)} %bitcast_convert_fusion), channel_id=1, source_target_pairs={{0,16},{2,18},{4,20},{6,22},{8,24},{10,26},{12,28},{14,30},{16,0},... | collective-permute-start | bytes 393224 | tf_op jit(solution)/shard_map/ppermute | solution.py:357
  5.9 1.3 %collective-permute-start.2 = (bf16[64,1024]{1,0:T(8,128)(2,1)S(1)}, bf16[64,1024]{1,0:T(8,128)(2,1)S(1)}, u32[]{:S(2)}, u32[]{:S(2)}) collective-permute-start(bf16[64,1024]{1,0:T(8,128)(2,1)S(1)} %bitcast_convert_fusion), channel_id=1, source_target_pairs={{0,24},{2,26},{4,28},{6,30},{8,16},{10,18},{12,20},{14,22},{16,8},... | collective-permute-start | bytes 393224 | tf_op jit(solution)/shard_map/ppermute | solution.py:357
  7.3 0.2 collective-permute-start.3
  7.5 0.0 copy-start.6
  7.5 0.7 %copy-done.3 = f32[8,64]{1,0:T(8,128)S(1)} copy-done((f32[8,64]{1,0:T(8,128)S(1)}, f32[8,64]{1,0:T(8,128)}, u32[]{:S(2)}) %copy-start.3) | copy-done | bytes 2072
  8.2 0.0 copy-done.6
  8.2 4.2 %conduct.1 = (f32[8,64]{1,0:T(8,128)}, f32[32,8,128]{2,1,0:T(8,128)}) custom-call(s32[64]{0:T(128)S(1)} %copy-done.4, f32[64,1024]{1,0:T(8,128)S(1)} %bitcast.6, f32[80,1024]{1,0:T(8,128)S(1)} %collective-permute-done.refs_0_, f32[8,1024]{1,0:T(8,128)S(1)} %copy-done.2, f32[8,1024]{1,0:T(8,128)S(1)} %copy-done.1, f32[1,64]{1,0:T(1,128)S(1)} %bitcast.8, ...), custom_call_target="tpu_custom_call" | custom-call | flops 15728640 | bytes 786432 | tf_op jit(solution)/shard_map/conduct/pallas_call | solution.py:393
  12.4 5.2 %all-to-all-start = ((f32[32,8,128]{2,1,0:T(8,128)}), f32[32,8,128]{2,1,0:T(8,128)S(1)}, u32[]{:S(2)}, u32[]{:S(2)}) async-start(f32[32,8,128]{2,1,0:T(8,128)} %get-tuple-element.15), calls=%async_computation | async-start | bytes 262144 | tf_op jit(solution)/shard_map/all_to_all | solution.py:431
  17.7 0.1 constant_dynamic-slice_fusion
  17.8 2.7 %collective-permute-start.4 = (bf16[256,256]{1,0:T(8,128)(2,1)S(1)}, bf16[256,256]{1,0:T(8,128)(2,1)S(1)}, u32[]{:S(2)}, u32[]{:S(2)}) collective-permute-start(bf16[256,256]{1,0:T(8,128)(2,1)S(1)} %get-tuple-element.29), channel_id=1, source_target_pairs={{0,6},{2,4},{4,2},{6,0},{8,14},{10,12},{12,10},{14,8},{16,22},{18,... | collective-permute-start | bytes 393224 | tf_op jit(solution)/shard_map/ppermute | solution.py:357
  20.5 0.6 %collective-permute-start.5 = (bf16[256,256]{1,0:T(8,128)(2,1)S(1)}, bf16[256,256]{1,0:T(8,128)(2,1)S(1)}, u32[]{:S(2)}, u32[]{:S(2)}) collective-permute-start(bf16[256,256]{1,0:T(8,128)(2,1)S(1)} %get-tuple-element.28), channel_id=1, source_target_pairs={{0,4},{2,6},{4,0},{6,2},{8,12},{10,14},{12,8},{14,10},{16,20},{18,... | collective-permute-start | bytes 393224 | tf_op jit(solution)/shard_map/ppermute | solution.py:357
  21.1 0.3 collective-permute-start.6
  21.3 4.5 %all-to-all-done.refs_0_ = f32[32,8,128]{2,1,0:T(8,128)S(1)} async-done(((f32[32,8,128]{2,1,0:T(8,128)}), f32[32,8,128]{2,1,0:T(8,128)S(1)}, u32[]{:S(2)}, u32[]{:S(2)}) %all-to-all-start) | async-done | bytes 131104 | tf_op jit(solution)/shard_map/all_to_all | solution.py:431
  25.8 4.2 %solve.1.refs_0_ = bf16[32,128]{1,0:T(8,128)(2,1)S(1)} custom-call(f32[32,8,128]{2,1,0:T(8,128)S(1)} %all-to-all-done.refs_0_), custom_call_target="tpu_custom_call" | custom-call | flops 4194304 | bytes 131072 | tf_op jit(solution)/shard_map/solve/pallas_call | solution.py:440
  30.0 0.4 %apply.1 = (f32[64,256]{1,0:T(8,128)S(1)}, bf16[64,256]{1,0:T(8,128)(2,1)S(1)}, bf16[64,256]{1,0:T(8,128)(2,1)S(1)}, bf16[64,256]{1,0:T(8,128)(2,1)S(1)}) custom-call(bf16[32,128]{1,0:T(8,128)(2,1)S(1)} %solve.1.refs_0_, bf16[256,256]{1,0:T(8,128)(2,1)S(1)} %collective-permute-done.4.refs_1_, bf16[256,256]{1,0:T(8,128)(2,1)S(1)} %collective-permute-done.5.refs_2_, ...), custom_call_target="tpu_custom_call" | custom-call | flops 134217728 | bytes 524288 | tf_op jit(solution)/shard_map/apply/pallas_call | solution.py:469
  30.4 0.9 %collective-permute-start.7 = (bf16[64,256]{1,0:T(8,128)(2,1)S(1)}, bf16[64,256]{1,0:T(8,128)(2,1)S(1)}, u32[]{:S(2)}, u32[]{:S(2)}) collective-permute-start(bf16[64,256]{1,0:T(8,128)(2,1)S(1)} %get-tuple-element.21), channel_id=1, source_target_pairs={{0,6},{2,4},{4,2},{6,0},{8,14},{10,12},{12,10},{14,8},{16,22},{18,... | collective-permute-start | bytes 98312 | tf_op jit(solution)/shard_map/ppermute | solution.py:357
  31.3 1.2 %collective-permute-start.8 = (bf16[64,256]{1,0:T(8,128)(2,1)S(1)}, bf16[64,256]{1,0:T(8,128)(2,1)S(1)}, u32[]{:S(2)}, u32[]{:S(2)}) collective-permute-start(bf16[64,256]{1,0:T(8,128)(2,1)S(1)} %get-tuple-element.22), channel_id=1, source_target_pairs={{0,4},{2,6},{4,0},{6,2},{8,12},{10,14},{12,8},{14,10},{16,20},{18,... | collective-permute-start | bytes 98312 | tf_op jit(solution)/shard_map/ppermute | solution.py:357
  32.5 1.4 %collective-permute-start.9 = (bf16[64,256]{1,0:T(8,128)(2,1)S(1)}, bf16[64,256]{1,0:T(8,128)(2,1)S(1)}, u32[]{:S(2)}, u32[]{:S(2)}) collective-permute-start(bf16[64,256]{1,0:T(8,128)(2,1)S(1)} %get-tuple-element.23), channel_id=1, source_target_pairs={{0,2},{2,0},{4,6},{6,4},{8,10},{10,8},{12,14},{14,12},{16,18},{18,... | collective-permute-start | bytes 98312 | tf_op jit(solution)/shard_map/ppermute | solution.py:357
  34.0 1.6 %collective-permute-done.7.refs_0_ = bf16[64,256]{1,0:T(8,128)(2,1)S(1)} collective-permute-done((bf16[64,256]{1,0:T(8,128)(2,1)S(1)}, bf16[64,256]{1,0:T(8,128)(2,1)S(1)}, u32[]{:S(2)}, u32[]{:S(2)}) %collective-permute-start.7) | collective-permute-done | bytes 32800 | tf_op jit(solution)/shard_map/ppermute | solution.py:357
  35.5 0.1 collective-permute-done.8.refs_1_
  35.6 0.8 %collective-permute-done.9.refs_2_ = bf16[64,256]{1,0:T(8,128)(2,1)S(1)} collective-permute-done((bf16[64,256]{1,0:T(8,128)(2,1)S(1)}, bf16[64,256]{1,0:T(8,128)(2,1)S(1)}, u32[]{:S(2)}, u32[]{:S(2)}) %collective-permute-start.9) | collective-permute-done | bytes 32800 | tf_op jit(solution)/shard_map/ppermute | solution.py:357
  36.4 0.7 %merge.1 = f32[64,1024]{1,0:T(8,128)} custom-call(f32[64,1024]{1,0:T(8,128)S(1)} %bitcast.7, bf16[64,256]{1,0:T(8,128)(2,1)S(1)} %collective-permute-done.7.refs_0_, bf16[64,256]{1,0:T(8,128)(2,1)S(1)} %collective-permute-done.8.refs_1_, bf16[64,256]{1,0:T(8,128)(2,1)S(1)} %collective-permute-done.9.refs_2_, f32[64,256]{1,0:T(8,128)S(1)} %get-tuple-element.24.refs_3_), custom_call_target="tpu_custom_call" | custom-call | tf_op jit(solution)/shard_map/merge/pallas_call | solution.py:488
  (23 shorter events, 0.1 us)
Async XLA Ops:
  0.6 1.0 %copy-start = (f32[8,8,1024]{2,1,0:T(8,128)S(1)}, f32[8,8,1024]{2,1,0:T(8,128)}, u32[]{:S(2)}) copy-start(f32[8,8,1024]{2,1,0:T(8,128)} %param.7) | copy-start | bytes 786436
  0.6 1.0 %copy-start.2 = (f32[8,1024]{1,0:T(8,128)S(1)}, f32[8,1024]{1,0:T(8,128)}, u32[]{:S(2)}) copy-start(f32[8,1024]{1,0:T(8,128)} %refs_1_.1) | copy-start | bytes 98308
  0.6 1.0 %copy-start.1 = (f32[8,1024]{1,0:T(8,128)S(1)}, f32[8,1024]{1,0:T(8,128)}, u32[]{:S(2)}) copy-start(f32[8,1024]{1,0:T(8,128)} %refs_2_.1) | copy-start | bytes 98308
  1.7 5.8 %collective-permute-start = (f32[80,1024]{1,0:T(8,128)S(1)}, f32[80,1024]{1,0:T(8,128)S(1)}, u32[]{:S(2)}, u32[]{:S(2)}) collective-permute-start(f32[80,1024]{1,0:T(8,128)S(1)} %pad_maximum_fusion), channel_id=1, source_target_pairs={{0,1},{1,0},{2,3},{3,2},{4,5},{5,4},{6,7},{7,6},{8,9},{9,8},{10,11... | collective-permute-start | bytes 983048 | tf_op jit(solution)/shard_map/ppermute | solution.py:377
  2.3 15.3 %collective-permute-start.1 = (bf16[64,1024]{1,0:T(8,128)(2,1)S(1)}, bf16[64,1024]{1,0:T(8,128)(2,1)S(1)}, u32[]{:S(2)}, u32[]{:S(2)}) collective-permute-start(bf16[64,1024]{1,0:T(8,128)(2,1)S(1)} %bitcast_convert_fusion), channel_id=1, source_target_pairs={{0,16},{2,18},{4,20},{6,22},{8,24},{10,26},{12,28},{14,30},{16,0},... | collective-permute-start | bytes 393224 | tf_op jit(solution)/shard_map/ppermute | solution.py:357
  5.9 11.7 %collective-permute-start.2 = (bf16[64,1024]{1,0:T(8,128)(2,1)S(1)}, bf16[64,1024]{1,0:T(8,128)(2,1)S(1)}, u32[]{:S(2)}, u32[]{:S(2)}) collective-permute-start(bf16[64,1024]{1,0:T(8,128)(2,1)S(1)} %bitcast_convert_fusion), channel_id=1, source_target_pairs={{0,24},{2,26},{4,28},{6,30},{8,16},{10,18},{12,20},{14,22},{16,8},... | collective-permute-start | bytes 393224 | tf_op jit(solution)/shard_map/ppermute | solution.py:357
  7.3 10.3 %collective-permute-start.3 = (bf16[64,1024]{1,0:T(8,128)(2,1)S(1)}, bf16[64,1024]{1,0:T(8,128)(2,1)S(1)}, u32[]{:S(2)}, u32[]{:S(2)}) collective-permute-start(bf16[64,1024]{1,0:T(8,128)(2,1)S(1)} %bitcast_convert_fusion), channel_id=1, source_target_pairs={{0,8},{2,10},{4,12},{6,14},{8,0},{10,2},{12,4},{14,6},{16,24},{18,... | collective-permute-start | bytes 393224 | tf_op jit(solution)/shard_map/ppermute | solution.py:357
  7.5 0.7 %copy-start.3 = (f32[8,64]{1,0:T(8,128)S(1)}, f32[8,64]{1,0:T(8,128)}, u32[]{:S(2)}) copy-start(f32[8,64]{1,0:T(8,128)} %refs_5_.1) | copy-start | bytes 6148
  7.5 0.7 %copy-start.4 = (s32[64]{0:T(128)S(1)}, s32[64]{0:T(128)}, u32[]{:S(2)}) copy-start(s32[64]{0:T(128)} %columns_hbm.1) | copy-start | bytes 772
  7.5 0.7 %copy-start.5 = (f32[64]{0:T(128)S(1)}, f32[64]{0:T(128)}, u32[]{:S(2)}) copy-start(f32[64]{0:T(128)} %param.11) | copy-start | bytes 772
  7.5 0.7 %copy-start.6 = (f32[64]{0:T(128)S(1)}, f32[64]{0:T(128)}, u32[]{:S(2)}) copy-start(f32[64]{0:T(128)} %param.12) | copy-start | bytes 772
  12.4 13.4 %all-to-all-start = ((f32[32,8,128]{2,1,0:T(8,128)}), f32[32,8,128]{2,1,0:T(8,128)S(1)}, u32[]{:S(2)}, u32[]{:S(2)}) async-start(f32[32,8,128]{2,1,0:T(8,128)} %get-tuple-element.15), calls=%async_computation | async-start | bytes 262144 | tf_op jit(solution)/shard_map/all_to_all | solution.py:431
  17.8 12.2 %collective-permute-start.4 = (bf16[256,256]{1,0:T(8,128)(2,1)S(1)}, bf16[256,256]{1,0:T(8,128)(2,1)S(1)}, u32[]{:S(2)}, u32[]{:S(2)}) collective-permute-start(bf16[256,256]{1,0:T(8,128)(2,1)S(1)} %get-tuple-element.29), channel_id=1, source_target_pairs={{0,6},{2,4},{4,2},{6,0},{8,14},{10,12},{12,10},{14,8},{16,22},{18,... | collective-permute-start | bytes 393224 | tf_op jit(solution)/shard_map/ppermute | solution.py:357
  20.5 9.5 %collective-permute-start.5 = (bf16[256,256]{1,0:T(8,128)(2,1)S(1)}, bf16[256,256]{1,0:T(8,128)(2,1)S(1)}, u32[]{:S(2)}, u32[]{:S(2)}) collective-permute-start(bf16[256,256]{1,0:T(8,128)(2,1)S(1)} %get-tuple-element.28), channel_id=1, source_target_pairs={{0,4},{2,6},{4,0},{6,2},{8,12},{10,14},{12,8},{14,10},{16,20},{18,... | collective-permute-start | bytes 393224 | tf_op jit(solution)/shard_map/ppermute | solution.py:357
  21.1 8.9 %collective-permute-start.6 = (bf16[256,256]{1,0:T(8,128)(2,1)S(1)}, bf16[256,256]{1,0:T(8,128)(2,1)S(1)}, u32[]{:S(2)}, u32[]{:S(2)}) collective-permute-start(bf16[256,256]{1,0:T(8,128)(2,1)S(1)} %get-tuple-element.27), channel_id=1, source_target_pairs={{0,2},{2,0},{4,6},{6,4},{8,10},{10,8},{12,14},{14,12},{16,18},{18,... | collective-permute-start | bytes 393224 | tf_op jit(solution)/shard_map/ppermute | solution.py:357
  30.4 5.1 %collective-permute-start.7 = (bf16[64,256]{1,0:T(8,128)(2,1)S(1)}, bf16[64,256]{1,0:T(8,128)(2,1)S(1)}, u32[]{:S(2)}, u32[]{:S(2)}) collective-permute-start(bf16[64,256]{1,0:T(8,128)(2,1)S(1)} %get-tuple-element.21), channel_id=1, source_target_pairs={{0,6},{2,4},{4,2},{6,0},{8,14},{10,12},{12,10},{14,8},{16,22},{18,... | collective-permute-start | bytes 98312 | tf_op jit(solution)/shard_map/ppermute | solution.py:357
  31.3 4.3 %collective-permute-start.8 = (bf16[64,256]{1,0:T(8,128)(2,1)S(1)}, bf16[64,256]{1,0:T(8,128)(2,1)S(1)}, u32[]{:S(2)}, u32[]{:S(2)}) collective-permute-start(bf16[64,256]{1,0:T(8,128)(2,1)S(1)} %get-tuple-element.22), channel_id=1, source_target_pairs={{0,4},{2,6},{4,0},{6,2},{8,12},{10,14},{12,8},{14,10},{16,20},{18,... | collective-permute-start | bytes 98312 | tf_op jit(solution)/shard_map/ppermute | solution.py:357
  32.5 3.9 %collective-permute-start.9 = (bf16[64,256]{1,0:T(8,128)(2,1)S(1)}, bf16[64,256]{1,0:T(8,128)(2,1)S(1)}, u32[]{:S(2)}, u32[]{:S(2)}) collective-permute-start(bf16[64,256]{1,0:T(8,128)(2,1)S(1)} %get-tuple-element.23), channel_id=1, source_target_pairs={{0,2},{2,0},{4,6},{6,4},{8,10},{10,8},{12,14},{14,12},{16,18},{18,... | collective-permute-start | bytes 98312 | tf_op jit(solution)/shard_map/ppermute | solution.py:357

commit v10 on v9

--- a/solution.py
+++ b/solution.py
@@ -295,10 +295,9 @@
     solved = solved_ref[...]
     pair, order = solved.shape
     wide = order * lines
-    spread = (
-        lax.broadcasted_iota(jnp.int32, (order, wide), 1) // lines
-        == lax.broadcasted_iota(jnp.int32, (order, wide), 0)
-    ).astype(jnp.bfloat16)
+    column = lax.broadcasted_iota(jnp.int32, (order, wide), 1)
+    begin = lax.broadcasted_iota(jnp.int32, (order, wide), 0) * lines
+    spread = jnp.logical_and(column >= begin, column < begin + lines).astype(jnp.bfloat16)
     stretched = jnp.dot(solved, spread, preferred_element_type=jnp.float32)
     on_line = lax.broadcasted_iota(jnp.int32, (lines, wide), 1) % lines == (
         lax.broadcasted_iota(jnp.int32, (lines, wide), 0)

time: 37.4 us -> 37.5 us (level)
  no operation moved by 1% of the time
where the time goes in v10:
time: 37.5 us; the launch traced here: 37.2 us
  starting transfers between devices  18 us (48%)
  Pallas kernels  9.53 us (25%)
  waiting for transfers between devices  6.96 us (19%)
  other arithmetic  1.03 us (3%)
  local copies, waits for them, and re-layouts  0.82 us (2%)
  between operations  0.82 us (2%)
    ppermute x9, starting transfers between devices, across(): return lax.ppermute(value, 'mem', [(i, i ^ bit) for i in range(owners)])  12.3 us
    all_to_all x1, starting transfers between devices, body(): everyone = lax.all_to_all(payload, ('mem', 'sp'), 0, 0, tiled=True)  5.18 us
    all_to_all x1, waiting for transfers between devices, body(): everyone = lax.all_to_all(payload, ('mem', 'sp'), 0, 0, tiled=True)  4.48 us
    pallas_call x1, Pallas kernels, body(): pl.pallas_call(lambda *refs: solve_kernel(norm_scale, slabs, offsets, tur...  4.17 us
    pallas_call x1, Pallas kernels, body(): pl.pallas_call(kernel, out_shape=(jax.ShapeDtypeStruct((members, probes),...  4.17 us
    ppermute x9, waiting for transfers between devices, across(): return lax.ppermute(value, 'mem', [(i, i ^ bit) for i in range(owners)])  2.48 us
    convert_element_type x1, other arithmetic, body(): field_round = field_flat.astype(jnp.bfloat16)  1.01 us
  transfers between devices with their start and end apart: 11, of which 4 were waited for; matrix products, arithmetic and copies ran while one was open for 0% of the time, Pallas kernels for 22%

profile of v10, /device:TPU:0, one launch (start us, length us, event | category | flops | bytes accessed | tf_op | source)
XLA Modules:
  0.0 37.2 jit_solution(5828714489494539884)
XLA Ops:
  0.7 1.0 %bitcast_convert_fusion = bf16[64,1024]{1,0:T(8,128)(2,1)S(1)} fusion(f32[8,8,1024]{2,1,0:T(8,128)} %param.7), kind=kLoop, calls=%fused_computation.9 | loop fusion | flops 65536 | bytes 393216 | tf_op jit(solution)/shard_map/convert_element_type | solution.py:359
  1.7 0.5 %collective-permute-start = (f32[80,1024]{1,0:T(8,128)S(1)}, f32[80,1024]{1,0:T(8,128)S(1)}, u32[]{:S(2)}, u32[]{:S(2)}) collective-permute-start(f32[80,1024]{1,0:T(8,128)S(1)} %pad_maximum_fusion), channel_id=1, source_target_pairs={{0,1},{1,0},{2,3},{3,2},{4,5},{5,4},{6,7},{7,6},{8,9},{9,8},{10,11... | collective-permute-start | bytes 983048 | tf_op jit(solution)/shard_map/ppermute | solution.py:376
  2.3 3.7 %collective-permute-start.1 = (bf16[64,1024]{1,0:T(8,128)(2,1)S(1)}, bf16[64,1024]{1,0:T(8,128)(2,1)S(1)}, u32[]{:S(2)}, u32[]{:S(2)}) collective-permute-start(bf16[64,1024]{1,0:T(8,128)(2,1)S(1)} %bitcast_convert_fusion), channel_id=1, source_target_pairs={{0,16},{2,18},{4,20},{6,22},{8,24},{10,26},{12,28},{14,30},{16,0},... | collective-permute-start | bytes 393224 | tf_op jit(solution)/shard_map/ppermute | solution.py:356
  5.9 1.3 %collective-permute-start.2 = (bf16[64,1024]{1,0:T(8,128)(2,1)S(1)}, bf16[64,1024]{1,0:T(8,128)(2,1)S(1)}, u32[]{:S(2)}, u32[]{:S(2)}) collective-permute-start(bf16[64,1024]{1,0:T(8,128)(2,1)S(1)} %bitcast_convert_fusion), channel_id=1, source_target_pairs={{0,24},{2,26},{4,28},{6,30},{8,16},{10,18},{12,20},{14,22},{16,8},... | collective-permute-start | bytes 393224 | tf_op jit(solution)/shard_map/ppermute | solution.py:356
  7.3 0.2 collective-permute-start.3
  7.5 0.0 copy-start.6
  7.5 0.7 %copy-done.3 = f32[8,64]{1,0:T(8,128)S(1)} copy-done((f32[8,64]{1,0:T(8,128)S(1)}, f32[8,64]{1,0:T(8,128)}, u32[]{:S(2)}) %copy-start.3) | copy-done | bytes 2072
  8.2 0.0 copy-done.6
  8.2 4.2 %conduct.1 = (f32[8,64]{1,0:T(8,128)}, f32[32,8,128]{2,1,0:T(8,128)}) custom-call(s32[64]{0:T(128)S(1)} %copy-done.4, f32[64,1024]{1,0:T(8,128)S(1)} %bitcast.6, f32[80,1024]{1,0:T(8,128)S(1)} %collective-permute-done.refs_0_, f32[8,1024]{1,0:T(8,128)S(1)} %copy-done.2, f32[8,1024]{1,0:T(8,128)S(1)} %copy-done.1, f32[1,64]{1,0:T(1,128)S(1)} %bitcast.8, ...), custom_call_target="tpu_custom_call" | custom-call | flops 15728640 | bytes 786432 | tf_op jit(solution)/shard_map/conduct/pallas_call | solution.py:392
  12.4 5.2 %all-to-all-start = ((f32[32,8,128]{2,1,0:T(8,128)}), f32[32,8,128]{2,1,0:T(8,128)S(1)}, u32[]{:S(2)}, u32[]{:S(2)}) async-start(f32[32,8,128]{2,1,0:T(8,128)} %get-tuple-element.15), calls=%async_computation | async-start | bytes 262144 | tf_op jit(solution)/shard_map/all_to_all | solution.py:430
  17.7 0.1 constant_dynamic-slice_fusion
  17.8 2.7 %collective-permute-start.4 = (bf16[256,256]{1,0:T(8,128)(2,1)S(1)}, bf16[256,256]{1,0:T(8,128)(2,1)S(1)}, u32[]{:S(2)}, u32[]{:S(2)}) collective-permute-start(bf16[256,256]{1,0:T(8,128)(2,1)S(1)} %get-tuple-element.29), channel_id=1, source_target_pairs={{0,6},{2,4},{4,2},{6,0},{8,14},{10,12},{12,10},{14,8},{16,22},{18,... | collective-permute-start | bytes 393224 | tf_op jit(solution)/shard_map/ppermute | solution.py:356
  20.5 0.6 %collective-permute-start.5 = (bf16[256,256]{1,0:T(8,128)(2,1)S(1)}, bf16[256,256]{1,0:T(8,128)(2,1)S(1)}, u32[]{:S(2)}, u32[]{:S(2)}) collective-permute-start(bf16[256,256]{1,0:T(8,128)(2,1)S(1)} %get-tuple-element.28), channel_id=1, source_target_pairs={{0,4},{2,6},{4,0},{6,2},{8,12},{10,14},{12,8},{14,10},{16,20},{18,... | collective-permute-start | bytes 393224 | tf_op jit(solution)/shard_map/ppermute | solution.py:356
  21.1 0.3 collective-permute-start.6
  21.3 4.5 %all-to-all-done.refs_0_ = f32[32,8,128]{2,1,0:T(8,128)S(1)} async-done(((f32[32,8,128]{2,1,0:T(8,128)}), f32[32,8,128]{2,1,0:T(8,128)S(1)}, u32[]{:S(2)}, u32[]{:S(2)}) %all-to-all-start) | async-done | bytes 131104 | tf_op jit(solution)/shard_map/all_to_all | solution.py:430
  25.8 4.2 %solve.1.refs_0_ = bf16[32,128]{1,0:T(8,128)(2,1)S(1)} custom-call(f32[32,8,128]{2,1,0:T(8,128)S(1)} %all-to-all-done.refs_0_), custom_call_target="tpu_custom_call" | custom-call | flops 4194304 | bytes 131072 | tf_op jit(solution)/shard_map/solve/pallas_call | solution.py:439
  30.0 0.5 %apply.1 = (f32[64,256]{1,0:T(8,128)S(1)}, bf16[64,256]{1,0:T(8,128)(2,1)S(1)}, bf16[64,256]{1,0:T(8,128)(2,1)S(1)}, bf16[64,256]{1,0:T(8,128)(2,1)S(1)}) custom-call(bf16[32,128]{1,0:T(8,128)(2,1)S(1)} %solve.1.refs_0_, bf16[256,256]{1,0:T(8,128)(2,1)S(1)} %collective-permute-done.4.refs_1_, bf16[256,256]{1,0:T(8,128)(2,1)S(1)} %collective-permute-done.5.refs_2_, ...), custom_call_target="tpu_custom_call" | custom-call | flops 134217728 | bytes 524288 | tf_op jit(solution)/shard_map/apply/pallas_call | solution.py:468
  30.5 0.9 %collective-permute-start.7 = (bf16[64,256]{1,0:T(8,128)(2,1)S(1)}, bf16[64,256]{1,0:T(8,128)(2,1)S(1)}, u32[]{:S(2)}, u32[]{:S(2)}) collective-permute-start(bf16[64,256]{1,0:T(8,128)(2,1)S(1)} %get-tuple-element.21), channel_id=1, source_target_pairs={{0,6},{2,4},{4,2},{6,0},{8,14},{10,12},{12,10},{14,8},{16,22},{18,... | collective-permute-start | bytes 98312 | tf_op jit(solution)/shard_map/ppermute | solution.py:356
  31.4 1.2 %collective-permute-start.8 = (bf16[64,256]{1,0:T(8,128)(2,1)S(1)}, bf16[64,256]{1,0:T(8,128)(2,1)S(1)}, u32[]{:S(2)}, u32[]{:S(2)}) collective-permute-start(bf16[64,256]{1,0:T(8,128)(2,1)S(1)} %get-tuple-element.22), channel_id=1, source_target_pairs={{0,4},{2,6},{4,0},{6,2},{8,12},{10,14},{12,8},{14,10},{16,20},{18,... | collective-permute-start | bytes 98312 | tf_op jit(solution)/shard_map/ppermute | solution.py:356
  32.6 1.4 %collective-permute-start.9 = (bf16[64,256]{1,0:T(8,128)(2,1)S(1)}, bf16[64,256]{1,0:T(8,128)(2,1)S(1)}, u32[]{:S(2)}, u32[]{:S(2)}) collective-permute-start(bf16[64,256]{1,0:T(8,128)(2,1)S(1)} %get-tuple-element.23), channel_id=1, source_target_pairs={{0,2},{2,0},{4,6},{6,4},{8,10},{10,8},{12,14},{14,12},{16,18},{18,... | collective-permute-start | bytes 98312 | tf_op jit(solution)/shard_map/ppermute | solution.py:356
  34.0 1.6 %collective-permute-done.7.refs_0_ = bf16[64,256]{1,0:T(8,128)(2,1)S(1)} collective-permute-done((bf16[64,256]{1,0:T(8,128)(2,1)S(1)}, bf16[64,256]{1,0:T(8,128)(2,1)S(1)}, u32[]{:S(2)}, u32[]{:S(2)}) %collective-permute-start.7) | collective-permute-done | bytes 32800 | tf_op jit(solution)/shard_map/ppermute | solution.py:356
  35.6 0.1 collective-permute-done.8.refs_1_
  35.7 0.8 %collective-permute-done.9.refs_2_ = bf16[64,256]{1,0:T(8,128)(2,1)S(1)} collective-permute-done((bf16[64,256]{1,0:T(8,128)(2,1)S(1)}, bf16[64,256]{1,0:T(8,128)(2,1)S(1)}, u32[]{:S(2)}, u32[]{:S(2)}) %collective-permute-start.9) | collective-permute-done | bytes 32800 | tf_op jit(solution)/shard_map/ppermute | solution.py:356
  36.5 0.7 %merge.1 = f32[64,1024]{1,0:T(8,128)} custom-call(f32[64,1024]{1,0:T(8,128)S(1)} %bitcast.7, bf16[64,256]{1,0:T(8,128)(2,1)S(1)} %collective-permute-done.7.refs_0_, bf16[64,256]{1,0:T(8,128)(2,1)S(1)} %collective-permute-done.8.refs_1_, bf16[64,256]{1,0:T(8,128)(2,1)S(1)} %collective-permute-done.9.refs_2_, f32[64,256]{1,0:T(8,128)S(1)} %get-tuple-element.24.refs_3_), custom_call_target="tpu_custom_call" | custom-call | tf_op jit(solution)/shard_map/merge/pallas_call | solution.py:487
  (23 shorter events, 0.1 us)
Async XLA Ops:
  0.6 1.0 %copy-start = (f32[8,8,1024]{2,1,0:T(8,128)S(1)}, f32[8,8,1024]{2,1,0:T(8,128)}, u32[]{:S(2)}) copy-start(f32[8,8,1024]{2,1,0:T(8,128)} %param.7) | copy-start | bytes 786436
  0.6 1.0 %copy-start.2 = (f32[8,1024]{1,0:T(8,128)S(1)}, f32[8,1024]{1,0:T(8,128)}, u32[]{:S(2)}) copy-start(f32[8,1024]{1,0:T(8,128)} %refs_1_.1) | copy-start | bytes 98308
  0.6 1.0 %copy-start.1 = (f32[8,1024]{1,0:T(8,128)S(1)}, f32[8,1024]{1,0:T(8,128)}, u32[]{:S(2)}) copy-start(f32[8,1024]{1,0:T(8,128)} %refs_2_.1) | copy-start | bytes 98308
  1.7 5.8 %collective-permute-start = (f32[80,1024]{1,0:T(8,128)S(1)}, f32[80,1024]{1,0:T(8,128)S(1)}, u32[]{:S(2)}, u32[]{:S(2)}) collective-permute-start(f32[80,1024]{1,0:T(8,128)S(1)} %pad_maximum_fusion), channel_id=1, source_target_pairs={{0,1},{1,0},{2,3},{3,2},{4,5},{5,4},{6,7},{7,6},{8,9},{9,8},{10,11... | collective-permute-start | bytes 983048 | tf_op jit(solution)/shard_map/ppermute | solution.py:376
  2.3 15.3 %collective-permute-start.1 = (bf16[64,1024]{1,0:T(8,128)(2,1)S(1)}, bf16[64,1024]{1,0:T(8,128)(2,1)S(1)}, u32[]{:S(2)}, u32[]{:S(2)}) collective-permute-start(bf16[64,1024]{1,0:T(8,128)(2,1)S(1)} %bitcast_convert_fusion), channel_id=1, source_target_pairs={{0,16},{2,18},{4,20},{6,22},{8,24},{10,26},{12,28},{14,30},{16,0},... | collective-permute-start | bytes 393224 | tf_op jit(solution)/shard_map/ppermute | solution.py:356
  5.9 11.7 %collective-permute-start.2 = (bf16[64,1024]{1,0:T(8,128)(2,1)S(1)}, bf16[64,1024]{1,0:T(8,128)(2,1)S(1)}, u32[]{:S(2)}, u32[]{:S(2)}) collective-permute-start(bf16[64,1024]{1,0:T(8,128)(2,1)S(1)} %bitcast_convert_fusion), channel_id=1, source_target_pairs={{0,24},{2,26},{4,28},{6,30},{8,16},{10,18},{12,20},{14,22},{16,8},... | collective-permute-start | bytes 393224 | tf_op jit(solution)/shard_map/ppermute | solution.py:356
  7.3 10.3 %collective-permute-start.3 = (bf16[64,1024]{1,0:T(8,128)(2,1)S(1)}, bf16[64,1024]{1,0:T(8,128)(2,1)S(1)}, u32[]{:S(2)}, u32[]{:S(2)}) collective-permute-start(bf16[64,1024]{1,0:T(8,128)(2,1)S(1)} %bitcast_convert_fusion), channel_id=1, source_target_pairs={{0,8},{2,10},{4,12},{6,14},{8,0},{10,2},{12,4},{14,6},{16,24},{18,... | collective-permute-start | bytes 393224 | tf_op jit(solution)/shard_map/ppermute | solution.py:356
  7.5 0.7 %copy-start.3 = (f32[8,64]{1,0:T(8,128)S(1)}, f32[8,64]{1,0:T(8,128)}, u32[]{:S(2)}) copy-start(f32[8,64]{1,0:T(8,128)} %refs_5_.1) | copy-start | bytes 6148
  7.5 0.7 %copy-start.4 = (s32[64]{0:T(128)S(1)}, s32[64]{0:T(128)}, u32[]{:S(2)}) copy-start(s32[64]{0:T(128)} %columns_hbm.1) | copy-start | bytes 772
  7.5 0.7 %copy-start.5 = (f32[64]{0:T(128)S(1)}, f32[64]{0:T(128)}, u32[]{:S(2)}) copy-start(f32[64]{0:T(128)} %param.11) | copy-start | bytes 772
  7.5 0.7 %copy-start.6 = (f32[64]{0:T(128)S(1)}, f32[64]{0:T(128)}, u32[]{:S(2)}) copy-start(f32[64]{0:T(128)} %param.12) | copy-start | bytes 772
  12.4 13.4 %all-to-all-start = ((f32[32,8,128]{2,1,0:T(8,128)}), f32[32,8,128]{2,1,0:T(8,128)S(1)}, u32[]{:S(2)}, u32[]{:S(2)}) async-start(f32[32,8,128]{2,1,0:T(8,128)} %get-tuple-element.15), calls=%async_computation | async-start | bytes 262144 | tf_op jit(solution)/shard_map/all_to_all | solution.py:430
  17.8 12.2 %collective-permute-start.4 = (bf16[256,256]{1,0:T(8,128)(2,1)S(1)}, bf16[256,256]{1,0:T(8,128)(2,1)S(1)}, u32[]{:S(2)}, u32[]{:S(2)}) collective-permute-start(bf16[256,256]{1,0:T(8,128)(2,1)S(1)} %get-tuple-element.29), channel_id=1, source_target_pairs={{0,6},{2,4},{4,2},{6,0},{8,14},{10,12},{12,10},{14,8},{16,22},{18,... | collective-permute-start | bytes 393224 | tf_op jit(solution)/shard_map/ppermute | solution.py:356
  20.5 9.5 %collective-permute-start.5 = (bf16[256,256]{1,0:T(8,128)(2,1)S(1)}, bf16[256,256]{1,0:T(8,128)(2,1)S(1)}, u32[]{:S(2)}, u32[]{:S(2)}) collective-permute-start(bf16[256,256]{1,0:T(8,128)(2,1)S(1)} %get-tuple-element.28), channel_id=1, source_target_pairs={{0,4},{2,6},{4,0},{6,2},{8,12},{10,14},{12,8},{14,10},{16,20},{18,... | collective-permute-start | bytes 393224 | tf_op jit(solution)/shard_map/ppermute | solution.py:356
  21.1 8.9 %collective-permute-start.6 = (bf16[256,256]{1,0:T(8,128)(2,1)S(1)}, bf16[256,256]{1,0:T(8,128)(2,1)S(1)}, u32[]{:S(2)}, u32[]{:S(2)}) collective-permute-start(bf16[256,256]{1,0:T(8,128)(2,1)S(1)} %get-tuple-element.27), channel_id=1, source_target_pairs={{0,2},{2,0},{4,6},{6,4},{8,10},{10,8},{12,14},{14,12},{16,18},{18,... | collective-permute-start | bytes 393224 | tf_op jit(solution)/shard_map/ppermute | solution.py:356
  30.5 5.1 %collective-permute-start.7 = (bf16[64,256]{1,0:T(8,128)(2,1)S(1)}, bf16[64,256]{1,0:T(8,128)(2,1)S(1)}, u32[]{:S(2)}, u32[]{:S(2)}) collective-permute-start(bf16[64,256]{1,0:T(8,128)(2,1)S(1)} %get-tuple-element.21), channel_id=1, source_target_pairs={{0,6},{2,4},{4,2},{6,0},{8,14},{10,12},{12,10},{14,8},{16,22},{18,... | collective-permute-start | bytes 98312 | tf_op jit(solution)/shard_map/ppermute | solution.py:356
  31.4 4.3 %collective-permute-start.8 = (bf16[64,256]{1,0:T(8,128)(2,1)S(1)}, bf16[64,256]{1,0:T(8,128)(2,1)S(1)}, u32[]{:S(2)}, u32[]{:S(2)}) collective-permute-start(bf16[64,256]{1,0:T(8,128)(2,1)S(1)} %get-tuple-element.22), channel_id=1, source_target_pairs={{0,4},{2,6},{4,0},{6,2},{8,12},{10,14},{12,8},{14,10},{16,20},{18,... | collective-permute-start | bytes 98312 | tf_op jit(solution)/shard_map/ppermute | solution.py:356
  32.6 3.9 %collective-permute-start.9 = (bf16[64,256]{1,0:T(8,128)(2,1)S(1)}, bf16[64,256]{1,0:T(8,128)(2,1)S(1)}, u32[]{:S(2)}, u32[]{:S(2)}) collective-permute-start(bf16[64,256]{1,0:T(8,128)(2,1)S(1)} %get-tuple-element.23), channel_id=1, source_target_pairs={{0,2},{2,0},{4,6},{6,4},{8,10},{10,8},{12,14},{14,12},{16,18},{18,... | collective-permute-start | bytes 98312 | tf_op jit(solution)/shard_map/ppermute | solution.py:356
